TPU v7x, 32 devices: a whole 2x2x4 slice. The times are simulated.
32 devices in a mesh: prow: 2 (over x), pcol: 4 (over z), dz: 4 (over y, core).
Axes of the slice: x: 2, y: 2, z: 4, core: 2. Of those that a mesh axis runs over, the one named last changes fastest.
Arguments:
- coeffs: bfloat16 [1024, 512], P('prow', 'pcol'), may hold values from -0.25 to 0.25
- occupations: int32 [512], P('pcol'), may hold values from 0 to 2
- counts: int32 [64], replicated, may hold values from 5 to 13
- intersection: int32 [32, 8], replicated, may hold values from 0 to 63, as said below
- phi_values: bfloat16 [4096, 128], P(('prow', 'pcol', 'dz')), may hold values from -0.5 to 0.5
- panel_values: bfloat16 [4096, 512], P(('prow', 'pcol', 'dz')), may hold values from -6 to 6
- proj_site: bfloat16 [64, 16, 16], P(('prow', 'pcol')), may hold values from -1.5 to 1.5
- proj_panel: bfloat16 [64, 16, 512], P(('prow', 'pcol'), None, 'dz'), may hold values from -6 to 6
Outputs:
- density: float32 [4096], P(('prow', 'pcol', 'dz'))
- rho_ij: float32 [64, 256], P(('prow', 'pcol'))
Inputs may be any that keep to these rules, and one draw needn't show every extreme that they name: `intersection`: each domain lists 8 distinct atoms in no particular order; of the 8 atoms a * 8 .. (a + 1) * 8 - 1 of any owner a, a domain lists either none or exactly 2, and exactly 4 owners have 2 each.
All inputs are finite; a program needn't handle non-finite values.
Results may differ from a plain program's by a relative error of at most 0.0029.
Values may be sent and summed in bfloat16 or wider, within the bound.
No kernel may reach another device: no remote copies, remote signals or barrier semaphores. Data moves between devices by JAX's collectives and lax.ppermute only.
A program may use at most 64 MiB of HBM per device.

v0:
```python
import jax
import jax.numpy as jnp
from jax import lax
from jax.sharding import PartitionSpec as P

SLOTS = 16
NPROJ = 16
PW = 512
CAP = 2


def spread(block, axis, holder):
    block = jnp.where(lax.axis_index(axis) == holder, block, jnp.zeros_like(block))
    return lax.psum(block, axis)


def shards(
    coeffs, occupations, counts, intersection, phi_values, panel_values, proj_site, proj_panel
):
    n_row = lax.axis_size("prow")
    n_col = lax.axis_size("pcol")
    n_slab = lax.axis_size("dz")
    rows_blk = coeffs.shape[0]
    atoms_blk = rows_blk // SLOTS
    start_atom = lax.axis_index("prow") * atoms_blk
    block_counts = lax.dynamic_slice_in_dim(counts, start_atom, atoms_blk)
    slot_ids = lax.broadcasted_iota(jnp.int32, (atoms_blk, SLOTS), 1)
    live = (slot_ids < block_counts[:, None]).reshape(rows_blk, 1)
    masked = jnp.where(live, coeffs, jnp.zeros((), coeffs.dtype))
    weights = (occupations.astype(jnp.float32) * 0.5).astype(coeffs.dtype)
    panel = spread(coeffs[:PW], "prow", 0)
    panel_slots = lax.broadcasted_iota(jnp.int32, (PW // SLOTS, SLOTS), 1)
    panel_live = (panel_slots < counts[: PW // SLOTS][:, None]).reshape(PW, 1)
    panel = jnp.where(panel_live, panel, jnp.zeros((), panel.dtype))
    scaled = masked * weights[None, :]
    owned = lax.psum_scatter(
        lax.dot_general(
            scaled, panel, (((1,), (1,)), ((), ())), preferred_element_type=jnp.float32
        ),
        "pcol",
        scatter_dimension=0,
        tiled=True,
    )
    owned_rows = owned.astype(jnp.bfloat16)
    atoms_own = owned_rows.shape[0] // SLOTS
    owned_blocks = owned_rows.reshape(atoms_own, SLOTS, PW)
    owner_id = lax.axis_index("prow") * n_col + lax.axis_index("pcol")
    slab = lax.axis_index("dz")
    receivers = n_row * n_col
    by_slab = intersection.reshape(receivers, n_slab, intersection.shape[1])
    lists = lax.dynamic_index_in_dim(by_slab, slab, 1, keepdims=False)
    mine = lists // atoms_own == owner_id
    ranks = jnp.cumsum(mine.astype(jnp.int32), axis=1) - 1
    slot_pick = lax.broadcasted_iota(jnp.int32, (1, 1, CAP), 2)
    picked = mine[:, :, None] & (ranks[:, :, None] == slot_pick)
    local_atom = jnp.sum(jnp.where(picked, (lists - owner_id * atoms_own)[:, :, None], 0), axis=1)
    valid = jnp.any(picked, axis=1)
    outgoing = jnp.where(
        valid[:, :, None, None], owned_blocks[local_atom], jnp.zeros((), owned_rows.dtype)
    )
    incoming = lax.all_to_all(
        outgoing.reshape(receivers * CAP * SLOTS, PW),
        ("prow", "pcol"),
        split_axis=0,
        concat_axis=0,
        tiled=True,
    )
    incoming = incoming.reshape(receivers * CAP, SLOTS, PW)
    domain = owner_id * n_slab + slab
    wanted = lax.dynamic_index_in_dim(intersection, domain, 0, keepdims=False)
    wanted_owner = wanted // atoms_own
    listed = wanted.shape[0]
    same_owner = wanted_owner[:, None] == wanted_owner[None, :]
    earlier = lax.broadcasted_iota(jnp.int32, (listed, listed), 1) < lax.broadcasted_iota(
        jnp.int32, (listed, listed), 0
    )
    rank_in = jnp.sum((same_owner & earlier).astype(jnp.int32), axis=1)
    slot_of = wanted_owner * CAP + rank_in
    domain_rows = incoming[slot_of].reshape(listed * SLOTS, PW)
    mixed = jnp.dot(phi_values, domain_rows, preferred_element_type=jnp.float32)
    density = jnp.sum(mixed * panel_values.astype(jnp.float32), axis=1)
    projected = jnp.einsum(
        "aim,amn->ain", proj_site, owned_blocks, preferred_element_type=jnp.float32
    )
    slab_cols = proj_panel.shape[2]
    part_proj = lax.dynamic_slice_in_dim(projected, slab * slab_cols, slab_cols, 2)
    partial_rho = jnp.einsum(
        "ain,ajn->aij", part_proj, proj_panel.astype(jnp.float32), precision=lax.Precision.HIGHEST
    )
    rho_full = lax.psum(partial_rho, "dz")
    return (density, rho_full.reshape(atoms_own, NPROJ * NPROJ))


def solution(mesh):
    return jax.shard_map(
        shards,
        mesh=mesh,
        in_specs=(
            P("prow", "pcol"),
            P("pcol"),
            P(),
            P(),
            P(("prow", "pcol", "dz"), None),
            P(("prow", "pcol", "dz"), None),
            P(("prow", "pcol"), None, None),
            P(("prow", "pcol"), None, "dz"),
        ),
        out_specs=(P(("prow", "pcol", "dz")), P(("prow", "pcol"), None)),
        check_vma=False,
    )
```

profile of v0, /device:TPU:0, one launch (start us, length us, event | category | flops | bytes accessed | tf_op | source)
XLA Modules:
  0.0 88.0 jit_solution(8320304785023686756)
XLA Ops:
  7.2 1.6 %broadcast_select_fusion = bf16[512,128]{1,0:T(8,128)(2,1)} fusion(bf16[512,128]{1,0:T(8,128)(2,1)} %param.8, pred[]{:T(512)S(6)} %eq.50), kind=kLoop, calls=%fused_computation.12 | loop fusion | flops 65536 | bytes 262145 | tf_op jit(solution)/shard_map/jit(_where)/select_n | solution.py:13
  8.9 0.6 copy-done.6
  9.9 0.6 copy-done.7
  10.4 24.0 %all-reduce.2.cloned.1.call-done = bf16[512,128]{1,0:T(8,128)(2,1)} async-done(((bf16[512,128]{1,0:T(8,128)(2,1)}), bf16[512,128]{1,0:T(8,128)(2,1)}) %all-reduce.2.cloned.1.call-update) | async-done | bytes 131088 | tf_op jit(solution)/shard_map/psum | solution.py:14
  34.4 2.3 %fusion.2 = f32[512,512]{1,0:T(8,128)} fusion(bf16[512,128]{1,0:T(8,128)(2,1)} %all-reduce.2.cloned.1.call-done, bf16[512,128]{1,0:T(8,128)(2,1)S(1)} %copy-done.1, pred[512]{0:T(512)(128)(4,1)S(1)} %lt.74, pred[512]{0:T(512)(128)(4,1)S(1)} %lt.71, bf16[128]{0:T(256)(128)(2,1)S(1)} %multiply_convert_fusion), kind=kOutput, calls=%fused_computation.6 | convolution fusion | flops 67305472 | bytes 1312000 | tf_op jit(solution)/shard_map/dot_general | solution.py:37
  36.8 0.6 copy-done.5
  37.5 0.2 reduce_window_sum.11
  37.7 0.1 select_reduce_fusion
  38.0 0.2 fusion.13
  38.6 0.2 dynamic-slice_reduce_fusion
  38.8 0.2 convert_reduce_fusion
  39.0 25.0 %reduce-scatter.2.cloned.1.call-done = f32[128,512]{1,0:T(8,128)} async-done(((f32[512,512]{1,0:T(8,128)}), f32[128,512]{1,0:T(8,128)}) %reduce-scatter.2.cloned.1.call-update) | async-done | bytes 262160 | tf_op jit(solution)/shard_map/reduce_scatter | solution.py:36
  64.1 1.0 %convert_element_type.26 = bf16[128,512]{1,0:T(8,128)(2,1)S(1)} convert(f32[128,512]{1,0:T(8,128)} %reduce-scatter.2.cloned.1.call-done) | non-fusion elementwise | flops 65536 | bytes 393216 | tf_op jit(solution)/shard_map/convert_element_type | solution.py:44
  65.0 0.6 gather_fusion
  65.6 0.8 bitcast_select_fusion
  66.4 3.4 %all-to-all-start = ((bf16[8,32,512]{2,1,0:T(8,128)(2,1)}), bf16[8,32,512]{2,1,0:T(8,128)(2,1)S(1)}, u32[]{:S(2)}, u32[]{:S(2)}) async-start(bf16[8,32,512]{2,1,0:T(8,128)(2,1)} %bitcast_select_fusion), calls=%async_computation.1 | async-start | bytes 524288 | tf_op jit(solution)/shard_map/all_to_all | solution.py:61
  69.9 0.2 fusion.27
  70.0 0.6 copy-done.3
  70.6 0.2 fusion.8
  70.9 7.4 %psum.15 = f32[8,256]{1,0:T(8,128)} all-reduce(f32[8,256]{1,0:T(8,128)S(1)} %reshape.250), channel_id=1, replica_groups=mesh['prow'=2,'pcol'=4,'dz'=4] {'dz'}, use_global_device_ids=true, to_apply=%region_7.8 | all-reduce | flops 2048 | bytes 16384 | tf_op jit(solution)/shard_map/psum | solution.py:90
  78.3 1.4 %all-to-all-done = bf16[8,32,512]{2,1,0:T(8,128)(2,1)S(1)} async-done(((bf16[8,32,512]{2,1,0:T(8,128)(2,1)}), bf16[8,32,512]{2,1,0:T(8,128)(2,1)S(1)}, u32[]{:S(2)}, u32[]{:S(2)}) %all-to-all-start) | async-done | bytes 262176 | tf_op jit(solution)/shard_map/all_to_all | solution.py:61
  79.7 0.6 gather_fusion.1
  80.2 0.2 copy-done.4
  80.4 0.8 fusion.1
  (37 shorter events, 1.3 us)
Async XLA Ops:
  7.2 62.7 %copy-start = (bf16[8,16,16]{2,1,0:T(8,128)(2,1)S(1)}, bf16[8,16,16]{2,1,0:T(8,128)(2,1)}, u32[]{:S(2)}) copy-start(bf16[8,16,16]{2,1,0:T(8,128)(2,1)} %param.14) | copy-start | bytes 12292
  7.2 27.3 %all-reduce.2.cloned.1.call-start = ((), (), s32[]{:S(2)}) async-start(), calls=%async_computation.2 | async-start | bytes 262144 | tf_op jit(solution)/shard_map/psum | solution.py:14
  8.8 25.6 %copy-start.1 = (bf16[512,128]{1,0:T(8,128)(2,1)S(1)}, bf16[512,128]{1,0:T(8,128)(2,1)}, u32[]{:S(2)}) copy-start(bf16[512,128]{1,0:T(8,128)(2,1)} %param.8) | copy-start | bytes 393220
  8.8 55.3 %reduce-scatter.2.cloned.1.call-start = ((), (), s32[]{:S(2)}) async-start(), calls=%async_computation.3 | async-start | bytes 1310720 | tf_op jit(solution)/shard_map/reduce_scatter | solution.py:36
  8.9 0.7 copy-start.6
  9.8 0.7 copy-start.7
  36.8 0.7 copy-start.5
  36.8 1.7 %copy-start.2 = (bf16[128,512]{1,0:T(8,128)(2,1)S(1)}, bf16[128,512]{1,0:T(8,128)(2,1)}, u32[]{:S(2)}) copy-start(bf16[128,512]{1,0:T(8,128)(2,1)} %param.13) | copy-start | bytes 393220
  66.4 13.2 %all-to-all-start = ((bf16[8,32,512]{2,1,0:T(8,128)(2,1)}), bf16[8,32,512]{2,1,0:T(8,128)(2,1)S(1)}, u32[]{:S(2)}, u32[]{:S(2)}) async-start(bf16[8,32,512]{2,1,0:T(8,128)(2,1)} %bitcast_select_fusion), calls=%async_computation.1 | async-start | bytes 524288 | tf_op jit(solution)/shard_map/all_to_all | solution.py:61
  69.8 0.8 copy-start.3
  79.6 0.8 copy-start.4
Sparse Core Ops, SparseCore 0:
  10.3 24.1 all-reduce.1
  36.9 27.1 reduce-scatter.1
where the time goes:
time: 88.5 us; the launch traced here: 88 us
  waiting for transfers between devices  50.5 us (57%)
  between operations  14.2 us (16%)
  blocking collectives  7.39 us (8%)
  local copies, waits for them, and re-layouts  4.77 us (5%)
  other arithmetic  4.31 us (5%)
  starting transfers between devices  3.49 us (4%)
  matrix products  3.4 us (4%)
    reduce_scatter x1, waiting for transfers between devices, shards(): lax.psum_scatter(lax.dot_general(scaled, panel, (((1,), (1,)), ((), ())),...  25 us
    psum x1, waiting for transfers between devices, spread(): return lax.psum(block, axis)  24 us
    psum x1, blocking collectives, shards(): rho_full = lax.psum(partial_rho, 'dz')  7.39 us
    all_to_all x1, starting transfers between devices, shards(): lax.all_to_all(outgoing.reshape(receivers * CAP * SLOTS, PW), ('prow', 'p...  3.41 us
    unnamed x18, local copies, waits for them, and re-layouts  2.87 us
    dot_general x1, matrix products, shards(): lax.dot_general(scaled, panel, (((1,), (1,)), ((), ())), preferred_elemen...  2.32 us
  transfers between devices with their start and end apart: 3, of which 3 were waited for; matrix products, arithmetic and copies ran while one was open for 3% of the time, Pallas kernels for 0%

commit v1 on v0

--- a/solution.py
+++ b/solution.py
@@ -1,12 +1,21 @@
+import functools
+
 import jax
 import jax.numpy as jnp
 from jax import lax
+from jax.experimental import pallas as pl
+from jax.experimental.pallas import tpu as pltpu
 from jax.sharding import PartitionSpec as P
 
 SLOTS = 16
+LIVE = 13
 NPROJ = 16
 PW = 512
 CAP = 2
+GATHER_LIMIT = 2**21
+
+F32 = jnp.float32
+BF16 = jnp.bfloat16
 
 
 def spread(block, axis, holder):
@@ -14,7 +23,7 @@
     return lax.psum(block, axis)
 
 
-def shards(
+def exchange_shards(
     coeffs, occupations, counts, intersection, phi_values, panel_values, proj_site, proj_panel
 ):
     n_row = lax.axis_size("prow")
@@ -91,6 +100,205 @@
     return (density, rho_full.reshape(atoms_own, NPROJ * NPROJ))
 
 
+def iota(shape, dim):
+    return lax.broadcasted_iota(jnp.int32, shape, dim)
+
+
+def pick(condition):
+    return jnp.where(condition, 1.0, 0.0).astype(BF16)
+
+
+def take(left, right):
+    return jnp.dot(left, right, preferred_element_type=F32).astype(BF16)
+
+
+def packed_rows(rows):
+    return rows // SLOTS * LIVE + 16
+
+
+def pack_kernel(counts_ref, occ_ref, coeffs_ref, out_ref):
+    rows = coeffs_ref.shape[0]
+    atoms = rows // SLOTS
+    first = lax.axis_index("prow") * atoms
+    group = 16
+    old = iota((group * LIVE, group * SLOTS), 1)
+    new = iota((group * LIVE, group * SLOTS), 0)
+    slot = old & (SLOTS - 1)
+    move = pick(((old >> 4) * LIVE + slot == new) & (slot < LIVE))
+    lane_slot = iota((SLOTS, coeffs_ref.shape[1]), 0)
+    for g in range(atoms // group):
+        tiles = []
+        for a in range(group):
+            at = (g * group + a) * SLOTS
+            tile = coeffs_ref[at : at + SLOTS, :]
+            tiles.append(jnp.where(lane_slot < counts_ref[first + g * group + a], tile, jnp.zeros_like(tile)))
+        block = jnp.concatenate(tiles, axis=0)
+        out_ref[g * group * LIVE : (g + 1) * group * LIVE, :] = jnp.dot(
+            move, block, preferred_element_type=F32
+        ).astype(BF16)
+    weights = occ_ref[...].astype(F32) * 0.5
+    out_ref[atoms * LIVE :, :] = jnp.broadcast_to(weights, (16, weights.shape[1])).astype(BF16)
+
+
+def left_kernel(n_col, n_slab, lists_ref, phi_ref, panel_ref, site_ref, proj_ref, out_ref):
+    x, z, s = lax.axis_index("prow"), lax.axis_index("pcol"), lax.axis_index("dz")
+    cells, listed = phi_ref.shape[0], lists_ref.shape[1]
+    packed = out_ref.shape[2]
+    own = site_ref.shape[0]
+    atoms_own = own // NPROJ
+    blk_atoms = (packed - 16) // LIVE
+    domain = (x * n_col + z) * n_slab + s
+    slot = iota((SLOTS, packed), 0)
+    new = iota((SLOTS, packed), 1)
+    old = iota((PW, packed), 0)
+    to_panel = pick(
+        ((old >> 4) * LIVE + (old & (SLOTS - 1)) == iota((PW, packed), 1)) & ((old & (SLOTS - 1)) < LIVE)
+    )
+    panel_side = take(jnp.concatenate([panel_ref[...], proj_ref[...]], axis=0), to_panel)
+    spread_lanes = pick(iota((SLOTS, own), 0) == (iota((SLOTS, own), 1) & (SLOTS - 1)))
+    tiled = take(site_ref[...], spread_lanes)
+    mine = (iota((own, own), 0) & (atoms_own - 1)) == (iota((own, own), 1) >> 4)
+    tiled = jnp.where(mine, tiled, jnp.zeros_like(tiled))
+    to_own = jnp.concatenate(
+        [pick((new == (z * atoms_own + a) * LIVE + slot) & (slot < LIVE)) for a in range(atoms_own)], axis=0
+    )
+    site_side = take(tiled, to_own)
+    for b in range(2):
+        to_listed = jnp.concatenate(
+            [
+                pick(
+                    (new == (lists_ref[domain, p] - b * blk_atoms) * LIVE + slot)
+                    & (slot < LIVE)
+                    & (new < blk_atoms * LIVE)
+                )
+                for p in range(listed)
+            ],
+            axis=0,
+        )
+        out_ref[b, 0:cells, :] = take(phi_ref[...], to_listed)
+        if b == 0:
+            out_ref[b, cells : 2 * cells, :] = panel_side[:cells]
+            out_ref[b, 2 * cells + own :, :] = panel_side[cells:]
+        else:
+            out_ref[b, cells : 2 * cells, :] = jnp.zeros((cells, packed), BF16)
+            out_ref[b, 2 * cells + own :, :] = jnp.zeros((own, packed), BF16)
+        out_ref[b, 2 * cells : 2 * cells + own, :] = jnp.where(x == b, site_side, jnp.zeros_like(site_side))
+
+
+def sum_kernel(n_pairs, cells, left_ref, *refs):
+    blocks, (density_ref, rho_ref) = refs[: 2 * n_pairs], refs[2 * n_pairs :]
+    x = lax.axis_index("prow")
+    swapped = x ^ (lax.axis_index("dz") & 1)
+    own = left_ref.shape[1] - 2 * cells
+    own = own // 2
+    weight_row = left_ref.shape[2] - 16
+    total = None
+    rho = None
+    for k in range(n_pairs):
+        near = x if k == 0 else swapped
+        a_ref, b_ref = blocks[2 * k], blocks[2 * k + 1]
+        r = jnp.dot(left_ref[near], a_ref[...], preferred_element_type=F32)
+        r += jnp.dot(left_ref[1 - near], b_ref[...], preferred_element_type=F32)
+        f = a_ref[weight_row : weight_row + 16, :].astype(F32)[0:1]
+        term = r[:cells] * f * r[cells : 2 * cells]
+        part = lax.dot_general(
+            r[2 * cells : 2 * cells + own] * f,
+            r[2 * cells + own :],
+            (((1,), (1,)), ((), ())),
+            precision=lax.Precision.HIGHEST,
+            preferred_element_type=F32,
+        )
+        total = term if total is None else total + term
+        rho = part if rho is None else rho + part
+    density_ref[...] = jnp.sum(total.T, axis=0, keepdims=True)
+    atoms = own // NPROJ
+    rho = jnp.where((iota((own, own), 0) & (atoms - 1)) == (iota((own, own), 1) >> 4), rho, 0.0)
+    wide = NPROJ * NPROJ
+    fold = jnp.where(
+        (iota((own, wide), 0) & (NPROJ - 1)) == (iota((own, wide), 1) & (NPROJ - 1)), 1.0, 0.0
+    ).astype(F32)
+    rows = jnp.dot(rho, fold, precision=lax.Precision.HIGHEST, preferred_element_type=F32)
+    keep = (iota((own, wide), 0) // atoms) == (iota((own, wide), 1) >> 4)
+    rho_ref[...] = jnp.sum(jnp.where(keep, rows, 0.0).reshape(NPROJ, atoms, wide), axis=0)
+
+
+VMEM = pl.BlockSpec(memory_space=pltpu.VMEM)
+SMEM = pl.BlockSpec(memory_space=pltpu.SMEM)
+PARAMS = pltpu.CompilerParams(vmem_limit_bytes=32 * 2**20)
+
+
+def gather_shards(
+    coeffs, occupations, counts, intersection, phi_values, panel_values, proj_site, proj_panel
+):
+    n_row, n_col, n_slab = (lax.axis_size(a) for a in ("prow", "pcol", "dz"))
+    axes = ("prow", "pcol", "dz")
+
+    def move(block, target):
+        pairs = []
+        for i in range(n_row * n_col * n_slab):
+            x, z, s = i // (n_col * n_slab), i // n_slab % n_col, i % n_slab
+            tx, tz, ts = target(x, z, s)
+            pairs.append((i, (tx * n_col + tz) * n_slab + ts))
+        return lax.ppermute(block, axes, pairs)
+
+    rows, states = coeffs.shape
+    packed = packed_rows(rows)
+    atoms_own = proj_site.shape[0]
+    own = atoms_own * NPROJ
+    cells = phi_values.shape[0]
+    block = pl.pallas_call(
+        pack_kernel,
+        out_shape=jax.ShapeDtypeStruct((packed, states), BF16),
+        in_specs=[SMEM, VMEM, VMEM],
+        out_specs=VMEM,
+        compiler_params=PARAMS,
+    )(counts, occupations.reshape(1, states), coeffs)
+    got = {}
+    for k in list(range(n_col - 1, 0, -1)):
+        got[k] = move(block, lambda x, z, s: (x ^ (s & 1), z ^ k, s))
+    other = move(block, lambda x, z, s: (x ^ 1, z, s))
+    half = move(proj_panel, lambda x, z, s: (x, z, s ^ 2))
+    slab = lax.axis_index("dz")
+    mine_first = (slab & 2) == 0
+    pair = jnp.stack([jnp.where(mine_first, proj_panel, half), jnp.where(mine_first, half, proj_panel)])
+    swap = move(pair, lambda x, z, s: (x, z, s ^ 1))
+    even = (slab & 1) == 0
+    evens, odds = jnp.where(even, pair, swap), jnp.where(even, swap, pair)
+    whole = jnp.stack([evens[0], odds[0], evens[1], odds[1]], axis=2).reshape(own, PW)
+    site = proj_site.transpose(1, 0, 2).reshape(own, SLOTS)
+    left = pl.pallas_call(
+        functools.partial(left_kernel, n_col, n_slab),
+        out_shape=jax.ShapeDtypeStruct((2, 2 * cells + 2 * own, packed), BF16),
+        in_specs=[SMEM, VMEM, VMEM, VMEM, VMEM],
+        out_specs=VMEM,
+        compiler_params=PARAMS,
+        cost_estimate=pl.CostEstimate(flops=2 * 10**8, bytes_accessed=2 * 10**6, transcendentals=0),
+    )(intersection, phi_values, panel_values, site, whole)
+    blocks = [block, other]
+    for k in got:
+        blocks += [got[k], move(got[k], lambda x, z, s: (x, z, s ^ 1))]
+    density, rho = pl.pallas_call(
+        functools.partial(sum_kernel, n_col, cells),
+        out_shape=(
+            jax.ShapeDtypeStruct((1, cells), F32),
+            jax.ShapeDtypeStruct((atoms_own, NPROJ * NPROJ), F32),
+        ),
+        in_specs=[VMEM] * (1 + len(blocks)),
+        out_specs=(VMEM, VMEM),
+        compiler_params=PARAMS,
+    )(left, *blocks)
+    return density.reshape(cells), rho
+
+
+def shards(coeffs, occupations, counts, intersection, phi_values, panel_values, proj_site, proj_panel):
+    n_row, n_col, n_slab = (lax.axis_size(a) for a in ("prow", "pcol", "dz"))
+    rows = coeffs.shape[0]
+    fits = coeffs.size * 2 * n_row * n_col <= GATHER_LIMIT
+    regular = n_row == 2 and n_col == 4 and n_slab == 4 and rows >= PW and rows % 256 == 0
+    plan = gather_shards if fits and regular else exchange_shards
+    return plan(coeffs, occupations, counts, intersection, phi_values, panel_values, proj_site, proj_panel)
+
+
 def solution(mesh):
     return jax.shard_map(
         shards,

time: 88.5 us -> 28.7 us (0.32)
  waiting for transfers between devices: 50.5 us -> 9.38 us
  between operations: 14.2 us -> 0.77 us
  blocking collectives: 7.39 us -> 0 us
  starting transfers between devices: 3.49 us -> 10.1 us
  Pallas kernels: 0 us -> 5.13 us
  other arithmetic: 4.31 us -> 0.81 us
  matrix products: 3.4 us -> 0 us
  local copies, waits for them, and re-layouts: 4.77 us -> 2.34 us
    reduce_scatter x1 -> x0, waiting for transfers between devices: 25 us -> none  [shards(): lax.psum_scatter(lax.dot_general(scaled, panel, (((1,), (1,)), ((), ())),...]
    psum x1 -> x0, waiting for transfers between devices: 24 us -> none  [spread(): return lax.psum(block, axis)]
    ppermute x0 -> x9, starting transfers between devices: none -> 10.1 us  [move(): return lax.ppermute(block, axes, pairs)]
    ppermute x0 -> x9, waiting for transfers between devices: none -> 9.38 us  [move(): return lax.ppermute(block, axes, pairs)]
    psum x1 -> x0, blocking collectives: 7.39 us -> none  [shards(): rho_full = lax.psum(partial_rho, 'dz')]
    pallas_call x0 -> x3, Pallas kernels: none -> 5.13 us  [the longest x1 2.98 us: gather_shards(): pl.pallas_call(functools.partial(sum_kernel, n_col, cells), out_shape=(ja...]
    all_to_all x1 -> x0, starting transfers between devices: 3.41 us -> none  [shards(): lax.all_to_all(outgoing.reshape(receivers * CAP * SLOTS, PW), ('prow', 'p...]
    dot_general x4 -> x0, matrix products: 3.4 us -> none  [the longest x1 2.32 us: shards(): lax.dot_general(scaled, panel, (((1,), (1,)), ((), ())), preferred_elemen...]
  transfers between devices with their start and end apart: 3 -> 9, of which waited for: 3 -> 3; matrix products, arithmetic and copies ran while one was open for 3% -> 1% of each run, Pallas kernels for 0% -> 8%
where the time goes in v1:
time: 28.7 us; the launch traced here: 28.5 us
  starting transfers between devices  10.1 us (35%)
  waiting for transfers between devices  9.38 us (33%)
  Pallas kernels  5.13 us (18%)
  local copies, waits for them, and re-layouts  2.34 us (8%)
  other arithmetic  0.81 us (3%)
  between operations  0.77 us (3%)
    ppermute x9, starting transfers between devices, move(): return lax.ppermute(block, axes, pairs)  10.1 us
    ppermute x9, waiting for transfers between devices, move(): return lax.ppermute(block, axes, pairs)  9.38 us
    pallas_call x1, Pallas kernels, gather_shards(): pl.pallas_call(functools.partial(sum_kernel, n_col, cells), out_shape=(ja...  2.98 us
    unnamed x16, local copies, waits for them, and re-layouts  2.21 us
    pallas_call x1, Pallas kernels, gather_shards(): pl.pallas_call(functools.partial(left_kernel, n_col, n_slab), out_shape=j...  1.38 us
    another operation x2, other arithmetic, gather_shards(): jnp.stack([jnp.where(mine_first, proj_panel, half), jnp.where(mine_first,...  0.77 us
    pallas_call x1, Pallas kernels, gather_shards(): pl.pallas_call(pack_kernel, out_shape=jax.ShapeDtypeStruct((packed, state...  0.77 us
  transfers between devices with their start and end apart: 9, of which 3 were waited for; matrix products, arithmetic and copies ran while one was open for 1% of the time, Pallas kernels for 8%

profile of v1, /device:TPU:0, one launch (start us, length us, event | category | flops | bytes accessed | tf_op | source)
XLA Modules:
  0.0 28.5 jit_solution(14660661797444673645)
XLA Ops:
  0.6 3.0 %collective-permute-start = (bf16[8,16,128]{2,1,0:T(8,128)(2,1)}, bf16[8,16,128]{2,1,0:T(8,128)(2,1)S(1)}, u32[]{:S(2)}, u32[]{:S(2)}) collective-permute-start(bf16[8,16,128]{2,1,0:T(8,128)(2,1)} %param.15), channel_id=1, source_target_pairs={{0,2},{1,3},{2,0},{3,1},{4,6},{5,7},{6,4},{7,5},{8,10},{9,11},{10,... | collective-permute-start | bytes 98312 | tf_op jit(solution)/shard_map/ppermute | solution.py:242
  3.7 2.1 %collective-permute-done = bf16[8,16,128]{2,1,0:T(8,128)(2,1)S(1)} collective-permute-done((bf16[8,16,128]{2,1,0:T(8,128)(2,1)}, bf16[8,16,128]{2,1,0:T(8,128)(2,1)S(1)}, u32[]{:S(2)}, u32[]{:S(2)}) %collective-permute-start) | collective-permute-done | bytes 32800 | tf_op jit(solution)/shard_map/ppermute | solution.py:242
  5.8 0.8 %select_bitcast_fusion.1 = (bf16[1,8,16,128]{3,2,1,0:T(8,128)(2,1)S(1)}, bf16[1,8,16,128]{3,2,1,0:T(8,128)(2,1)S(1)}) fusion(bf16[8,16,128]{2,1,0:T(8,128)(2,1)} %param.15, bf16[8,16,128]{2,1,0:T(8,128)(2,1)S(1)} %collective-permute-done, pred[]{:T(512)S(6)} %eq.7), kind=kLoop, calls=%fused_computation.11 | loop fusion | flops 32768 | bytes 131073 | tf_op jit(solution)/shard_map/stack | solution.py:263
  6.5 0.0 copy-start.3
  6.6 0.0 copy-start.4
  6.6 0.1 collective-permute-start.1
  6.7 0.5 %copy-done.3 = s32[64]{0:T(128)S(1)} copy-done((s32[64]{0:T(128)S(1)}, s32[64]{0:T(128)}, u32[]{:S(2)}) %copy-start.3) | copy-done | bytes 280
  7.2 0.0 copy-done.4
  7.2 0.8 %shard_map.96.refs_0_ = bf16[432,128]{1,0:T(8,128)(2,1)S(1)} custom-call(s32[64]{0:T(128)S(1)} %copy-done.3, s32[1,128]{1,0:T(1,128)S(1)} %bitcast.25, bf16[512,128]{1,0:T(8,128)(2,1)S(1)} %copy-done), custom_call_target="tpu_custom_call" | custom-call | tf_op jit(solution)/shard_map/pallas_call | solution.py:249
  8.0 4.2 %collective-permute-start.3 = (bf16[432,128]{1,0:T(8,128)(2,1)S(1)}, bf16[432,128]{1,0:T(8,128)(2,1)S(1)}, u32[]{:S(2)}, u32[]{:S(2)}) collective-permute-start(bf16[432,128]{1,0:T(8,128)(2,1)S(1)} %shard_map.96.refs_0_), channel_id=1, source_target_pairs={{0,12},{1,29},{2,14},{3,31},{4,8},{5,25},{6,10},{7,27},{8,4},{9,21... | collective-permute-start | bytes 331784 | tf_op jit(solution)/shard_map/ppermute | solution.py:242
  12.2 0.0 collective-permute-start.5
  12.2 0.6 %collective-permute-start.7 = (bf16[432,128]{1,0:T(8,128)(2,1)S(1)}, bf16[432,128]{1,0:T(8,128)(2,1)S(1)}, u32[]{:S(2)}, u32[]{:S(2)}) collective-permute-start(bf16[432,128]{1,0:T(8,128)(2,1)S(1)} %shard_map.96.refs_0_), channel_id=1, source_target_pairs={{0,4},{1,21},{2,6},{3,23},{4,0},{5,17},{6,2},{7,19},{8,12},{9,29},... | collective-permute-start | bytes 331784 | tf_op jit(solution)/shard_map/ppermute | solution.py:242
  12.8 1.6 %collective-permute-start.2 = (bf16[432,128]{1,0:T(8,128)(2,1)S(1)}, bf16[432,128]{1,0:T(8,128)(2,1)S(1)}, u32[]{:S(2)}, u32[]{:S(2)}) collective-permute-start(bf16[432,128]{1,0:T(8,128)(2,1)S(1)} %shard_map.96.refs_0_), channel_id=1, source_target_pairs={{0,16},{1,17},{2,18},{3,19},{4,20},{5,21},{6,22},{7,23},{8,24},{9,... | collective-permute-start | bytes 331784 | tf_op jit(solution)/shard_map/ppermute | solution.py:242
  14.5 0.7 %copy-done.6 = s32[32,8]{0,1:T(8,128)S(1)} copy-done((s32[32,8]{0,1:T(8,128)S(1)}, s32[32,8]{0,1:T(8,128)}, u32[]{:S(2)}) %copy-start.6) | copy-done | bytes 1048
  15.1 0.1 copy.12.lists_ref
  15.3 0.9 %collective-permute-done.3.refs_2_ = bf16[432,128]{1,0:T(8,128)(2,1)S(1)} collective-permute-done((bf16[432,128]{1,0:T(8,128)(2,1)S(1)}, bf16[432,128]{1,0:T(8,128)(2,1)S(1)}, u32[]{:S(2)}, u32[]{:S(2)}) %collective-permute-start.3) | collective-permute-done | bytes 110624 | tf_op jit(solution)/shard_map/ppermute | solution.py:242
  16.1 6.4 %collective-permute-done.5.refs_4_ = bf16[432,128]{1,0:T(8,128)(2,1)S(1)} collective-permute-done((bf16[432,128]{1,0:T(8,128)(2,1)S(1)}, bf16[432,128]{1,0:T(8,128)(2,1)S(1)}, u32[]{:S(2)}, u32[]{:S(2)}) %collective-permute-start.5) | collective-permute-done | bytes 110624 | tf_op jit(solution)/shard_map/ppermute | solution.py:242
  22.5 0.5 %collective-permute-start.8 = (bf16[432,128]{1,0:T(8,128)(2,1)S(1)}, bf16[432,128]{1,0:T(8,128)(2,1)S(1)}, u32[]{:S(2)}, u32[]{:S(2)}) collective-permute-start(bf16[432,128]{1,0:T(8,128)(2,1)S(1)} %collective-permute-done.7.refs_6_), channel_id=1, source_target_pairs={{0,1},{1,0},{2,3},{3,2},{4,5},{5,4},{6,7},{7,6},{8,9},{9,8},{10,11... | collective-permute-start | bytes 331784 | tf_op jit(solution)/shard_map/ppermute | solution.py:242
  23.1 0.1 copy.11
  23.2 0.0 copy-start.1
  23.2 0.0 copy-start.2
  23.2 0.9 %copy-done.1 = bf16[128,512]{1,0:T(8,128)(2,1)S(1)} copy-done((bf16[128,512]{1,0:T(8,128)(2,1)S(1)}, bf16[128,512]{1,0:T(8,128)(2,1)}, u32[]{:S(2)}) %copy-start.1) | copy-done | bytes 131096
  24.1 1.4 %shard_map.95.left_ref = bf16[2,512,432]{2,1,0:T(8,128)(2,1)S(1)} custom-call(s32[32,8]{1,0:T(8,128)S(1)} %copy.12.lists_ref, bf16[128,128]{1,0:T(8,128)(2,1)S(1)} %copy-done.2, bf16[128,512]{1,0:T(8,128)(2,1)S(1)} %copy-done.1, bf16[128,16]{1,0:T(8,128)(2,1)S(1)} %bitcast.24, bf16[128,512]{1,0:T(8,128)(2,1)S(1)} %bitcast.23), custom_call_target="tpu_custom_call" | custom-call | flops 200000000 | bytes 2000000 | tf_op jit(solution)/shard_map/pallas_call | solution.py:269
  25.5 3.0 %shard_map.97 = (f32[1,128]{1,0:T(1,128)}, f32[8,256]{1,0:T(8,128)}) custom-call(bf16[2,512,432]{2,1,0:T(8,128)(2,1)S(1)} %shard_map.95.left_ref, bf16[432,128]{1,0:T(8,128)(2,1)S(1)} %shard_map.96.refs_0_, bf16[432,128]{1,0:T(8,128)(2,1)S(1)} %collective-permute-done.2.refs_1_, bf16[432,128]{1,0:T(8,128)(2,1)S(1)} %collective-permute-done.3.refs_2_, ...), custom_call_target="tpu_custom_call" | custom-call | tf_op jit(solution)/shard_map/pallas_call | solution.py:280
  (20 shorter events, 0.1 us)
Async XLA Ops:
  0.6 5.1 %collective-permute-start = (bf16[8,16,128]{2,1,0:T(8,128)(2,1)}, bf16[8,16,128]{2,1,0:T(8,128)(2,1)S(1)}, u32[]{:S(2)}, u32[]{:S(2)}) collective-permute-start(bf16[8,16,128]{2,1,0:T(8,128)(2,1)} %param.15), channel_id=1, source_target_pairs={{0,2},{1,3},{2,0},{3,1},{4,6},{5,7},{6,4},{7,5},{8,10},{9,11},{10,... | collective-permute-start | bytes 98312 | tf_op jit(solution)/shard_map/ppermute | solution.py:242
  3.7 3.0 %copy-start = (bf16[512,128]{1,0:T(8,128)(2,1)S(1)}, bf16[512,128]{1,0:T(8,128)(2,1)}, u32[]{:S(2)}) copy-start(bf16[512,128]{1,0:T(8,128)(2,1)} %coeffs_ref.1) | copy-start | bytes 393220
  6.5 0.7 %copy-start.3 = (s32[64]{0:T(128)S(1)}, s32[64]{0:T(128)}, u32[]{:S(2)}) copy-start(s32[64]{0:T(128)} %counts_ref.1) | copy-start | bytes 772
  6.6 0.7 %copy-start.4 = (s32[128]{0:T(128)S(1)}, s32[128]{0:T(128)}, u32[]{:S(2)}) copy-start(s32[128]{0:T(128)} %param.9) | copy-start | bytes 1540
  6.6 8.6 %collective-permute-start.1 = (bf16[2,8,16,128]{3,2,1,0:T(8,128)(2,1)S(1)}, bf16[2,8,16,128]{3,2,1,0:T(8,128)(2,1)S(1)}, u32[]{:S(2)}, u32[]{:S(2)}) collective-permute-start(bf16[2,8,16,128]{3,2,1,0:T(8,128)(2,1)S(1)} %pad_maximum_fusion.1), channel_id=1, source_target_pairs={{0,1},{1,0},{2,3},{3,2},{4,5},{5,4},{6,7},{7,6},{8,9},{9,8},{10,11... | collective-permute-start | bytes 196616 | tf_op jit(solution)/shard_map/ppermute | solution.py:242
  7.2 7.2 %copy-start.5 = (bf16[8,16,16]{2,1,0:T(8,128)(2,1)S(1)}, bf16[8,16,16]{2,1,0:T(8,128)(2,1)}, u32[]{:S(2)}) copy-start(bf16[8,16,16]{2,1,0:T(8,128)(2,1)} %param.14) | copy-start | bytes 12292
  8.0 8.1 %collective-permute-start.3 = (bf16[432,128]{1,0:T(8,128)(2,1)S(1)}, bf16[432,128]{1,0:T(8,128)(2,1)S(1)}, u32[]{:S(2)}, u32[]{:S(2)}) collective-permute-start(bf16[432,128]{1,0:T(8,128)(2,1)S(1)} %shard_map.96.refs_0_), channel_id=1, source_target_pairs={{0,12},{1,29},{2,14},{3,31},{4,8},{5,25},{6,10},{7,27},{8,4},{9,21... | collective-permute-start | bytes 331784 | tf_op jit(solution)/shard_map/ppermute | solution.py:242
  12.2 10.4 %collective-permute-start.5 = (bf16[432,128]{1,0:T(8,128)(2,1)S(1)}, bf16[432,128]{1,0:T(8,128)(2,1)S(1)}, u32[]{:S(2)}, u32[]{:S(2)}) collective-permute-start(bf16[432,128]{1,0:T(8,128)(2,1)S(1)} %shard_map.96.refs_0_), channel_id=1, source_target_pairs={{0,8},{1,25},{2,10},{3,27},{4,12},{5,29},{6,14},{7,31},{8,0},{9,17... | collective-permute-start | bytes 331784 | tf_op jit(solution)/shard_map/ppermute | solution.py:242
  12.2 10.4 %collective-permute-start.7 = (bf16[432,128]{1,0:T(8,128)(2,1)S(1)}, bf16[432,128]{1,0:T(8,128)(2,1)S(1)}, u32[]{:S(2)}, u32[]{:S(2)}) collective-permute-start(bf16[432,128]{1,0:T(8,128)(2,1)S(1)} %shard_map.96.refs_0_), channel_id=1, source_target_pairs={{0,4},{1,21},{2,6},{3,23},{4,0},{5,17},{6,2},{7,19},{8,12},{9,29},... | collective-permute-start | bytes 331784 | tf_op jit(solution)/shard_map/ppermute | solution.py:242
  12.8 12.7 %collective-permute-start.2 = (bf16[432,128]{1,0:T(8,128)(2,1)S(1)}, bf16[432,128]{1,0:T(8,128)(2,1)S(1)}, u32[]{:S(2)}, u32[]{:S(2)}) collective-permute-start(bf16[432,128]{1,0:T(8,128)(2,1)S(1)} %shard_map.96.refs_0_), channel_id=1, source_target_pairs={{0,16},{1,17},{2,18},{3,19},{4,20},{5,21},{6,22},{7,23},{8,24},{9,... | collective-permute-start | bytes 331784 | tf_op jit(solution)/shard_map/ppermute | solution.py:242
  14.4 0.7 %copy-start.6 = (s32[32,8]{0,1:T(8,128)S(1)}, s32[32,8]{0,1:T(8,128)}, u32[]{:S(2)}) copy-start(s32[32,8]{0,1:T(8,128)} %param.11) | copy-start | bytes 3076
  16.1 9.3 %collective-permute-start.4 = (bf16[432,128]{1,0:T(8,128)(2,1)S(1)}, bf16[432,128]{1,0:T(8,128)(2,1)S(1)}, u32[]{:S(2)}, u32[]{:S(2)}) collective-permute-start(bf16[432,128]{1,0:T(8,128)(2,1)S(1)} %collective-permute-done.3.refs_2_), channel_id=1, source_target_pairs={{0,1},{1,0},{2,3},{3,2},{4,5},{5,4},{6,7},{7,6},{8,9},{9,8},{10,11... | collective-permute-start | bytes 331784 | tf_op jit(solution)/shard_map/ppermute | solution.py:242
  22.5 3.0 %collective-permute-start.6 = (bf16[432,128]{1,0:T(8,128)(2,1)S(1)}, bf16[432,128]{1,0:T(8,128)(2,1)S(1)}, u32[]{:S(2)}, u32[]{:S(2)}) collective-permute-start(bf16[432,128]{1,0:T(8,128)(2,1)S(1)} %collective-permute-done.5.refs_4_), channel_id=1, source_target_pairs={{0,1},{1,0},{2,3},{3,2},{4,5},{5,4},{6,7},{7,6},{8,9},{9,8},{10,11... | collective-permute-start | bytes 331784 | tf_op jit(solution)/shard_map/ppermute | solution.py:242
  22.5 3.0 %collective-permute-start.8 = (bf16[432,128]{1,0:T(8,128)(2,1)S(1)}, bf16[432,128]{1,0:T(8,128)(2,1)S(1)}, u32[]{:S(2)}, u32[]{:S(2)}) collective-permute-start(bf16[432,128]{1,0:T(8,128)(2,1)S(1)} %collective-permute-done.7.refs_6_), channel_id=1, source_target_pairs={{0,1},{1,0},{2,3},{3,2},{4,5},{5,4},{6,7},{7,6},{8,9},{9,8},{10,11... | collective-permute-start | bytes 331784 | tf_op jit(solution)/shard_map/ppermute | solution.py:242
  23.2 0.9 %copy-start.1 = (bf16[128,512]{1,0:T(8,128)(2,1)S(1)}, bf16[128,512]{1,0:T(8,128)(2,1)}, u32[]{:S(2)}) copy-start(bf16[128,512]{1,0:T(8,128)(2,1)} %panel_ref.1) | copy-start | bytes 393220
  23.2 0.9 %copy-start.2 = (bf16[128,128]{1,0:T(8,128)(2,1)S(1)}, bf16[128,128]{1,0:T(8,128)(2,1)}, u32[]{:S(2)}) copy-start(bf16[128,128]{1,0:T(8,128)(2,1)} %phi_ref.1) | copy-start | bytes 98308

commit v2 on v1

--- a/solution.py
+++ b/solution.py
@@ -116,31 +116,44 @@
     return rows // SLOTS * LIVE + 16
 
 
-def pack_kernel(counts_ref, occ_ref, coeffs_ref, out_ref):
+def pack_kernel(occ_ref, coeffs_ref, out_ref, occ, held, arrived):
     rows = coeffs_ref.shape[0]
-    atoms = rows // SLOTS
-    first = lax.axis_index("prow") * atoms
     group = 16
-    old = iota((group * LIVE, group * SLOTS), 1)
-    new = iota((group * LIVE, group * SLOTS), 0)
+    span = group * SLOTS
+    copies = [
+        pltpu.make_async_copy(
+            coeffs_ref.at[pl.ds(g * span, span)], held.at[pl.ds(g * span, span)], arrived.at[g]
+        )
+        for g in range(rows // span)
+    ]
+    last = pltpu.make_async_copy(occ_ref, occ, arrived.at[rows // span])
+    for copy in copies:
+        copy.start()
+    last.start()
+    old = iota((group * LIVE, span), 1)
     slot = old & (SLOTS - 1)
-    move = pick(((old >> 4) * LIVE + slot == new) & (slot < LIVE))
-    lane_slot = iota((SLOTS, coeffs_ref.shape[1]), 0)
-    for g in range(atoms // group):
-        tiles = []
-        for a in range(group):
-            at = (g * group + a) * SLOTS
-            tile = coeffs_ref[at : at + SLOTS, :]
-            tiles.append(jnp.where(lane_slot < counts_ref[first + g * group + a], tile, jnp.zeros_like(tile)))
-        block = jnp.concatenate(tiles, axis=0)
-        out_ref[g * group * LIVE : (g + 1) * group * LIVE, :] = jnp.dot(
-            move, block, preferred_element_type=F32
-        ).astype(BF16)
-    weights = occ_ref[...].astype(F32) * 0.5
-    out_ref[atoms * LIVE :, :] = jnp.broadcast_to(weights, (16, weights.shape[1])).astype(BF16)
-
-
-def left_kernel(n_col, n_slab, lists_ref, phi_ref, panel_ref, site_ref, proj_ref, out_ref):
+    move = pick(((old >> 4) * LIVE + slot == iota((group * LIVE, span), 0)) & (slot < LIVE))
+    for g, copy in enumerate(copies):
+        copy.wait()
+        out_ref[g * group * LIVE : (g + 1) * group * LIVE, :] = take(move, held[g * span : (g + 1) * span, :])
+    last.wait()
+    weights = occ[...].reshape(1, occ.shape[0]).astype(F32) * 0.5
+    out_ref[rows // SLOTS * LIVE :, :] = jnp.broadcast_to(weights, (16, weights.shape[1])).astype(BF16)
+
+
+def panel_map(counts_ref, packed, first=lambda t: t):
+    slot = iota((SLOTS, packed), 0)
+    new = iota((SLOTS, packed), 1)
+    return jnp.concatenate(
+        [
+            pick((new == first(t) * LIVE + slot) & (slot < counts_ref[first(t)]))
+            for t in range(PW // SLOTS)
+        ],
+        axis=0,
+    )
+
+
+def left_kernel(n_col, n_slab, lists_ref, counts_ref, phi_ref, panel_ref, site_ref, out_ref):
     x, z, s = lax.axis_index("prow"), lax.axis_index("pcol"), lax.axis_index("dz")
     cells, listed = phi_ref.shape[0], lists_ref.shape[1]
     packed = out_ref.shape[2]
@@ -150,17 +163,17 @@
     domain = (x * n_col + z) * n_slab + s
     slot = iota((SLOTS, packed), 0)
     new = iota((SLOTS, packed), 1)
-    old = iota((PW, packed), 0)
-    to_panel = pick(
-        ((old >> 4) * LIVE + (old & (SLOTS - 1)) == iota((PW, packed), 1)) & ((old & (SLOTS - 1)) < LIVE)
-    )
-    panel_side = take(jnp.concatenate([panel_ref[...], proj_ref[...]], axis=0), to_panel)
     spread_lanes = pick(iota((SLOTS, own), 0) == (iota((SLOTS, own), 1) & (SLOTS - 1)))
     tiled = take(site_ref[...], spread_lanes)
     mine = (iota((own, own), 0) & (atoms_own - 1)) == (iota((own, own), 1) >> 4)
     tiled = jnp.where(mine, tiled, jnp.zeros_like(tiled))
+    first = z * atoms_own
     to_own = jnp.concatenate(
-        [pick((new == (z * atoms_own + a) * LIVE + slot) & (slot < LIVE)) for a in range(atoms_own)], axis=0
+        [
+            pick((new == (first + a) * LIVE + slot) & (slot < counts_ref[x * blk_atoms + first + a]))
+            for a in range(atoms_own)
+        ],
+        axis=0,
     )
     site_side = take(tiled, to_own)
     for b in range(2):
@@ -168,7 +181,7 @@
             [
                 pick(
                     (new == (lists_ref[domain, p] - b * blk_atoms) * LIVE + slot)
-                    & (slot < LIVE)
+                    & (slot < counts_ref[lists_ref[domain, p]])
                     & (new < blk_atoms * LIVE)
                 )
                 for p in range(listed)
@@ -176,54 +189,76 @@
             axis=0,
         )
         out_ref[b, 0:cells, :] = take(phi_ref[...], to_listed)
-        if b == 0:
-            out_ref[b, cells : 2 * cells, :] = panel_side[:cells]
-            out_ref[b, 2 * cells + own :, :] = panel_side[cells:]
-        else:
-            out_ref[b, cells : 2 * cells, :] = jnp.zeros((cells, packed), BF16)
-            out_ref[b, 2 * cells + own :, :] = jnp.zeros((own, packed), BF16)
         out_ref[b, 2 * cells : 2 * cells + own, :] = jnp.where(x == b, site_side, jnp.zeros_like(site_side))
-
-
-def sum_kernel(n_pairs, cells, left_ref, *refs):
-    blocks, (density_ref, rho_ref) = refs[: 2 * n_pairs], refs[2 * n_pairs :]
-    x = lax.axis_index("prow")
-    swapped = x ^ (lax.axis_index("dz") & 1)
-    own = left_ref.shape[1] - 2 * cells
-    own = own // 2
+    out_ref[0, cells : 2 * cells, :] = take(panel_ref[...], panel_map(counts_ref, packed))
+    out_ref[1, cells : 2 * cells, :] = jnp.zeros((cells, packed), BF16)
+
+
+def split(values):
+    high = values.astype(BF16)
+    return high, (values - high.astype(F32)).astype(BF16)
+
+
+ROWS_BY_ROWS = (((1,), (1,)), ((), ()))
+
+
+def partial_sums(a, b, near, cells, left_ref):
     weight_row = left_ref.shape[2] - 16
-    total = None
-    rho = None
-    for k in range(n_pairs):
-        near = x if k == 0 else swapped
-        a_ref, b_ref = blocks[2 * k], blocks[2 * k + 1]
-        r = jnp.dot(left_ref[near], a_ref[...], preferred_element_type=F32)
-        r += jnp.dot(left_ref[1 - near], b_ref[...], preferred_element_type=F32)
-        f = a_ref[weight_row : weight_row + 16, :].astype(F32)[0:1]
-        term = r[:cells] * f * r[cells : 2 * cells]
-        part = lax.dot_general(
-            r[2 * cells : 2 * cells + own] * f,
-            r[2 * cells + own :],
-            (((1,), (1,)), ((), ())),
-            precision=lax.Precision.HIGHEST,
-            preferred_element_type=F32,
-        )
-        total = term if total is None else total + term
-        rho = part if rho is None else rho + part
-    density_ref[...] = jnp.sum(total.T, axis=0, keepdims=True)
+    r = jnp.dot(left_ref[near], a, preferred_element_type=F32)
+    r += jnp.dot(left_ref[1 - near], b, preferred_element_type=F32)
+    f = a[weight_row:, :].astype(F32)[0:1]
+    term = r[:cells] * f * r[cells : 2 * cells]
+    half = term.shape[1] // 2
+    panel = jnp.where(near == 0, a, b)
+    projected = sum(
+        lax.dot_general(part, panel, ROWS_BY_ROWS, preferred_element_type=F32)
+        for part in split(r[2 * cells :] * f)
+    )
+    return term[:, :half] + term[:, half:], projected
+
+
+def early_kernel(
+    cells, n_slab, counts_ref, left_ref, a_ref, b_ref, c_ref, d_ref, here_ref, far_ref, term_ref, projected_ref, proj_ref
+):
+    x, s = lax.axis_index("prow"), lax.axis_index("dz")
+    odd = (s & 1) == 1
+    a = jnp.concatenate([a_ref[...], jnp.where(odd, d_ref[...], c_ref[...])], axis=1)
+    b = jnp.concatenate([b_ref[...], jnp.where(odd, c_ref[...], d_ref[...])], axis=1)
+    term_ref[...], projected_ref[...] = partial_sums(a, b, x, cells, left_ref)
+    atoms = PW // SLOTS // n_slab
+    columns = panel_map(
+        counts_ref, projected_ref.shape[1], lambda t: (s ^ (t // atoms)) * atoms + t % atoms
+    )
+    proj_ref[...] = take(jnp.concatenate([here_ref[...], far_ref[...]], axis=1), columns)
+
+
+def late_kernel(
+    cells, left_ref, a_ref, b_ref, c_ref, d_ref, term_ref, projected_ref, proj_ref, density_ref, rho_ref
+):
+    near = lax.axis_index("prow") ^ (lax.axis_index("dz") & 1)
+    a = jnp.concatenate([a_ref[...], c_ref[...]], axis=1)
+    b = jnp.concatenate([b_ref[...], d_ref[...]], axis=1)
+    term, projected = partial_sums(a, b, near, cells, left_ref)
+    term += term_ref[...]
+    projected += projected_ref[...]
+    density_ref[...] = jnp.sum(term.T, axis=0, keepdims=True)
+    own = proj_ref.shape[0]
     atoms = own // NPROJ
+    rho = sum(
+        lax.dot_general(part, proj_ref[...], ROWS_BY_ROWS, preferred_element_type=F32)
+        for part in split(projected)
+    )
     rho = jnp.where((iota((own, own), 0) & (atoms - 1)) == (iota((own, own), 1) >> 4), rho, 0.0)
     wide = NPROJ * NPROJ
-    fold = jnp.where(
-        (iota((own, wide), 0) & (NPROJ - 1)) == (iota((own, wide), 1) & (NPROJ - 1)), 1.0, 0.0
-    ).astype(F32)
-    rows = jnp.dot(rho, fold, precision=lax.Precision.HIGHEST, preferred_element_type=F32)
+    fold = pick((iota((own, wide), 0) & (NPROJ - 1)) == (iota((own, wide), 1) & (NPROJ - 1)))
+    rows = sum(jnp.dot(part, fold, preferred_element_type=F32) for part in split(rho))
     keep = (iota((own, wide), 0) // atoms) == (iota((own, wide), 1) >> 4)
     rho_ref[...] = jnp.sum(jnp.where(keep, rows, 0.0).reshape(NPROJ, atoms, wide), axis=0)
 
 
 VMEM = pl.BlockSpec(memory_space=pltpu.VMEM)
 SMEM = pl.BlockSpec(memory_space=pltpu.SMEM)
+HBM = pl.BlockSpec(memory_space=pltpu.HBM)
 PARAMS = pltpu.CompilerParams(vmem_limit_bytes=32 * 2**20)
 
 
@@ -241,52 +276,66 @@
             pairs.append((i, (tx * n_col + tz) * n_slab + ts))
         return lax.ppermute(block, axes, pairs)
 
+    def swap(block):
+        return move(block, lambda x, z, s: (x, z, s ^ 1))
+
     rows, states = coeffs.shape
     packed = packed_rows(rows)
     atoms_own = proj_site.shape[0]
     own = atoms_own * NPROJ
     cells = phi_values.shape[0]
+    pair = jnp.concatenate([proj_panel, swap(proj_panel)], axis=2)
+    far_pair = move(pair, lambda x, z, s: (x, z, s ^ 2))
     block = pl.pallas_call(
         pack_kernel,
         out_shape=jax.ShapeDtypeStruct((packed, states), BF16),
-        in_specs=[SMEM, VMEM, VMEM],
+        in_specs=[HBM, HBM],
         out_specs=VMEM,
+        scratch_shapes=[
+            pltpu.VMEM((states,), jnp.int32),
+            pltpu.VMEM((rows, states), BF16),
+            pltpu.SemaphoreType.DMA((rows // 256 + 1,)),
+        ],
         compiler_params=PARAMS,
-    )(counts, occupations.reshape(1, states), coeffs)
-    got = {}
-    for k in list(range(n_col - 1, 0, -1)):
-        got[k] = move(block, lambda x, z, s: (x ^ (s & 1), z ^ k, s))
+    )(
+        pltpu.with_memory_space_constraint(occupations, pltpu.HBM),
+        pltpu.with_memory_space_constraint(coeffs, pltpu.HBM),
+    )
+    got = {k: move(block, lambda x, z, s: (x ^ (s & 1), z ^ k, s)) for k in (2, 3, 1)}
     other = move(block, lambda x, z, s: (x ^ 1, z, s))
-    half = move(proj_panel, lambda x, z, s: (x, z, s ^ 2))
-    slab = lax.axis_index("dz")
-    mine_first = (slab & 2) == 0
-    pair = jnp.stack([jnp.where(mine_first, proj_panel, half), jnp.where(mine_first, half, proj_panel)])
-    swap = move(pair, lambda x, z, s: (x, z, s ^ 1))
-    even = (slab & 1) == 0
-    evens, odds = jnp.where(even, pair, swap), jnp.where(even, swap, pair)
-    whole = jnp.stack([evens[0], odds[0], evens[1], odds[1]], axis=2).reshape(own, PW)
     site = proj_site.transpose(1, 0, 2).reshape(own, SLOTS)
     left = pl.pallas_call(
         functools.partial(left_kernel, n_col, n_slab),
-        out_shape=jax.ShapeDtypeStruct((2, 2 * cells + 2 * own, packed), BF16),
-        in_specs=[SMEM, VMEM, VMEM, VMEM, VMEM],
+        out_shape=jax.ShapeDtypeStruct((2, 2 * cells + own, packed), BF16),
+        in_specs=[SMEM, SMEM, VMEM, VMEM, VMEM],
         out_specs=VMEM,
         compiler_params=PARAMS,
         cost_estimate=pl.CostEstimate(flops=2 * 10**8, bytes_accessed=2 * 10**6, transcendentals=0),
-    )(intersection, phi_values, panel_values, site, whole)
-    blocks = [block, other]
-    for k in got:
-        blocks += [got[k], move(got[k], lambda x, z, s: (x, z, s ^ 1))]
+    )(intersection, counts, phi_values, panel_values, site)
+    got[2], left = lax.optimization_barrier((got[2], left))
+    got[3], far_pair = lax.optimization_barrier((got[3], far_pair))
+    swapped = {k: swap(got[k]) for k in got}
+    early = pl.pallas_call(
+        functools.partial(early_kernel, cells, n_slab),
+        out_shape=(
+            jax.ShapeDtypeStruct((cells, states), F32),
+            jax.ShapeDtypeStruct((own, packed), F32),
+            jax.ShapeDtypeStruct((own, packed), BF16),
+        ),
+        in_specs=[SMEM] + [VMEM] * 7,
+        out_specs=(VMEM, VMEM, VMEM),
+        compiler_params=PARAMS,
+    )(counts, left, block, other, got[2], swapped[2], pair.reshape(own, -1), far_pair.reshape(own, -1))
     density, rho = pl.pallas_call(
-        functools.partial(sum_kernel, n_col, cells),
+        functools.partial(late_kernel, cells),
         out_shape=(
             jax.ShapeDtypeStruct((1, cells), F32),
             jax.ShapeDtypeStruct((atoms_own, NPROJ * NPROJ), F32),
         ),
-        in_specs=[VMEM] * (1 + len(blocks)),
+        in_specs=[VMEM] * 8,
         out_specs=(VMEM, VMEM),
         compiler_params=PARAMS,
-    )(left, *blocks)
+    )(left, got[3], swapped[3], got[1], swapped[1], *early)
     return density.reshape(cells), rho
 
 

time: 28.7 us -> 20.4 us (0.71)
  waiting for transfers between devices: 9.38 us -> 2.69 us
  local copies, waits for them, and re-layouts: 2.34 us -> 1.44 us
  other arithmetic: 0.81 us -> 0 us
  starting transfers between devices: 10.1 us -> 9.44 us
  Pallas kernels: 5.13 us -> 5.77 us
    ppermute x9, waiting for transfers between devices: 9.38 us -> 2.69 us  [move(): return lax.ppermute(block, axes, pairs)]
    another operation x3 -> x0, other arithmetic: 0.79 us -> none  [the longest x2 0.77 us: gather_shards(): jnp.stack([jnp.where(mine_first, proj_panel, half), jnp.where(mine_first,...]
    unnamed x16 -> x14, local copies, waits for them, and re-layouts: 2.21 us -> 1.42 us
    ppermute x9, starting transfers between devices: 10.1 us -> 9.44 us  [move(): return lax.ppermute(block, axes, pairs)]
    pallas_call x1, Pallas kernels: 0.77 us -> 1.26 us  [gather_shards(): pl.pallas_call(pack_kernel, out_shape=jax.ShapeDtypeStruct((packed, state...]
    pallas_call x1 -> x2, Pallas kernels: 2.98 us -> 3.29 us  [the longest x1 1.78 us: gather_shards(): pl.pallas_call(functools.partial(late_kernel, cells), out_shape=(jax.Shap...]
  transfers between devices with their start and end apart: 9 -> 9, of which waited for: 3 -> 3; matrix products, arithmetic and copies ran while one was open for 1% -> 1% of each run, Pallas kernels for 8% -> 14%
where the time goes in v2:
time: 20.4 us; the launch traced here: 20.1 us
  starting transfers between devices  9.44 us (46%)
  Pallas kernels  5.77 us (28%)
  waiting for transfers between devices  2.69 us (13%)
  local copies, waits for them, and re-layouts  1.44 us (7%)
  between operations  0.72 us (4%)
    ppermute x9, starting transfers between devices, move(): return lax.ppermute(block, axes, pairs)  9.44 us
    ppermute x9, waiting for transfers between devices, move(): return lax.ppermute(block, axes, pairs)  2.69 us
    pallas_call x1, Pallas kernels, gather_shards(): pl.pallas_call(functools.partial(late_kernel, cells), out_shape=(jax.Shap...  1.78 us
    pallas_call x1, Pallas kernels, gather_shards(): pl.pallas_call(functools.partial(early_kernel, cells, n_slab), out_shape=...  1.5 us
    unnamed x14, local copies, waits for them, and re-layouts  1.42 us
    pallas_call x1, Pallas kernels, gather_shards(): pl.pallas_call(pack_kernel, out_shape=jax.ShapeDtypeStruct((packed, state...  1.26 us
    pallas_call x1, Pallas kernels, gather_shards(): pl.pallas_call(functools.partial(left_kernel, n_col, n_slab), out_shape=j...  1.23 us
  transfers between devices with their start and end apart: 9, of which 3 were waited for; matrix products, arithmetic and copies ran while one was open for 1% of the time, Pallas kernels for 14%

profile of v2, /device:TPU:0, one launch (start us, length us, event | category | flops | bytes accessed | tf_op | source)
XLA Modules:
  0.0 20.1 jit_solution(7441699747857037333)
XLA Ops:
  0.7 1.3 %shard_map.95.a_ref = bf16[432,128]{1,0:T(8,128)(2,1)S(1)} custom-call(s32[128]{0:T(128)} %occ_ref.1, bf16[512,128]{1,0:T(8,128)(2,1)} %coeffs_ref.1), custom_call_target="tpu_custom_call" | custom-call | tf_op jit(solution)/shard_map/pallas_call | solution.py:289
  1.9 0.0 copy-start
  1.9 4.1 %collective-permute-start = (bf16[432,128]{1,0:T(8,128)(2,1)S(1)}, bf16[432,128]{1,0:T(8,128)(2,1)S(1)}, u32[]{:S(2)}, u32[]{:S(2)}) collective-permute-start(bf16[432,128]{1,0:T(8,128)(2,1)S(1)} %shard_map.95.a_ref), channel_id=1, source_target_pairs={{0,8},{1,25},{2,10},{3,27},{4,12},{5,29},{6,14},{7,31},{8,0},{9,17... | collective-permute-start | bytes 331784 | tf_op jit(solution)/shard_map/ppermute | solution.py:277
  6.0 1.3 %collective-permute-start.1 = (bf16[432,128]{1,0:T(8,128)(2,1)S(1)}, bf16[432,128]{1,0:T(8,128)(2,1)S(1)}, u32[]{:S(2)}, u32[]{:S(2)}) collective-permute-start(bf16[432,128]{1,0:T(8,128)(2,1)S(1)} %shard_map.95.a_ref), channel_id=1, source_target_pairs={{0,12},{1,29},{2,14},{3,31},{4,8},{5,25},{6,10},{7,27},{8,4},{9,21... | collective-permute-start | bytes 331784 | tf_op jit(solution)/shard_map/ppermute | solution.py:277
  7.4 0.2 %collective-permute-start.5 = (bf16[432,128]{1,0:T(8,128)(2,1)S(1)}, bf16[432,128]{1,0:T(8,128)(2,1)S(1)}, u32[]{:S(2)}, u32[]{:S(2)}) collective-permute-start(bf16[432,128]{1,0:T(8,128)(2,1)S(1)} %shard_map.95.a_ref), channel_id=1, source_target_pairs={{0,4},{1,21},{2,6},{3,23},{4,0},{5,17},{6,2},{7,19},{8,12},{9,29},... | collective-permute-start | bytes 331784 | tf_op jit(solution)/shard_map/ppermute | solution.py:277
  7.6 0.2 collective-permute-start.2
  7.8 1.0 %collective-permute-done.2 = bf16[8,16,128]{2,1,0:T(8,128)(2,1)S(1)} collective-permute-done((bf16[8,16,128]{2,1,0:T(8,128)(2,1)S(1)}, bf16[8,16,128]{2,1,0:T(8,128)(2,1)S(1)}, u32[]{:S(2)}, u32[]{:S(2)}) %collective-permute-start.2) | collective-permute-done | bytes 32800 | tf_op jit(solution)/shard_map/ppermute | solution.py:277
  8.8 1.6 %collective-permute-start.3 = (bf16[8,16,256]{2,1,0:T(8,128)(2,1)S(1)}, bf16[8,16,256]{2,1,0:T(8,128)(2,1)S(1)}, u32[]{:S(2)}, u32[]{:S(2)}) collective-permute-start(bf16[8,16,256]{2,1,0:T(8,128)(2,1)S(1)} %constant_dynamic-update-slice_fusion), channel_id=1, source_target_pairs={{0,2},{1,3},{2,0},{3,1},{4,6},{5,7},{6,4},{7,5},{8,10},{9,11},{10,... | collective-permute-start | bytes 196616 | tf_op jit(solution)/shard_map/ppermute | solution.py:277
  10.4 1.5 %collective-permute-start.7 = (bf16[432,128]{1,0:T(8,128)(2,1)S(1)}, bf16[432,128]{1,0:T(8,128)(2,1)S(1)}, u32[]{:S(2)}, u32[]{:S(2)}) collective-permute-start(bf16[432,128]{1,0:T(8,128)(2,1)S(1)} %shard_map.95.a_ref), channel_id=1, source_target_pairs={{0,16},{1,17},{2,18},{3,19},{4,20},{5,21},{6,22},{7,23},{8,24},{9,... | collective-permute-start | bytes 331784 | tf_op jit(solution)/shard_map/ppermute | solution.py:277
  11.9 0.7 %copy-done.5 = s32[32,8]{0,1:T(8,128)S(1)} copy-done((s32[32,8]{0,1:T(8,128)S(1)}, s32[32,8]{0,1:T(8,128)}, u32[]{:S(2)}) %copy-start.5) | copy-done | bytes 1048
  12.6 0.1 copy.11.lists_ref
  12.7 0.0 copy-done.1
  12.7 0.6 %copy-done.2 = s32[64]{0:T(128)S(1)} copy-done((s32[64]{0:T(128)S(1)}, s32[64]{0:T(128)}, u32[]{:S(2)}) %copy-start.2) | copy-done | bytes 280
  13.3 1.2 %shard_map.96.left_ref = bf16[2,384,432]{2,1,0:T(8,128)(2,1)S(1)} custom-call(s32[32,8]{1,0:T(8,128)S(1)} %copy.11.lists_ref, s32[64]{0:T(128)S(1)} %copy-done.2, bf16[128,128]{1,0:T(8,128)(2,1)S(1)} %copy-done.1, bf16[128,512]{1,0:T(8,128)(2,1)S(1)} %copy-done, bf16[128,16]{1,0:T(8,128)(2,1)S(1)} %bitcast.8), custom_call_target="tpu_custom_call" | custom-call | flops 200000000 | bytes 2000000 | tf_op jit(solution)/shard_map/pallas_call | solution.py:307
  14.6 0.1 collective-permute-done.c_ref
  14.7 0.0 collective-permute-start.8
  14.7 0.0 collective-permute-done.3
  14.7 0.0 collective-permute-done.1.a_ref
  14.7 0.5 %collective-permute-start.4 = (bf16[432,128]{1,0:T(8,128)(2,1)S(1)}, bf16[432,128]{1,0:T(8,128)(2,1)S(1)}, u32[]{:S(2)}, u32[]{:S(2)}) collective-permute-start(bf16[432,128]{1,0:T(8,128)(2,1)S(1)} %collective-permute-done.1.a_ref), channel_id=1, source_target_pairs={{0,1},{1,0},{2,3},{3,2},{4,5},{5,4},{6,7},{7,6},{8,9},{9,8},{10,11... | collective-permute-start | bytes 331784 | tf_op jit(solution)/shard_map/ppermute | solution.py:277
  15.2 1.6 %collective-permute-done.5.c_ref = bf16[432,128]{1,0:T(8,128)(2,1)S(1)} collective-permute-done((bf16[432,128]{1,0:T(8,128)(2,1)S(1)}, bf16[432,128]{1,0:T(8,128)(2,1)S(1)}, u32[]{:S(2)}, u32[]{:S(2)}) %collective-permute-start.5) | collective-permute-done | bytes 110624 | tf_op jit(solution)/shard_map/ppermute | solution.py:277
  16.8 1.5 %shard_map.97 = (f32[128,128]{1,0:T(8,128)S(1)}, f32[128,432]{1,0:T(8,128)S(1)}, bf16[128,432]{1,0:T(8,128)(2,1)S(1)}) custom-call(s32[64]{0:T(128)S(1)} %copy-done.2, bf16[2,384,432]{2,1,0:T(8,128)(2,1)S(1)} %shard_map.96.left_ref, bf16[432,128]{1,0:T(8,128)(2,1)S(1)} %shard_map.95.a_ref, bf16[432,128]{1,0:T(8,128)(2,1)S(1)} %collective-permute-done.7.b_ref, ...), custom_call_target="tpu_custom_call" | custom-call | tf_op jit(solution)/shard_map/pallas_call | solution.py:318
  18.3 0.0 collective-permute-done.4.b_ref
  18.3 0.0 collective-permute-done.6.d_ref
  18.3 1.8 %shard_map.98 = (f32[1,128]{1,0:T(1,128)}, f32[8,256]{1,0:T(8,128)}) custom-call(bf16[2,384,432]{2,1,0:T(8,128)(2,1)S(1)} %shard_map.96.left_ref, bf16[432,128]{1,0:T(8,128)(2,1)S(1)} %collective-permute-done.1.a_ref, bf16[432,128]{1,0:T(8,128)(2,1)S(1)} %collective-permute-done.4.b_ref, bf16[432,128]{1,0:T(8,128)(2,1)S(1)} %collective-permute-done.5.c_ref, ...), custom_call_target="tpu_custom_call" | custom-call | tf_op jit(solution)/shard_map/pallas_call | solution.py:329
  (14 shorter events, 0.1 us)
Async XLA Ops:
  0.6 7.0 %copy-start.3 = (bf16[8,16,128]{2,1,0:T(8,128)(2,1)S(1)}, bf16[8,16,128]{2,1,0:T(8,128)(2,1)}, u32[]{:S(2)}) copy-start(bf16[8,16,128]{2,1,0:T(8,128)(2,1)} %param.15) | copy-start | bytes 98308
  0.6 11.3 %copy-start.4 = (bf16[8,16,16]{2,1,0:T(8,128)(2,1)S(1)}, bf16[8,16,16]{2,1,0:T(8,128)(2,1)}, u32[]{:S(2)}) copy-start(bf16[8,16,16]{2,1,0:T(8,128)(2,1)} %param.14) | copy-start | bytes 12292
  1.9 10.8 %copy-start = (bf16[128,512]{1,0:T(8,128)(2,1)S(1)}, bf16[128,512]{1,0:T(8,128)(2,1)}, u32[]{:S(2)}) copy-start(bf16[128,512]{1,0:T(8,128)(2,1)} %panel_ref.1) | copy-start | bytes 393220
  1.9 12.7 %collective-permute-start = (bf16[432,128]{1,0:T(8,128)(2,1)S(1)}, bf16[432,128]{1,0:T(8,128)(2,1)S(1)}, u32[]{:S(2)}, u32[]{:S(2)}) collective-permute-start(bf16[432,128]{1,0:T(8,128)(2,1)S(1)} %shard_map.95.a_ref), channel_id=1, source_target_pairs={{0,8},{1,25},{2,10},{3,27},{4,12},{5,29},{6,14},{7,31},{8,0},{9,17... | collective-permute-start | bytes 331784 | tf_op jit(solution)/shard_map/ppermute | solution.py:277
  6.0 8.6 %collective-permute-start.1 = (bf16[432,128]{1,0:T(8,128)(2,1)S(1)}, bf16[432,128]{1,0:T(8,128)(2,1)S(1)}, u32[]{:S(2)}, u32[]{:S(2)}) collective-permute-start(bf16[432,128]{1,0:T(8,128)(2,1)S(1)} %shard_map.95.a_ref), channel_id=1, source_target_pairs={{0,12},{1,29},{2,14},{3,31},{4,8},{5,25},{6,10},{7,27},{8,4},{9,21... | collective-permute-start | bytes 331784 | tf_op jit(solution)/shard_map/ppermute | solution.py:277
  7.4 9.4 %collective-permute-start.5 = (bf16[432,128]{1,0:T(8,128)(2,1)S(1)}, bf16[432,128]{1,0:T(8,128)(2,1)S(1)}, u32[]{:S(2)}, u32[]{:S(2)}) collective-permute-start(bf16[432,128]{1,0:T(8,128)(2,1)S(1)} %shard_map.95.a_ref), channel_id=1, source_target_pairs={{0,4},{1,21},{2,6},{3,23},{4,0},{5,17},{6,2},{7,19},{8,12},{9,29},... | collective-permute-start | bytes 331784 | tf_op jit(solution)/shard_map/ppermute | solution.py:277
  7.6 1.2 %collective-permute-start.2 = (bf16[8,16,128]{2,1,0:T(8,128)(2,1)S(1)}, bf16[8,16,128]{2,1,0:T(8,128)(2,1)S(1)}, u32[]{:S(2)}, u32[]{:S(2)}) collective-permute-start(bf16[8,16,128]{2,1,0:T(8,128)(2,1)S(1)} %copy-done.3), channel_id=1, source_target_pairs={{0,1},{1,0},{2,3},{3,2},{4,5},{5,4},{6,7},{7,6},{8,9},{9,8},{10,11... | collective-permute-start | bytes 98312 | tf_op jit(solution)/shard_map/ppermute | solution.py:277
  8.8 5.8 %collective-permute-start.3 = (bf16[8,16,256]{2,1,0:T(8,128)(2,1)S(1)}, bf16[8,16,256]{2,1,0:T(8,128)(2,1)S(1)}, u32[]{:S(2)}, u32[]{:S(2)}) collective-permute-start(bf16[8,16,256]{2,1,0:T(8,128)(2,1)S(1)} %constant_dynamic-update-slice_fusion), channel_id=1, source_target_pairs={{0,2},{1,3},{2,0},{3,1},{4,6},{5,7},{6,4},{7,5},{8,10},{9,11},{10,... | collective-permute-start | bytes 196616 | tf_op jit(solution)/shard_map/ppermute | solution.py:277
  10.4 6.3 %collective-permute-start.7 = (bf16[432,128]{1,0:T(8,128)(2,1)S(1)}, bf16[432,128]{1,0:T(8,128)(2,1)S(1)}, u32[]{:S(2)}, u32[]{:S(2)}) collective-permute-start(bf16[432,128]{1,0:T(8,128)(2,1)S(1)} %shard_map.95.a_ref), channel_id=1, source_target_pairs={{0,16},{1,17},{2,18},{3,19},{4,20},{5,21},{6,22},{7,23},{8,24},{9,... | collective-permute-start | bytes 331784 | tf_op jit(solution)/shard_map/ppermute | solution.py:277
  11.9 0.7 %copy-start.5 = (s32[32,8]{0,1:T(8,128)S(1)}, s32[32,8]{0,1:T(8,128)}, u32[]{:S(2)}) copy-start(s32[32,8]{0,1:T(8,128)} %param.11) | copy-start | bytes 3076
  11.9 0.8 %copy-start.1 = (bf16[128,128]{1,0:T(8,128)(2,1)S(1)}, bf16[128,128]{1,0:T(8,128)(2,1)}, u32[]{:S(2)}) copy-start(bf16[128,128]{1,0:T(8,128)(2,1)} %phi_ref.1) | copy-start | bytes 98308
  12.7 0.7 %copy-start.2 = (s32[64]{0:T(128)S(1)}, s32[64]{0:T(128)}, u32[]{:S(2)}) copy-start(s32[64]{0:T(128)} %counts_ref.3) | copy-start | bytes 772
  14.7 2.1 %collective-permute-start.8 = (bf16[432,128]{1,0:T(8,128)(2,1)S(1)}, bf16[432,128]{1,0:T(8,128)(2,1)S(1)}, u32[]{:S(2)}, u32[]{:S(2)}) collective-permute-start(bf16[432,128]{1,0:T(8,128)(2,1)S(1)} %collective-permute-done.c_ref), channel_id=1, source_target_pairs={{0,1},{1,0},{2,3},{3,2},{4,5},{5,4},{6,7},{7,6},{8,9},{9,8},{10,11... | collective-permute-start | bytes 331784 | tf_op jit(solution)/shard_map/ppermute | solution.py:277
  14.7 3.6 %collective-permute-start.4 = (bf16[432,128]{1,0:T(8,128)(2,1)S(1)}, bf16[432,128]{1,0:T(8,128)(2,1)S(1)}, u32[]{:S(2)}, u32[]{:S(2)}) collective-permute-start(bf16[432,128]{1,0:T(8,128)(2,1)S(1)} %collective-permute-done.1.a_ref), channel_id=1, source_target_pairs={{0,1},{1,0},{2,3},{3,2},{4,5},{5,4},{6,7},{7,6},{8,9},{9,8},{10,11... | collective-permute-start | bytes 331784 | tf_op jit(solution)/shard_map/ppermute | solution.py:277
  16.7 1.5 %collective-permute-start.6 = (bf16[432,128]{1,0:T(8,128)(2,1)S(1)}, bf16[432,128]{1,0:T(8,128)(2,1)S(1)}, u32[]{:S(2)}, u32[]{:S(2)}) collective-permute-start(bf16[432,128]{1,0:T(8,128)(2,1)S(1)} %collective-permute-done.5.c_ref), channel_id=1, source_target_pairs={{0,1},{1,0},{2,3},{3,2},{4,5},{5,4},{6,7},{7,6},{8,9},{9,8},{10,11... | collective-permute-start | bytes 331784 | tf_op jit(solution)/shard_map/ppermute | solution.py:277

commit v3 on v2

--- a/solution.py
+++ b/solution.py
@@ -199,55 +199,49 @@
     return high, (values - high.astype(F32)).astype(BF16)
 
 
-ROWS_BY_ROWS = (((1,), (1,)), ((), ()))
-
-
-def partial_sums(a, b, near, cells, left_ref):
+def partial_sums(a, b, near, cells, left_ref, proj_ref):
     weight_row = left_ref.shape[2] - 16
     r = jnp.dot(left_ref[near], a, preferred_element_type=F32)
     r += jnp.dot(left_ref[1 - near], b, preferred_element_type=F32)
+    right = jnp.dot(proj_ref[...], jnp.where(near == 0, a, b), preferred_element_type=F32)
     f = a[weight_row:, :].astype(F32)[0:1]
     term = r[:cells] * f * r[cells : 2 * cells]
-    half = term.shape[1] // 2
-    panel = jnp.where(near == 0, a, b)
-    projected = sum(
-        lax.dot_general(part, panel, ROWS_BY_ROWS, preferred_element_type=F32)
-        for part in split(r[2 * cells :] * f)
-    )
-    return term[:, :half] + term[:, half:], projected
-
-
-def early_kernel(
-    cells, n_slab, counts_ref, left_ref, a_ref, b_ref, c_ref, d_ref, here_ref, far_ref, term_ref, projected_ref, proj_ref
-):
+    term = sum(term[:, at : at + cells] for at in range(0, term.shape[1], cells))
+    high, low = split(r[2 * cells :] * f)
+    right_high, right_low = split(right)
+    rho = sum(
+        lax.dot_general(one, two, (((1,), (1,)), ((), ())), preferred_element_type=F32)
+        for one, two in ((high, right_high), (low, right_high), (high, right_low))
+    )
+    return term, rho
+
+
+def proj_kernel(n_slab, counts_ref, here_ref, far_ref, out_ref):
+    s = lax.axis_index("dz")
+    atoms = PW // SLOTS // n_slab
+    columns = panel_map(counts_ref, out_ref.shape[1], lambda t: (s ^ (t // atoms)) * atoms + t % atoms)
+    out_ref[...] = take(jnp.concatenate([here_ref[...], far_ref[...]], axis=1), columns)
+
+
+def early_kernel(cells, left_ref, proj_ref, a_ref, b_ref, c_ref, d_ref, term_ref, rho_ref):
     x, s = lax.axis_index("prow"), lax.axis_index("dz")
     odd = (s & 1) == 1
-    a = jnp.concatenate([a_ref[...], jnp.where(odd, d_ref[...], c_ref[...])], axis=1)
-    b = jnp.concatenate([b_ref[...], jnp.where(odd, c_ref[...], d_ref[...])], axis=1)
-    term_ref[...], projected_ref[...] = partial_sums(a, b, x, cells, left_ref)
-    atoms = PW // SLOTS // n_slab
-    columns = panel_map(
-        counts_ref, projected_ref.shape[1], lambda t: (s ^ (t // atoms)) * atoms + t % atoms
-    )
-    proj_ref[...] = take(jnp.concatenate([here_ref[...], far_ref[...]], axis=1), columns)
-
-
-def late_kernel(
-    cells, left_ref, a_ref, b_ref, c_ref, d_ref, term_ref, projected_ref, proj_ref, density_ref, rho_ref
-):
+    c, d = c_ref[...], d_ref[...]
+    a = jnp.concatenate([a_ref[...], jnp.where(odd, d, c)], axis=1)
+    b = jnp.concatenate([b_ref[...], jnp.where(odd, c, d)], axis=1)
+    term_ref[...], rho_ref[...] = partial_sums(a, b, x, cells, left_ref, proj_ref)
+
+
+def late_kernel(cells, left_ref, proj_ref, a_ref, b_ref, c_ref, d_ref, term_ref, part_ref, density_ref, rho_ref):
     near = lax.axis_index("prow") ^ (lax.axis_index("dz") & 1)
     a = jnp.concatenate([a_ref[...], c_ref[...]], axis=1)
     b = jnp.concatenate([b_ref[...], d_ref[...]], axis=1)
-    term, projected = partial_sums(a, b, near, cells, left_ref)
+    term, rho = partial_sums(a, b, near, cells, left_ref, proj_ref)
     term += term_ref[...]
-    projected += projected_ref[...]
+    rho += part_ref[...]
     density_ref[...] = jnp.sum(term.T, axis=0, keepdims=True)
     own = proj_ref.shape[0]
     atoms = own // NPROJ
-    rho = sum(
-        lax.dot_general(part, proj_ref[...], ROWS_BY_ROWS, preferred_element_type=F32)
-        for part in split(projected)
-    )
     rho = jnp.where((iota((own, own), 0) & (atoms - 1)) == (iota((own, own), 1) >> 4), rho, 0.0)
     wide = NPROJ * NPROJ
     fold = pick((iota((own, wide), 0) & (NPROJ - 1)) == (iota((own, wide), 1) & (NPROJ - 1)))
@@ -312,20 +306,24 @@
         compiler_params=PARAMS,
         cost_estimate=pl.CostEstimate(flops=2 * 10**8, bytes_accessed=2 * 10**6, transcendentals=0),
     )(intersection, counts, phi_values, panel_values, site)
-    got[2], left = lax.optimization_barrier((got[2], left))
-    got[3], far_pair = lax.optimization_barrier((got[3], far_pair))
-    swapped = {k: swap(got[k]) for k in got}
+    proj = pl.pallas_call(
+        functools.partial(proj_kernel, n_slab),
+        out_shape=jax.ShapeDtypeStruct((own, packed), BF16),
+        in_specs=[SMEM, VMEM, VMEM],
+        out_specs=VMEM,
+        compiler_params=PARAMS,
+    )(counts, pair.reshape(own, -1), far_pair.reshape(own, -1))
+    got[3], left = lax.optimization_barrier((got[3], left))
+    swapped = {3: swap(got[3])}
+    got[2], proj = lax.optimization_barrier((got[2], proj))
     early = pl.pallas_call(
-        functools.partial(early_kernel, cells, n_slab),
-        out_shape=(
-            jax.ShapeDtypeStruct((cells, states), F32),
-            jax.ShapeDtypeStruct((own, packed), F32),
-            jax.ShapeDtypeStruct((own, packed), BF16),
-        ),
-        in_specs=[SMEM] + [VMEM] * 7,
-        out_specs=(VMEM, VMEM, VMEM),
-        compiler_params=PARAMS,
-    )(counts, left, block, other, got[2], swapped[2], pair.reshape(own, -1), far_pair.reshape(own, -1))
+        functools.partial(early_kernel, cells),
+        out_shape=(jax.ShapeDtypeStruct((cells, states), F32), jax.ShapeDtypeStruct((own, own), F32)),
+        in_specs=[VMEM] * 6,
+        out_specs=(VMEM, VMEM),
+        compiler_params=PARAMS,
+    )(left, proj, block, other, got[3], swapped[3])
+    swapped |= {k: swap(got[k]) for k in (2, 1)}
     density, rho = pl.pallas_call(
         functools.partial(late_kernel, cells),
         out_shape=(
@@ -335,7 +333,7 @@
         in_specs=[VMEM] * 8,
         out_specs=(VMEM, VMEM),
         compiler_params=PARAMS,
-    )(left, got[3], swapped[3], got[1], swapped[1], *early)
+    )(left, proj, got[2], swapped[2], got[1], swapped[1], *early)
     return density.reshape(cells), rho
 
 

time: 20.4 us -> 19.8 us (0.971)
  Pallas kernels: 5.77 us -> 5.38 us
  waiting for transfers between devices: 2.69 us -> 2.45 us
    pallas_call x1, Pallas kernels: 1.78 us -> 1.45 us  [gather_shards(): pl.pallas_call(functools.partial(late_kernel, cells), out_shape=(jax.Shap...]
    ppermute x9, waiting for transfers between devices: 2.69 us -> 2.45 us  [move(): return lax.ppermute(block, axes, pairs)]
    pallas_call x1 -> x2, Pallas kernels: 1.5 us -> 1.45 us  [the longest x1 0.79 us: gather_shards(): pl.pallas_call(functools.partial(proj_kernel, n_slab), out_shape=jax.Shap...]
where the time goes in v3:
time: 19.8 us; the launch traced here: 19.5 us
  starting transfers between devices  9.5 us (48%)
  Pallas kernels  5.38 us (27%)
  waiting for transfers between devices  2.45 us (12%)
  local copies, waits for them, and re-layouts  1.44 us (7%)
  between operations  0.74 us (4%)
    ppermute x9, starting transfers between devices, move(): return lax.ppermute(block, axes, pairs)  9.5 us
    ppermute x9, waiting for transfers between devices, move(): return lax.ppermute(block, axes, pairs)  2.45 us
    pallas_call x1, Pallas kernels, gather_shards(): pl.pallas_call(functools.partial(late_kernel, cells), out_shape=(jax.Shap...  1.45 us
    unnamed x14, local copies, waits for them, and re-layouts  1.42 us
    pallas_call x1, Pallas kernels, gather_shards(): pl.pallas_call(pack_kernel, out_shape=jax.ShapeDtypeStruct((packed, state...  1.26 us
    pallas_call x1, Pallas kernels, gather_shards(): pl.pallas_call(functools.partial(left_kernel, n_col, n_slab), out_shape=j...  1.23 us
    pallas_call x1, Pallas kernels, gather_shards(): pl.pallas_call(functools.partial(proj_kernel, n_slab), out_shape=jax.Shap...  0.79 us
    pallas_call x1, Pallas kernels, gather_shards(): pl.pallas_call(functools.partial(early_kernel, cells), out_shape=(jax.Sha...  0.65 us
  transfers between devices with their start and end apart: 9, of which 3 were waited for; matrix products, arithmetic and copies ran while one was open for 1% of the time, Pallas kernels for 14%

profile of v3, /device:TPU:0, one launch (start us, length us, event | category | flops | bytes accessed | tf_op | source)
XLA Modules:
  0.0 19.5 jit_solution(5169828101097510132)
XLA Ops:
  0.7 1.3 %shard_map.95.a_ref = bf16[432,128]{1,0:T(8,128)(2,1)S(1)} custom-call(s32[128]{0:T(128)} %occ_ref.1, bf16[512,128]{1,0:T(8,128)(2,1)} %coeffs_ref.1), custom_call_target="tpu_custom_call" | custom-call | tf_op jit(solution)/shard_map/pallas_call | solution.py:283
  1.9 0.0 copy-start
  1.9 4.1 %collective-permute-start.1 = (bf16[432,128]{1,0:T(8,128)(2,1)S(1)}, bf16[432,128]{1,0:T(8,128)(2,1)S(1)}, u32[]{:S(2)}, u32[]{:S(2)}) collective-permute-start(bf16[432,128]{1,0:T(8,128)(2,1)S(1)} %shard_map.95.a_ref), channel_id=1, source_target_pairs={{0,8},{1,25},{2,10},{3,27},{4,12},{5,29},{6,14},{7,31},{8,0},{9,17... | collective-permute-start | bytes 331784 | tf_op jit(solution)/shard_map/ppermute | solution.py:271
  6.0 1.3 %collective-permute-start = (bf16[432,128]{1,0:T(8,128)(2,1)S(1)}, bf16[432,128]{1,0:T(8,128)(2,1)S(1)}, u32[]{:S(2)}, u32[]{:S(2)}) collective-permute-start(bf16[432,128]{1,0:T(8,128)(2,1)S(1)} %shard_map.95.a_ref), channel_id=1, source_target_pairs={{0,12},{1,29},{2,14},{3,31},{4,8},{5,25},{6,10},{7,27},{8,4},{9,21... | collective-permute-start | bytes 331784 | tf_op jit(solution)/shard_map/ppermute | solution.py:271
  7.4 0.2 %collective-permute-start.5 = (bf16[432,128]{1,0:T(8,128)(2,1)S(1)}, bf16[432,128]{1,0:T(8,128)(2,1)S(1)}, u32[]{:S(2)}, u32[]{:S(2)}) collective-permute-start(bf16[432,128]{1,0:T(8,128)(2,1)S(1)} %shard_map.95.a_ref), channel_id=1, source_target_pairs={{0,4},{1,21},{2,6},{3,23},{4,0},{5,17},{6,2},{7,19},{8,12},{9,29},... | collective-permute-start | bytes 331784 | tf_op jit(solution)/shard_map/ppermute | solution.py:271
  7.6 0.2 collective-permute-start.2
  7.8 1.0 %collective-permute-done.2 = bf16[8,16,128]{2,1,0:T(8,128)(2,1)S(1)} collective-permute-done((bf16[8,16,128]{2,1,0:T(8,128)(2,1)S(1)}, bf16[8,16,128]{2,1,0:T(8,128)(2,1)S(1)}, u32[]{:S(2)}, u32[]{:S(2)}) %collective-permute-start.2) | collective-permute-done | bytes 32800 | tf_op jit(solution)/shard_map/ppermute | solution.py:271
  8.8 1.6 %collective-permute-start.3 = (bf16[8,16,256]{2,1,0:T(8,128)(2,1)S(1)}, bf16[8,16,256]{2,1,0:T(8,128)(2,1)S(1)}, u32[]{:S(2)}, u32[]{:S(2)}) collective-permute-start(bf16[8,16,256]{2,1,0:T(8,128)(2,1)S(1)} %constant_dynamic-update-slice_fusion), channel_id=1, source_target_pairs={{0,2},{1,3},{2,0},{3,1},{4,6},{5,7},{6,4},{7,5},{8,10},{9,11},{10,... | collective-permute-start | bytes 196616 | tf_op jit(solution)/shard_map/ppermute | solution.py:271
  10.4 1.5 %collective-permute-start.7 = (bf16[432,128]{1,0:T(8,128)(2,1)S(1)}, bf16[432,128]{1,0:T(8,128)(2,1)S(1)}, u32[]{:S(2)}, u32[]{:S(2)}) collective-permute-start(bf16[432,128]{1,0:T(8,128)(2,1)S(1)} %shard_map.95.a_ref), channel_id=1, source_target_pairs={{0,16},{1,17},{2,18},{3,19},{4,20},{5,21},{6,22},{7,23},{8,24},{9,... | collective-permute-start | bytes 331784 | tf_op jit(solution)/shard_map/ppermute | solution.py:271
  11.9 0.7 %copy-done.5 = s32[32,8]{0,1:T(8,128)S(1)} copy-done((s32[32,8]{0,1:T(8,128)S(1)}, s32[32,8]{0,1:T(8,128)}, u32[]{:S(2)}) %copy-start.5) | copy-done | bytes 1048
  12.6 0.1 copy.11.lists_ref
  12.7 0.0 copy-done.1
  12.7 0.6 %copy-done.2 = s32[64]{0:T(128)S(1)} copy-done((s32[64]{0:T(128)S(1)}, s32[64]{0:T(128)}, u32[]{:S(2)}) %copy-start.2) | copy-done | bytes 280
  13.3 1.2 %shard_map.96.left_ref = bf16[2,384,432]{2,1,0:T(8,128)(2,1)S(1)} custom-call(s32[32,8]{1,0:T(8,128)S(1)} %copy.11.lists_ref, s32[64]{0:T(128)S(1)} %copy-done.2, bf16[128,128]{1,0:T(8,128)(2,1)S(1)} %copy-done.1, bf16[128,512]{1,0:T(8,128)(2,1)S(1)} %copy-done, bf16[128,16]{1,0:T(8,128)(2,1)S(1)} %bitcast.8), custom_call_target="tpu_custom_call" | custom-call | flops 200000000 | bytes 2000000 | tf_op jit(solution)/shard_map/pallas_call | solution.py:301
  14.6 0.0 collective-permute-done.3
  14.6 0.8 %shard_map.97.proj_ref = bf16[128,432]{1,0:T(8,128)(2,1)S(1)} custom-call(s32[64]{0:T(128)S(1)} %copy-done.2, bf16[128,256]{1,0:T(8,128)(2,1)S(1)} %bitcast.7, bf16[128,256]{1,0:T(8,128)(2,1)S(1)} %bitcast.9), custom_call_target="tpu_custom_call" | custom-call | tf_op jit(solution)/shard_map/pallas_call | solution.py:309
  15.4 0.1 collective-permute-start.8
  15.5 0.0 collective-permute-done.1.a_ref
  15.5 0.5 %collective-permute-start.4 = (bf16[432,128]{1,0:T(8,128)(2,1)S(1)}, bf16[432,128]{1,0:T(8,128)(2,1)S(1)}, u32[]{:S(2)}, u32[]{:S(2)}) collective-permute-start(bf16[432,128]{1,0:T(8,128)(2,1)S(1)} %collective-permute-done.1.a_ref), channel_id=1, source_target_pairs={{0,1},{1,0},{2,3},{3,2},{4,5},{5,4},{6,7},{7,6},{8,9},{9,8},{10,11... | collective-permute-start | bytes 331784 | tf_op jit(solution)/shard_map/ppermute | solution.py:271
  16.0 0.8 %collective-permute-done.5.c_ref = bf16[432,128]{1,0:T(8,128)(2,1)S(1)} collective-permute-done((bf16[432,128]{1,0:T(8,128)(2,1)S(1)}, bf16[432,128]{1,0:T(8,128)(2,1)S(1)}, u32[]{:S(2)}, u32[]{:S(2)}) %collective-permute-start.5) | collective-permute-done | bytes 110624 | tf_op jit(solution)/shard_map/ppermute | solution.py:271
  16.7 0.0 collective-permute-done.8.d_ref
  16.8 0.7 %shard_map.98 = (f32[128,128]{1,0:T(8,128)S(1)}, f32[128,128]{1,0:T(8,128)S(1)}) custom-call(bf16[2,384,432]{2,1,0:T(8,128)(2,1)S(1)} %shard_map.96.left_ref, bf16[128,432]{1,0:T(8,128)(2,1)S(1)} %shard_map.97.proj_ref, bf16[432,128]{1,0:T(8,128)(2,1)S(1)} %shard_map.95.a_ref, bf16[432,128]{1,0:T(8,128)(2,1)S(1)} %collective-permute-done.7.b_ref, ...), custom_call_target="tpu_custom_call" | custom-call | tf_op jit(solution)/shard_map/pallas_call | solution.py:319
  17.4 0.6 %collective-permute-done.6.d_ref = bf16[432,128]{1,0:T(8,128)(2,1)S(1)} collective-permute-done((bf16[432,128]{1,0:T(8,128)(2,1)S(1)}, bf16[432,128]{1,0:T(8,128)(2,1)S(1)}, u32[]{:S(2)}, u32[]{:S(2)}) %collective-permute-start.6) | collective-permute-done | bytes 110624 | tf_op jit(solution)/shard_map/ppermute | solution.py:271
  18.1 1.4 %shard_map.99 = (f32[1,128]{1,0:T(1,128)}, f32[8,256]{1,0:T(8,128)}) custom-call(bf16[2,384,432]{2,1,0:T(8,128)(2,1)S(1)} %shard_map.96.left_ref, bf16[128,432]{1,0:T(8,128)(2,1)S(1)} %shard_map.97.proj_ref, bf16[432,128]{1,0:T(8,128)(2,1)S(1)} %collective-permute-done.1.a_ref, bf16[432,128]{1,0:T(8,128)(2,1)S(1)} %collective-permute-done.4.b_ref, ...), custom_call_target="tpu_custom_call" | custom-call | tf_op jit(solution)/shard_map/pallas_call | solution.py:327
  (15 shorter events, 0.1 us)
Async XLA Ops:
  0.6 7.0 %copy-start.3 = (bf16[8,16,128]{2,1,0:T(8,128)(2,1)S(1)}, bf16[8,16,128]{2,1,0:T(8,128)(2,1)}, u32[]{:S(2)}) copy-start(bf16[8,16,128]{2,1,0:T(8,128)(2,1)} %param.15) | copy-start | bytes 98308
  0.6 11.3 %copy-start.4 = (bf16[8,16,16]{2,1,0:T(8,128)(2,1)S(1)}, bf16[8,16,16]{2,1,0:T(8,128)(2,1)}, u32[]{:S(2)}) copy-start(bf16[8,16,16]{2,1,0:T(8,128)(2,1)} %param.14) | copy-start | bytes 12292
  1.9 10.8 %copy-start = (bf16[128,512]{1,0:T(8,128)(2,1)S(1)}, bf16[128,512]{1,0:T(8,128)(2,1)}, u32[]{:S(2)}) copy-start(bf16[128,512]{1,0:T(8,128)(2,1)} %panel_ref.1) | copy-start | bytes 393220
  1.9 13.5 %collective-permute-start.1 = (bf16[432,128]{1,0:T(8,128)(2,1)S(1)}, bf16[432,128]{1,0:T(8,128)(2,1)S(1)}, u32[]{:S(2)}, u32[]{:S(2)}) collective-permute-start(bf16[432,128]{1,0:T(8,128)(2,1)S(1)} %shard_map.95.a_ref), channel_id=1, source_target_pairs={{0,8},{1,25},{2,10},{3,27},{4,12},{5,29},{6,14},{7,31},{8,0},{9,17... | collective-permute-start | bytes 331784 | tf_op jit(solution)/shard_map/ppermute | solution.py:271
  6.0 9.4 %collective-permute-start = (bf16[432,128]{1,0:T(8,128)(2,1)S(1)}, bf16[432,128]{1,0:T(8,128)(2,1)S(1)}, u32[]{:S(2)}, u32[]{:S(2)}) collective-permute-start(bf16[432,128]{1,0:T(8,128)(2,1)S(1)} %shard_map.95.a_ref), channel_id=1, source_target_pairs={{0,12},{1,29},{2,14},{3,31},{4,8},{5,25},{6,10},{7,27},{8,4},{9,21... | collective-permute-start | bytes 331784 | tf_op jit(solution)/shard_map/ppermute | solution.py:271
  7.4 9.4 %collective-permute-start.5 = (bf16[432,128]{1,0:T(8,128)(2,1)S(1)}, bf16[432,128]{1,0:T(8,128)(2,1)S(1)}, u32[]{:S(2)}, u32[]{:S(2)}) collective-permute-start(bf16[432,128]{1,0:T(8,128)(2,1)S(1)} %shard_map.95.a_ref), channel_id=1, source_target_pairs={{0,4},{1,21},{2,6},{3,23},{4,0},{5,17},{6,2},{7,19},{8,12},{9,29},... | collective-permute-start | bytes 331784 | tf_op jit(solution)/shard_map/ppermute | solution.py:271
  7.6 1.2 %collective-permute-start.2 = (bf16[8,16,128]{2,1,0:T(8,128)(2,1)S(1)}, bf16[8,16,128]{2,1,0:T(8,128)(2,1)S(1)}, u32[]{:S(2)}, u32[]{:S(2)}) collective-permute-start(bf16[8,16,128]{2,1,0:T(8,128)(2,1)S(1)} %copy-done.3), channel_id=1, source_target_pairs={{0,1},{1,0},{2,3},{3,2},{4,5},{5,4},{6,7},{7,6},{8,9},{9,8},{10,11... | collective-permute-start | bytes 98312 | tf_op jit(solution)/shard_map/ppermute | solution.py:271
  8.8 5.7 %collective-permute-start.3 = (bf16[8,16,256]{2,1,0:T(8,128)(2,1)S(1)}, bf16[8,16,256]{2,1,0:T(8,128)(2,1)S(1)}, u32[]{:S(2)}, u32[]{:S(2)}) collective-permute-start(bf16[8,16,256]{2,1,0:T(8,128)(2,1)S(1)} %constant_dynamic-update-slice_fusion), channel_id=1, source_target_pairs={{0,2},{1,3},{2,0},{3,1},{4,6},{5,7},{6,4},{7,5},{8,10},{9,11},{10,... | collective-permute-start | bytes 196616 | tf_op jit(solution)/shard_map/ppermute | solution.py:271
  10.4 6.3 %collective-permute-start.7 = (bf16[432,128]{1,0:T(8,128)(2,1)S(1)}, bf16[432,128]{1,0:T(8,128)(2,1)S(1)}, u32[]{:S(2)}, u32[]{:S(2)}) collective-permute-start(bf16[432,128]{1,0:T(8,128)(2,1)S(1)} %shard_map.95.a_ref), channel_id=1, source_target_pairs={{0,16},{1,17},{2,18},{3,19},{4,20},{5,21},{6,22},{7,23},{8,24},{9,... | collective-permute-start | bytes 331784 | tf_op jit(solution)/shard_map/ppermute | solution.py:271
  11.9 0.7 %copy-start.5 = (s32[32,8]{0,1:T(8,128)S(1)}, s32[32,8]{0,1:T(8,128)}, u32[]{:S(2)}) copy-start(s32[32,8]{0,1:T(8,128)} %param.11) | copy-start | bytes 3076
  11.9 0.8 %copy-start.1 = (bf16[128,128]{1,0:T(8,128)(2,1)S(1)}, bf16[128,128]{1,0:T(8,128)(2,1)}, u32[]{:S(2)}) copy-start(bf16[128,128]{1,0:T(8,128)(2,1)} %phi_ref.1) | copy-start | bytes 98308
  12.7 0.7 %copy-start.2 = (s32[64]{0:T(128)S(1)}, s32[64]{0:T(128)}, u32[]{:S(2)}) copy-start(s32[64]{0:T(128)} %counts_ref.3) | copy-start | bytes 772
  15.4 1.4 %collective-permute-start.8 = (bf16[432,128]{1,0:T(8,128)(2,1)S(1)}, bf16[432,128]{1,0:T(8,128)(2,1)S(1)}, u32[]{:S(2)}, u32[]{:S(2)}) collective-permute-start(bf16[432,128]{1,0:T(8,128)(2,1)S(1)} %collective-permute-done.c_ref), channel_id=1, source_target_pairs={{0,1},{1,0},{2,3},{3,2},{4,5},{5,4},{6,7},{7,6},{8,9},{9,8},{10,11... | collective-permute-start | bytes 331784 | tf_op jit(solution)/shard_map/ppermute | solution.py:271
  15.5 2.0 %collective-permute-start.4 = (bf16[432,128]{1,0:T(8,128)(2,1)S(1)}, bf16[432,128]{1,0:T(8,128)(2,1)S(1)}, u32[]{:S(2)}, u32[]{:S(2)}) collective-permute-start(bf16[432,128]{1,0:T(8,128)(2,1)S(1)} %collective-permute-done.1.a_ref), channel_id=1, source_target_pairs={{0,1},{1,0},{2,3},{3,2},{4,5},{5,4},{6,7},{7,6},{8,9},{9,8},{10,11... | collective-permute-start | bytes 331784 | tf_op jit(solution)/shard_map/ppermute | solution.py:271
  16.7 1.3 %collective-permute-start.6 = (bf16[432,128]{1,0:T(8,128)(2,1)S(1)}, bf16[432,128]{1,0:T(8,128)(2,1)S(1)}, u32[]{:S(2)}, u32[]{:S(2)}) collective-permute-start(bf16[432,128]{1,0:T(8,128)(2,1)S(1)} %collective-permute-done.5.c_ref), channel_id=1, source_target_pairs={{0,1},{1,0},{2,3},{3,2},{4,5},{5,4},{6,7},{7,6},{8,9},{9,8},{10,11... | collective-permute-start | bytes 331784 | tf_op jit(solution)/shard_map/ppermute | solution.py:271

commit v4 on v3

--- a/solution.py
+++ b/solution.py
@@ -141,21 +141,38 @@
     out_ref[rows // SLOTS * LIVE :, :] = jnp.broadcast_to(weights, (16, weights.shape[1])).astype(BF16)
 
 
-def panel_map(counts_ref, packed, first=lambda t: t):
+def panel_map(counts_ref, packed):
     slot = iota((SLOTS, packed), 0)
     new = iota((SLOTS, packed), 1)
     return jnp.concatenate(
-        [
-            pick((new == first(t) * LIVE + slot) & (slot < counts_ref[first(t)]))
-            for t in range(PW // SLOTS)
-        ],
-        axis=0,
-    )
-
-
-def left_kernel(n_col, n_slab, lists_ref, counts_ref, phi_ref, panel_ref, site_ref, out_ref):
+        [pick((new == t * LIVE + slot) & (slot < counts_ref[t])) for t in range(PW // SLOTS)], axis=0
+    )
+
+
+def left_kernel(
+    n_col,
+    n_slab,
+    lists_hbm,
+    counts_hbm,
+    phi_ref,
+    panel_ref,
+    site_ref,
+    out_ref,
+    columns_ref,
+    lists_ref,
+    counts_ref,
+    arrived,
+):
+    copies = [
+        pltpu.make_async_copy(source, target, arrived.at[i])
+        for i, (source, target) in enumerate(((lists_hbm, lists_ref), (counts_hbm, counts_ref)))
+    ]
+    for copy in copies:
+        copy.start()
+    for copy in copies:
+        copy.wait()
     x, z, s = lax.axis_index("prow"), lax.axis_index("pcol"), lax.axis_index("dz")
-    cells, listed = phi_ref.shape[0], lists_ref.shape[1]
+    cells, listed = phi_ref.shape[0], lists_ref.shape[0]
     packed = out_ref.shape[2]
     own = site_ref.shape[0]
     atoms_own = own // NPROJ
@@ -180,8 +197,8 @@
         to_listed = jnp.concatenate(
             [
                 pick(
-                    (new == (lists_ref[domain, p] - b * blk_atoms) * LIVE + slot)
-                    & (slot < counts_ref[lists_ref[domain, p]])
+                    (new == (lists_ref[p, domain] - b * blk_atoms) * LIVE + slot)
+                    & (slot < counts_ref[lists_ref[p, domain]])
                     & (new < blk_atoms * LIVE)
                 )
                 for p in range(listed)
@@ -190,7 +207,9 @@
         )
         out_ref[b, 0:cells, :] = take(phi_ref[...], to_listed)
         out_ref[b, 2 * cells : 2 * cells + own, :] = jnp.where(x == b, site_side, jnp.zeros_like(site_side))
-    out_ref[0, cells : 2 * cells, :] = take(panel_ref[...], panel_map(counts_ref, packed))
+    columns = panel_map(counts_ref, packed)
+    columns_ref[...] = columns
+    out_ref[0, cells : 2 * cells, :] = take(panel_ref[...], columns)
     out_ref[1, cells : 2 * cells, :] = jnp.zeros((cells, packed), BF16)
 
 
@@ -216,16 +235,19 @@
     return term, rho
 
 
-def proj_kernel(n_slab, counts_ref, here_ref, far_ref, out_ref):
-    s = lax.axis_index("dz")
-    atoms = PW // SLOTS // n_slab
-    columns = panel_map(counts_ref, out_ref.shape[1], lambda t: (s ^ (t // atoms)) * atoms + t % atoms)
-    out_ref[...] = take(jnp.concatenate([here_ref[...], far_ref[...]], axis=1), columns)
-
-
-def early_kernel(cells, left_ref, proj_ref, a_ref, b_ref, c_ref, d_ref, term_ref, rho_ref):
+def early_kernel(
+    cells, left_ref, columns_ref, here_ref, next_ref, a_ref, b_ref, c_ref, d_ref, term_ref, rho_ref, proj_ref
+):
     x, s = lax.axis_index("prow"), lax.axis_index("dz")
-    odd = (s & 1) == 1
+    odd, back = (s & 1) == 1, (s & 2) == 2
+    here, after = here_ref[...], next_ref[...]
+    evens, odds = jnp.where(odd, after, here), jnp.where(odd, here, after)
+    half = here.shape[1] // 2
+    low = [evens[:, :half], odds[:, :half]]
+    high = [evens[:, half:], odds[:, half:]]
+    front = [jnp.where(back, h, l) for l, h in zip(low, high)]
+    rear = [jnp.where(back, l, h) for l, h in zip(low, high)]
+    proj_ref[...] = take(jnp.concatenate(front + rear, axis=1), columns_ref[...])
     c, d = c_ref[...], d_ref[...]
     a = jnp.concatenate([a_ref[...], jnp.where(odd, d, c)], axis=1)
     b = jnp.concatenate([b_ref[...], jnp.where(odd, c, d)], axis=1)
@@ -278,8 +300,7 @@
     atoms_own = proj_site.shape[0]
     own = atoms_own * NPROJ
     cells = phi_values.shape[0]
-    pair = jnp.concatenate([proj_panel, swap(proj_panel)], axis=2)
-    far_pair = move(pair, lambda x, z, s: (x, z, s ^ 2))
+    far = move(proj_panel, lambda x, z, s: (x, z, s ^ 2))
     block = pl.pallas_call(
         pack_kernel,
         out_shape=jax.ShapeDtypeStruct((packed, states), BF16),
@@ -295,35 +316,49 @@
         pltpu.with_memory_space_constraint(occupations, pltpu.HBM),
         pltpu.with_memory_space_constraint(coeffs, pltpu.HBM),
     )
-    got = {k: move(block, lambda x, z, s: (x ^ (s & 1), z ^ k, s)) for k in (2, 3, 1)}
+    got = {k: move(block, lambda x, z, s: (x ^ (s & 1), z ^ k, s)) for k in (1, 2, 3)}
     other = move(block, lambda x, z, s: (x ^ 1, z, s))
     site = proj_site.transpose(1, 0, 2).reshape(own, SLOTS)
-    left = pl.pallas_call(
+    left, columns = pl.pallas_call(
         functools.partial(left_kernel, n_col, n_slab),
-        out_shape=jax.ShapeDtypeStruct((2, 2 * cells + own, packed), BF16),
-        in_specs=[SMEM, SMEM, VMEM, VMEM, VMEM],
-        out_specs=VMEM,
+        out_shape=(
+            jax.ShapeDtypeStruct((2, 2 * cells + own, packed), BF16),
+            jax.ShapeDtypeStruct((PW, packed), BF16),
+        ),
+        in_specs=[HBM, HBM, VMEM, VMEM, VMEM],
+        out_specs=(VMEM, VMEM),
+        scratch_shapes=[
+            pltpu.SMEM(intersection.shape[::-1], jnp.int32),
+            pltpu.SMEM(counts.shape, jnp.int32),
+            pltpu.SemaphoreType.DMA((2,)),
+        ],
         compiler_params=PARAMS,
         cost_estimate=pl.CostEstimate(flops=2 * 10**8, bytes_accessed=2 * 10**6, transcendentals=0),
-    )(intersection, counts, phi_values, panel_values, site)
-    proj = pl.pallas_call(
-        functools.partial(proj_kernel, n_slab),
-        out_shape=jax.ShapeDtypeStruct((own, packed), BF16),
-        in_specs=[SMEM, VMEM, VMEM],
-        out_specs=VMEM,
+    )(
+        pltpu.with_memory_space_constraint(intersection.T, pltpu.HBM),
+        pltpu.with_memory_space_constraint(counts, pltpu.HBM),
+        phi_values,
+        panel_values,
+        site,
+    )
+    far, left = lax.optimization_barrier((far, left))
+    pair = jnp.concatenate([proj_panel, far], axis=2)
+    next_pair = swap(pair)
+    got[2], left, next_pair = lax.optimization_barrier((got[2], left, next_pair))
+    swapped = {2: swap(got[2])}
+    got[1], other = lax.optimization_barrier((got[1], other))
+    term, rho, proj = pl.pallas_call(
+        functools.partial(early_kernel, cells),
+        out_shape=(
+            jax.ShapeDtypeStruct((cells, states), F32),
+            jax.ShapeDtypeStruct((own, own), F32),
+            jax.ShapeDtypeStruct((own, packed), BF16),
+        ),
+        in_specs=[VMEM] * 8,
+        out_specs=(VMEM, VMEM, VMEM),
         compiler_params=PARAMS,
-    )(counts, pair.reshape(own, -1), far_pair.reshape(own, -1))
-    got[3], left = lax.optimization_barrier((got[3], left))
-    swapped = {3: swap(got[3])}
-    got[2], proj = lax.optimization_barrier((got[2], proj))
-    early = pl.pallas_call(
-        functools.partial(early_kernel, cells),
-        out_shape=(jax.ShapeDtypeStruct((cells, states), F32), jax.ShapeDtypeStruct((own, own), F32)),
-        in_specs=[VMEM] * 6,
-        out_specs=(VMEM, VMEM),
-        compiler_params=PARAMS,
-    )(left, proj, block, other, got[3], swapped[3])
-    swapped |= {k: swap(got[k]) for k in (2, 1)}
+    )(left, columns, pair.reshape(own, -1), next_pair.reshape(own, -1), block, other, got[2], swapped[2])
+    swapped |= {k: swap(got[k]) for k in (1, 3)}
     density, rho = pl.pallas_call(
         functools.partial(late_kernel, cells),
         out_shape=(
@@ -333,7 +368,7 @@
         in_specs=[VMEM] * 8,
         out_specs=(VMEM, VMEM),
         compiler_params=PARAMS,
-    )(left, proj, got[2], swapped[2], got[1], swapped[1], *early)
+    )(left, proj, got[1], swapped[1], got[3], swapped[3], term, rho)
     return density.reshape(cells), rho
 
 

time: 19.8 us -> 19.1 us (0.965)
  local copies, waits for them, and re-layouts: 1.44 us -> 0.77 us
  Pallas kernels: 5.38 us -> 4.72 us
  starting transfers between devices: 9.5 us -> 9.95 us
  waiting for transfers between devices: 2.45 us -> 2.68 us
    pallas_call x2 -> x1, Pallas kernels: 2.02 us -> 1.26 us  [gather_shards(): pl.pallas_call(functools.partial(left_kernel, n_col, n_slab), out_shape=(...]
    unnamed x14 -> x9, local copies, waits for them, and re-layouts: 1.42 us -> 0.75 us
    ppermute x9, starting transfers between devices: 9.5 us -> 9.95 us  [move(): return lax.ppermute(block, axes, pairs)]
    ppermute x9, waiting for transfers between devices: 2.45 us -> 2.68 us  [move(): return lax.ppermute(block, axes, pairs)]
  transfers between devices with their start and end apart: 9 -> 9, of which waited for: 3 -> 4; matrix products, arithmetic and copies ran while one was open for 1% -> 0% of each run, Pallas kernels for 14% -> 11%
where the time goes in v4:
time: 19.1 us; the launch traced here: 18.9 us
  starting transfers between devices  9.95 us (52%)
  Pallas kernels  4.72 us (25%)
  waiting for transfers between devices  2.68 us (14%)
  local copies, waits for them, and re-layouts  0.77 us (4%)
  between operations  0.73 us (4%)
    ppermute x9, starting transfers between devices, move(): return lax.ppermute(block, axes, pairs)  9.95 us
    ppermute x9, waiting for transfers between devices, move(): return lax.ppermute(block, axes, pairs)  2.68 us
    pallas_call x1, Pallas kernels, gather_shards(): pl.pallas_call(functools.partial(late_kernel, cells), out_shape=(jax.Shap...  1.44 us
    pallas_call x1, Pallas kernels, gather_shards(): pl.pallas_call(pack_kernel, out_shape=jax.ShapeDtypeStruct((packed, state...  1.28 us
    pallas_call x1, Pallas kernels, gather_shards(): pl.pallas_call(functools.partial(left_kernel, n_col, n_slab), out_shape=(...  1.26 us
    unnamed x9, local copies, waits for them, and re-layouts  0.75 us
    pallas_call x1, Pallas kernels, gather_shards(): pl.pallas_call(functools.partial(early_kernel, cells), out_shape=(jax.Sha...  0.75 us
  transfers between devices with their start and end apart: 9, of which 4 were waited for; matrix products, arithmetic and copies ran while one was open for 0% of the time, Pallas kernels for 11%

profile of v4, /device:TPU:0, one launch (start us, length us, event | category | flops | bytes accessed | tf_op | source)
XLA Modules:
  0.0 18.9 jit_solution(4734955440663650485)
XLA Ops:
  0.7 1.3 %shard_map.95.a_ref = bf16[432,128]{1,0:T(8,128)(2,1)S(1)} custom-call(s32[128]{0:T(128)} %occ_ref.1, bf16[512,128]{1,0:T(8,128)(2,1)} %coeffs_ref.1), custom_call_target="tpu_custom_call" | custom-call | tf_op jit(solution)/shard_map/pallas_call | solution.py:304
  1.9 0.0 copy-start.2
  2.0 4.1 %collective-permute-start = (bf16[432,128]{1,0:T(8,128)(2,1)S(1)}, bf16[432,128]{1,0:T(8,128)(2,1)S(1)}, u32[]{:S(2)}, u32[]{:S(2)}) collective-permute-start(bf16[432,128]{1,0:T(8,128)(2,1)S(1)} %shard_map.95.a_ref), channel_id=1, source_target_pairs={{0,8},{1,25},{2,10},{3,27},{4,12},{5,29},{6,14},{7,31},{8,0},{9,17... | collective-permute-start | bytes 331784 | tf_op jit(solution)/shard_map/ppermute | solution.py:293
  6.1 1.6 %collective-permute-start.3 = (bf16[432,128]{1,0:T(8,128)(2,1)S(1)}, bf16[432,128]{1,0:T(8,128)(2,1)S(1)}, u32[]{:S(2)}, u32[]{:S(2)}) collective-permute-start(bf16[432,128]{1,0:T(8,128)(2,1)S(1)} %shard_map.95.a_ref), channel_id=1, source_target_pairs={{0,4},{1,21},{2,6},{3,23},{4,0},{5,17},{6,2},{7,19},{8,12},{9,29},... | collective-permute-start | bytes 331784 | tf_op jit(solution)/shard_map/ppermute | solution.py:293
  7.6 1.5 %collective-permute-start.4 = (bf16[432,128]{1,0:T(8,128)(2,1)S(1)}, bf16[432,128]{1,0:T(8,128)(2,1)S(1)}, u32[]{:S(2)}, u32[]{:S(2)}) collective-permute-start(bf16[432,128]{1,0:T(8,128)(2,1)S(1)} %shard_map.95.a_ref), channel_id=1, source_target_pairs={{0,16},{1,17},{2,18},{3,19},{4,20},{5,21},{6,22},{7,23},{8,24},{9,... | collective-permute-start | bytes 331784 | tf_op jit(solution)/shard_map/ppermute | solution.py:293
  9.1 0.2 %collective-permute-start.7 = (bf16[432,128]{1,0:T(8,128)(2,1)S(1)}, bf16[432,128]{1,0:T(8,128)(2,1)S(1)}, u32[]{:S(2)}, u32[]{:S(2)}) collective-permute-start(bf16[432,128]{1,0:T(8,128)(2,1)S(1)} %shard_map.95.a_ref), channel_id=1, source_target_pairs={{0,12},{1,29},{2,14},{3,31},{4,8},{5,25},{6,10},{7,27},{8,4},{9,21... | collective-permute-start | bytes 331784 | tf_op jit(solution)/shard_map/ppermute | solution.py:293
  9.3 1.5 %collective-permute-start.1 = (bf16[8,16,128]{2,1,0:T(8,128)(2,1)S(1)}, bf16[8,16,128]{2,1,0:T(8,128)(2,1)S(1)}, u32[]{:S(2)}, u32[]{:S(2)}) collective-permute-start(bf16[8,16,128]{2,1,0:T(8,128)(2,1)S(1)} %copy-done.3), channel_id=1, source_target_pairs={{0,2},{1,3},{2,0},{3,1},{4,6},{5,7},{6,4},{7,5},{8,10},{9,11},{10,... | collective-permute-start | bytes 98312 | tf_op jit(solution)/shard_map/ppermute | solution.py:293
  10.9 0.0 copy-start.1
  10.9 0.7 %copy-done.1 = bf16[128,128]{1,0:T(8,128)(2,1)S(1)} copy-done((bf16[128,128]{1,0:T(8,128)(2,1)S(1)}, bf16[128,128]{1,0:T(8,128)(2,1)}, u32[]{:S(2)}) %copy-start.1) | copy-done | bytes 32792
  11.6 1.3 %shard_map.96 = (bf16[2,384,432]{2,1,0:T(8,128)(2,1)S(1)}, bf16[512,432]{1,0:T(8,128)(2,1)S(1)}) custom-call(s32[8,32]{1,0:T(8,128)} %bitcast.12, s32[64]{0:T(128)} %counts_hbm.1, bf16[128,128]{1,0:T(8,128)(2,1)S(1)} %copy-done.1, bf16[128,512]{1,0:T(8,128)(2,1)S(1)} %copy-done, bf16[128,16]{1,0:T(8,128)(2,1)S(1)} %bitcast.10), custom_call_target="tpu_custom_call" | custom-call | flops 200000000 | bytes 2000000 | tf_op jit(solution)/shard_map/pallas_call | solution.py:322
  12.9 0.4 %collective-permute-done.1 = bf16[8,16,128]{2,1,0:T(8,128)(2,1)S(1)} collective-permute-done((bf16[8,16,128]{2,1,0:T(8,128)(2,1)S(1)}, bf16[8,16,128]{2,1,0:T(8,128)(2,1)S(1)}, u32[]{:S(2)}, u32[]{:S(2)}) %collective-permute-start.1) | collective-permute-done | bytes 32800 | tf_op jit(solution)/shard_map/ppermute | solution.py:293
  13.3 0.1 collective-permute-start.2
  13.4 1.2 %collective-permute-done.2 = bf16[8,16,256]{2,1,0:T(8,128)(2,1)S(1)} collective-permute-done((bf16[8,16,256]{2,1,0:T(8,128)(2,1)S(1)}, bf16[8,16,256]{2,1,0:T(8,128)(2,1)S(1)}, u32[]{:S(2)}, u32[]{:S(2)}) %collective-permute-start.2) | collective-permute-done | bytes 65568 | tf_op jit(solution)/shard_map/ppermute | solution.py:293
  14.6 0.0 collective-permute-done.c_ref
  14.6 0.2 collective-permute-start.5
  14.8 0.0 collective-permute-done.3.a_ref
  14.8 0.0 collective-permute-done.4.b_ref
  14.8 0.4 %collective-permute-start.6 = (bf16[432,128]{1,0:T(8,128)(2,1)S(1)}, bf16[432,128]{1,0:T(8,128)(2,1)S(1)}, u32[]{:S(2)}, u32[]{:S(2)}) collective-permute-start(bf16[432,128]{1,0:T(8,128)(2,1)S(1)} %collective-permute-done.3.a_ref), channel_id=1, source_target_pairs={{0,1},{1,0},{2,3},{3,2},{4,5},{5,4},{6,7},{7,6},{8,9},{9,8},{10,11... | collective-permute-start | bytes 331784 | tf_op jit(solution)/shard_map/ppermute | solution.py:293
  15.1 0.9 %collective-permute-done.7.c_ref = bf16[432,128]{1,0:T(8,128)(2,1)S(1)} collective-permute-done((bf16[432,128]{1,0:T(8,128)(2,1)S(1)}, bf16[432,128]{1,0:T(8,128)(2,1)S(1)}, u32[]{:S(2)}, u32[]{:S(2)}) %collective-permute-start.7) | collective-permute-done | bytes 110624 | tf_op jit(solution)/shard_map/ppermute | solution.py:293
  16.0 0.5 %collective-permute-start.8 = (bf16[432,128]{1,0:T(8,128)(2,1)S(1)}, bf16[432,128]{1,0:T(8,128)(2,1)S(1)}, u32[]{:S(2)}, u32[]{:S(2)}) collective-permute-start(bf16[432,128]{1,0:T(8,128)(2,1)S(1)} %collective-permute-done.7.c_ref), channel_id=1, source_target_pairs={{0,1},{1,0},{2,3},{3,2},{4,5},{5,4},{6,7},{7,6},{8,9},{9,8},{10,11... | collective-permute-start | bytes 331784 | tf_op jit(solution)/shard_map/ppermute | solution.py:293
  16.5 0.0 collective-permute-done.5.d_ref
  16.5 0.7 %shard_map.97 = (f32[128,128]{1,0:T(8,128)S(1)}, f32[128,128]{1,0:T(8,128)S(1)}, bf16[128,432]{1,0:T(8,128)(2,1)S(1)}) custom-call(bf16[2,384,432]{2,1,0:T(8,128)(2,1)S(1)} %get-tuple-element.19.left_ref, bf16[512,432]{1,0:T(8,128)(2,1)S(1)} %get-tuple-element.20.columns_ref, bf16[128,256]{1,0:T(8,128)(2,1)S(1)} %bitcast.8, bf16[128,256]{1,0:T(8,128)(2,1)S(1)} %bitcast.9, ...), custom_call_target="tpu_custom_call" | custom-call | tf_op jit(solution)/shard_map/pallas_call | solution.py:350
  17.2 0.2 %collective-permute-done.8.d_ref = bf16[432,128]{1,0:T(8,128)(2,1)S(1)} collective-permute-done((bf16[432,128]{1,0:T(8,128)(2,1)S(1)}, bf16[432,128]{1,0:T(8,128)(2,1)S(1)}, u32[]{:S(2)}, u32[]{:S(2)}) %collective-permute-start.8) | collective-permute-done | bytes 110624 | tf_op jit(solution)/shard_map/ppermute | solution.py:293
  17.4 1.4 %shard_map.98 = (f32[1,128]{1,0:T(1,128)}, f32[8,256]{1,0:T(8,128)}) custom-call(bf16[2,384,432]{2,1,0:T(8,128)(2,1)S(1)} %get-tuple-element.19.left_ref, bf16[128,432]{1,0:T(8,128)(2,1)S(1)} %get-tuple-element.24.proj_ref, bf16[432,128]{1,0:T(8,128)(2,1)S(1)} %collective-permute-done.3.a_ref, bf16[432,128]{1,0:T(8,128)(2,1)S(1)} %collective-permute-done.6.b_ref, ...), custom_call_target="tpu_custom_call" | custom-call | tf_op jit(solution)/shard_map/pallas_call | solution.py:362
  (9 shorter events, 0.0 us)
Async XLA Ops:
  0.6 8.7 %copy-start.3 = (bf16[8,16,128]{2,1,0:T(8,128)(2,1)S(1)}, bf16[8,16,128]{2,1,0:T(8,128)(2,1)}, u32[]{:S(2)}) copy-start(bf16[8,16,128]{2,1,0:T(8,128)(2,1)} %param.15) | copy-start | bytes 98308
  0.6 10.3 %copy-start = (bf16[128,512]{1,0:T(8,128)(2,1)S(1)}, bf16[128,512]{1,0:T(8,128)(2,1)}, u32[]{:S(2)}) copy-start(bf16[128,512]{1,0:T(8,128)(2,1)} %panel_ref.1) | copy-start | bytes 393220
  1.9 8.9 %copy-start.2 = (bf16[8,16,16]{2,1,0:T(8,128)(2,1)S(1)}, bf16[8,16,16]{2,1,0:T(8,128)(2,1)}, u32[]{:S(2)}) copy-start(bf16[8,16,16]{2,1,0:T(8,128)(2,1)} %param.14) | copy-start | bytes 12292
  2.0 12.6 %collective-permute-start = (bf16[432,128]{1,0:T(8,128)(2,1)S(1)}, bf16[432,128]{1,0:T(8,128)(2,1)S(1)}, u32[]{:S(2)}, u32[]{:S(2)}) collective-permute-start(bf16[432,128]{1,0:T(8,128)(2,1)S(1)} %shard_map.95.a_ref), channel_id=1, source_target_pairs={{0,8},{1,25},{2,10},{3,27},{4,12},{5,29},{6,14},{7,31},{8,0},{9,17... | collective-permute-start | bytes 331784 | tf_op jit(solution)/shard_map/ppermute | solution.py:293
  6.1 8.7 %collective-permute-start.3 = (bf16[432,128]{1,0:T(8,128)(2,1)S(1)}, bf16[432,128]{1,0:T(8,128)(2,1)S(1)}, u32[]{:S(2)}, u32[]{:S(2)}) collective-permute-start(bf16[432,128]{1,0:T(8,128)(2,1)S(1)} %shard_map.95.a_ref), channel_id=1, source_target_pairs={{0,4},{1,21},{2,6},{3,23},{4,0},{5,17},{6,2},{7,19},{8,12},{9,29},... | collective-permute-start | bytes 331784 | tf_op jit(solution)/shard_map/ppermute | solution.py:293
  7.6 7.1 %collective-permute-start.4 = (bf16[432,128]{1,0:T(8,128)(2,1)S(1)}, bf16[432,128]{1,0:T(8,128)(2,1)S(1)}, u32[]{:S(2)}, u32[]{:S(2)}) collective-permute-start(bf16[432,128]{1,0:T(8,128)(2,1)S(1)} %shard_map.95.a_ref), channel_id=1, source_target_pairs={{0,16},{1,17},{2,18},{3,19},{4,20},{5,21},{6,22},{7,23},{8,24},{9,... | collective-permute-start | bytes 331784 | tf_op jit(solution)/shard_map/ppermute | solution.py:293
  9.1 6.9 %collective-permute-start.7 = (bf16[432,128]{1,0:T(8,128)(2,1)S(1)}, bf16[432,128]{1,0:T(8,128)(2,1)S(1)}, u32[]{:S(2)}, u32[]{:S(2)}) collective-permute-start(bf16[432,128]{1,0:T(8,128)(2,1)S(1)} %shard_map.95.a_ref), channel_id=1, source_target_pairs={{0,12},{1,29},{2,14},{3,31},{4,8},{5,25},{6,10},{7,27},{8,4},{9,21... | collective-permute-start | bytes 331784 | tf_op jit(solution)/shard_map/ppermute | solution.py:293
  9.3 3.9 %collective-permute-start.1 = (bf16[8,16,128]{2,1,0:T(8,128)(2,1)S(1)}, bf16[8,16,128]{2,1,0:T(8,128)(2,1)S(1)}, u32[]{:S(2)}, u32[]{:S(2)}) collective-permute-start(bf16[8,16,128]{2,1,0:T(8,128)(2,1)S(1)} %copy-done.3), channel_id=1, source_target_pairs={{0,2},{1,3},{2,0},{3,1},{4,6},{5,7},{6,4},{7,5},{8,10},{9,11},{10,... | collective-permute-start | bytes 98312 | tf_op jit(solution)/shard_map/ppermute | solution.py:293
  10.9 0.8 %copy-start.1 = (bf16[128,128]{1,0:T(8,128)(2,1)S(1)}, bf16[128,128]{1,0:T(8,128)(2,1)}, u32[]{:S(2)}) copy-start(bf16[128,128]{1,0:T(8,128)(2,1)} %phi_ref.1) | copy-start | bytes 98308
  13.3 1.3 %collective-permute-start.2 = (bf16[8,16,256]{2,1,0:T(8,128)(2,1)S(1)}, bf16[8,16,256]{2,1,0:T(8,128)(2,1)S(1)}, u32[]{:S(2)}, u32[]{:S(2)}) collective-permute-start(bf16[8,16,256]{2,1,0:T(8,128)(2,1)S(1)} %constant_dynamic-update-slice_fusion), channel_id=1, source_target_pairs={{0,1},{1,0},{2,3},{3,2},{4,5},{5,4},{6,7},{7,6},{8,9},{9,8},{10,11... | collective-permute-start | bytes 196616 | tf_op jit(solution)/shard_map/ppermute | solution.py:293
  14.6 1.9 %collective-permute-start.5 = (bf16[432,128]{1,0:T(8,128)(2,1)S(1)}, bf16[432,128]{1,0:T(8,128)(2,1)S(1)}, u32[]{:S(2)}, u32[]{:S(2)}) collective-permute-start(bf16[432,128]{1,0:T(8,128)(2,1)S(1)} %collective-permute-done.c_ref), channel_id=1, source_target_pairs={{0,1},{1,0},{2,3},{3,2},{4,5},{5,4},{6,7},{7,6},{8,9},{9,8},{10,11... | collective-permute-start | bytes 331784 | tf_op jit(solution)/shard_map/ppermute | solution.py:293
  14.8 2.4 %collective-permute-start.6 = (bf16[432,128]{1,0:T(8,128)(2,1)S(1)}, bf16[432,128]{1,0:T(8,128)(2,1)S(1)}, u32[]{:S(2)}, u32[]{:S(2)}) collective-permute-start(bf16[432,128]{1,0:T(8,128)(2,1)S(1)} %collective-permute-done.3.a_ref), channel_id=1, source_target_pairs={{0,1},{1,0},{2,3},{3,2},{4,5},{5,4},{6,7},{7,6},{8,9},{9,8},{10,11... | collective-permute-start | bytes 331784 | tf_op jit(solution)/shard_map/ppermute | solution.py:293
  16.0 1.4 %collective-permute-start.8 = (bf16[432,128]{1,0:T(8,128)(2,1)S(1)}, bf16[432,128]{1,0:T(8,128)(2,1)S(1)}, u32[]{:S(2)}, u32[]{:S(2)}) collective-permute-start(bf16[432,128]{1,0:T(8,128)(2,1)S(1)} %collective-permute-done.7.c_ref), channel_id=1, source_target_pairs={{0,1},{1,0},{2,3},{3,2},{4,5},{5,4},{6,7},{7,6},{8,9},{9,8},{10,11... | collective-permute-start | bytes 331784 | tf_op jit(solution)/shard_map/ppermute | solution.py:293

commit v5 on v4

--- a/solution.py
+++ b/solution.py
@@ -116,29 +116,39 @@
     return rows // SLOTS * LIVE + 16
 
 
-def pack_kernel(occ_ref, coeffs_ref, out_ref, occ, held, arrived):
+def pack_kernel(occ_ref, coeffs_ref, out_ref, half_ref, occ, held, arrived):
     rows = coeffs_ref.shape[0]
     group = 16
     span = group * SLOTS
+    groups = rows // span
     copies = [
         pltpu.make_async_copy(
             coeffs_ref.at[pl.ds(g * span, span)], held.at[pl.ds(g * span, span)], arrived.at[g]
         )
-        for g in range(rows // span)
+        for g in range(groups)
     ]
-    last = pltpu.make_async_copy(occ_ref, occ, arrived.at[rows // span])
+    last = pltpu.make_async_copy(occ_ref, occ, arrived.at[groups])
     for copy in copies:
         copy.start()
     last.start()
     old = iota((group * LIVE, span), 1)
     slot = old & (SLOTS - 1)
     move = pick(((old >> 4) * LIVE + slot == iota((group * LIVE, span), 0)) & (slot < LIVE))
+    tiles = []
     for g, copy in enumerate(copies):
         copy.wait()
-        out_ref[g * group * LIVE : (g + 1) * group * LIVE, :] = take(move, held[g * span : (g + 1) * span, :])
+        tiles.append(take(move, held[g * span : (g + 1) * span, :]))
+        out_ref[g * group * LIVE : (g + 1) * group * LIVE, :] = tiles[-1]
     last.wait()
     weights = occ[...].reshape(1, occ.shape[0]).astype(F32) * 0.5
-    out_ref[rows // SLOTS * LIVE :, :] = jnp.broadcast_to(weights, (16, weights.shape[1])).astype(BF16)
+    weights = jnp.broadcast_to(weights, (16, weights.shape[1])).astype(BF16)
+    out_ref[rows // SLOTS * LIVE :, :] = weights
+    odd = (lax.axis_index("dz") & 1) == 1
+    size = half_ref.shape[0] - 16
+    for t in range(groups // 2):
+        at = t * group * LIVE
+        half_ref[at : at + group * LIVE, :] = jnp.where(odd, tiles[groups // 2 + t], tiles[t])
+    half_ref[size:, :] = weights
 
 
 def panel_map(counts_ref, packed):
@@ -218,11 +228,11 @@
     return high, (values - high.astype(F32)).astype(BF16)
 
 
-def partial_sums(a, b, near, cells, left_ref, proj_ref):
+def partial_sums(a, b, near, cells, left_ref, proj):
     weight_row = left_ref.shape[2] - 16
     r = jnp.dot(left_ref[near], a, preferred_element_type=F32)
     r += jnp.dot(left_ref[1 - near], b, preferred_element_type=F32)
-    right = jnp.dot(proj_ref[...], jnp.where(near == 0, a, b), preferred_element_type=F32)
+    right = jnp.dot(proj, jnp.where(near == 0, a, b), preferred_element_type=F32)
     f = a[weight_row:, :].astype(F32)[0:1]
     term = r[:cells] * f * r[cells : 2 * cells]
     term = sum(term[:, at : at + cells] for at in range(0, term.shape[1], cells))
@@ -235,34 +245,47 @@
     return term, rho
 
 
-def early_kernel(
-    cells, left_ref, columns_ref, here_ref, next_ref, a_ref, b_ref, c_ref, d_ref, term_ref, rho_ref, proj_ref
+def sum_kernel(
+    cells,
+    left_ref,
+    columns_ref,
+    block_ref,
+    other_ref,
+    here_ref,
+    next_ref,
+    a_ref,
+    b_ref,
+    c_ref,
+    d_ref,
+    density_ref,
+    rho_ref,
 ):
     x, s = lax.axis_index("prow"), lax.axis_index("dz")
     odd, back = (s & 1) == 1, (s & 2) == 2
     here, after = here_ref[...], next_ref[...]
     evens, odds = jnp.where(odd, after, here), jnp.where(odd, here, after)
-    half = here.shape[1] // 2
-    low = [evens[:, :half], odds[:, :half]]
-    high = [evens[:, half:], odds[:, half:]]
-    front = [jnp.where(back, h, l) for l, h in zip(low, high)]
-    rear = [jnp.where(back, l, h) for l, h in zip(low, high)]
-    proj_ref[...] = take(jnp.concatenate(front + rear, axis=1), columns_ref[...])
-    c, d = c_ref[...], d_ref[...]
-    a = jnp.concatenate([a_ref[...], jnp.where(odd, d, c)], axis=1)
-    b = jnp.concatenate([b_ref[...], jnp.where(odd, c, d)], axis=1)
-    term_ref[...], rho_ref[...] = partial_sums(a, b, x, cells, left_ref, proj_ref)
-
-
-def late_kernel(cells, left_ref, proj_ref, a_ref, b_ref, c_ref, d_ref, term_ref, part_ref, density_ref, rho_ref):
-    near = lax.axis_index("prow") ^ (lax.axis_index("dz") & 1)
-    a = jnp.concatenate([a_ref[...], c_ref[...]], axis=1)
-    b = jnp.concatenate([b_ref[...], d_ref[...]], axis=1)
-    term, rho = partial_sums(a, b, near, cells, left_ref, proj_ref)
-    term += term_ref[...]
-    rho += part_ref[...]
+    half = (left_ref.shape[2] - 16) // 2
+    size = half + 16
+
+    def joined(at):
+        return jnp.concatenate([evens[at : at + half], odds[at : at + size]], axis=0)
+
+    one, two = joined(0), joined(size)
+    fetched = jnp.concatenate([a_ref[...], c_ref[...]], axis=1)
+    swapped = jnp.concatenate([b_ref[...], d_ref[...]], axis=1)
+    near = jnp.concatenate(
+        [block_ref[...], jnp.where(back, two, one), jnp.where(odd, swapped, fetched)], axis=1
+    )
+    far = jnp.concatenate(
+        [other_ref[...], jnp.where(back, one, two), jnp.where(odd, fetched, swapped)], axis=1
+    )
+    own = left_ref.shape[1] - 2 * cells
+    last, first = 2 * size, 2 * size + own
+    front = [jnp.where(back, part[last:first], part[first:]) for part in (evens, odds)]
+    rear = [jnp.where(back, part[first:], part[last:first]) for part in (evens, odds)]
+    proj = take(jnp.concatenate(front + rear, axis=1), columns_ref[...])
+    term, rho = partial_sums(near, far, x, cells, left_ref, proj)
     density_ref[...] = jnp.sum(term.T, axis=0, keepdims=True)
-    own = proj_ref.shape[0]
     atoms = own // NPROJ
     rho = jnp.where((iota((own, own), 0) & (atoms - 1)) == (iota((own, own), 1) >> 4), rho, 0.0)
     wide = NPROJ * NPROJ
@@ -273,7 +296,6 @@
 
 
 VMEM = pl.BlockSpec(memory_space=pltpu.VMEM)
-SMEM = pl.BlockSpec(memory_space=pltpu.SMEM)
 HBM = pl.BlockSpec(memory_space=pltpu.HBM)
 PARAMS = pltpu.CompilerParams(vmem_limit_bytes=32 * 2**20)
 
@@ -300,12 +322,15 @@
     atoms_own = proj_site.shape[0]
     own = atoms_own * NPROJ
     cells = phi_values.shape[0]
-    far = move(proj_panel, lambda x, z, s: (x, z, s ^ 2))
-    block = pl.pallas_call(
+    half = packed_rows(rows // 2)
+    block, part = pl.pallas_call(
         pack_kernel,
-        out_shape=jax.ShapeDtypeStruct((packed, states), BF16),
+        out_shape=(
+            jax.ShapeDtypeStruct((packed, states), BF16),
+            jax.ShapeDtypeStruct((half, states), BF16),
+        ),
         in_specs=[HBM, HBM],
-        out_specs=VMEM,
+        out_specs=(VMEM, VMEM),
         scratch_shapes=[
             pltpu.VMEM((states,), jnp.int32),
             pltpu.VMEM((rows, states), BF16),
@@ -316,7 +341,8 @@
         pltpu.with_memory_space_constraint(occupations, pltpu.HBM),
         pltpu.with_memory_space_constraint(coeffs, pltpu.HBM),
     )
-    got = {k: move(block, lambda x, z, s: (x ^ (s & 1), z ^ k, s)) for k in (1, 2, 3)}
+    part = move(part, lambda x, z, s: (x ^ (s >> 1 & 1), z ^ 2, s))
+    got = {k: move(block, lambda x, z, s: (x ^ (s & 1), z ^ k, s)) for k in (1, 3)}
     other = move(block, lambda x, z, s: (x ^ 1, z, s))
     site = proj_site.transpose(1, 0, 2).reshape(own, SLOTS)
     left, columns = pl.pallas_call(
@@ -341,34 +367,23 @@
         panel_values,
         site,
     )
-    far, left = lax.optimization_barrier((far, left))
-    pair = jnp.concatenate([proj_panel, far], axis=2)
-    next_pair = swap(pair)
-    got[2], left, next_pair = lax.optimization_barrier((got[2], left, next_pair))
-    swapped = {2: swap(got[2])}
-    got[1], other = lax.optimization_barrier((got[1], other))
-    term, rho, proj = pl.pallas_call(
-        functools.partial(early_kernel, cells),
-        out_shape=(
-            jax.ShapeDtypeStruct((cells, states), F32),
-            jax.ShapeDtypeStruct((own, own), F32),
-            jax.ShapeDtypeStruct((own, packed), BF16),
-        ),
-        in_specs=[VMEM] * 8,
-        out_specs=(VMEM, VMEM, VMEM),
-        compiler_params=PARAMS,
-    )(left, columns, pair.reshape(own, -1), next_pair.reshape(own, -1), block, other, got[2], swapped[2])
-    swapped |= {k: swap(got[k]) for k in (1, 3)}
+    projectors = proj_panel.reshape(own, -1)
+    far = move(jnp.concatenate([part, projectors], axis=0), lambda x, z, s: (x, z, s ^ 2))
+    other, got[3], got[1], left, far = lax.optimization_barrier((other, got[3], got[1], left, far))
+    here = jnp.concatenate([part, far, projectors], axis=0)
+    after = swap(here)
+    swapped = {1: swap(got[1])}
+    swapped[3] = swap(got[3])
     density, rho = pl.pallas_call(
-        functools.partial(late_kernel, cells),
+        functools.partial(sum_kernel, cells),
         out_shape=(
             jax.ShapeDtypeStruct((1, cells), F32),
             jax.ShapeDtypeStruct((atoms_own, NPROJ * NPROJ), F32),
         ),
-        in_specs=[VMEM] * 8,
+        in_specs=[VMEM] * 10,
         out_specs=(VMEM, VMEM),
         compiler_params=PARAMS,
-    )(left, proj, got[1], swapped[1], got[3], swapped[3], term, rho)
+    )(left, columns, block, other, here, after, got[1], swapped[1], got[3], swapped[3])
     return density.reshape(cells), rho
 
 
@@ -376,7 +391,7 @@
     n_row, n_col, n_slab = (lax.axis_size(a) for a in ("prow", "pcol", "dz"))
     rows = coeffs.shape[0]
     fits = coeffs.size * 2 * n_row * n_col <= GATHER_LIMIT
-    regular = n_row == 2 and n_col == 4 and n_slab == 4 and rows >= PW and rows % 256 == 0
+    regular = n_row == 2 and n_col == 4 and n_slab == 4 and rows >= PW and rows % 512 == 0
     plan = gather_shards if fits and regular else exchange_shards
     return plan(coeffs, occupations, counts, intersection, phi_values, panel_values, proj_site, proj_panel)
 

time: 19.1 us -> 18.7 us (0.979)
  waiting for transfers between devices: 2.68 us -> 2.28 us
  Pallas kernels: 4.72 us -> 4.35 us
  starting transfers between devices: 9.95 us -> 10.3 us
    ppermute x9 -> x8, waiting for transfers between devices: 2.68 us -> 2.28 us  [move(): return lax.ppermute(block, axes, pairs)]
    pallas_call x3 -> x2, Pallas kernels: 3.47 us -> 3.11 us  [the longest x1 1.85 us: gather_shards(): pl.pallas_call(functools.partial(sum_kernel, cells), out_shape=(jax.Shape...]
    ppermute x9 -> x8, starting transfers between devices: 9.95 us -> 10.3 us  [move(): return lax.ppermute(block, axes, pairs)]
    unnamed x9 -> x8, local copies, waits for them, and re-layouts: 0.75 us -> 0.75 us
  transfers between devices with their start and end apart: 9 -> 8, of which waited for: 4 -> 3; matrix products, arithmetic and copies ran while one was open for 0% -> 0% of each run, Pallas kernels for 11% -> 7%
where the time goes in v5:
time: 18.7 us; the launch traced here: 18.4 us
  starting transfers between devices  10.3 us (55%)
  Pallas kernels  4.35 us (23%)
  waiting for transfers between devices  2.28 us (12%)
  local copies, waits for them, and re-layouts  0.76 us (4%)
  between operations  0.71 us (4%)
    ppermute x8, starting transfers between devices, move(): return lax.ppermute(block, axes, pairs)  10.3 us
    ppermute x8, waiting for transfers between devices, move(): return lax.ppermute(block, axes, pairs)  2.28 us
    pallas_call x1, Pallas kernels, gather_shards(): pl.pallas_call(functools.partial(sum_kernel, cells), out_shape=(jax.Shape...  1.85 us
    pallas_call x1, Pallas kernels, gather_shards(): pl.pallas_call(pack_kernel, out_shape=(jax.ShapeDtypeStruct((packed, stat...  1.26 us
    pallas_call x1, Pallas kernels, gather_shards(): pl.pallas_call(functools.partial(left_kernel, n_col, n_slab), out_shape=(...  1.25 us
    unnamed x8, local copies, waits for them, and re-layouts  0.75 us
  transfers between devices with their start and end apart: 8, of which 3 were waited for; matrix products, arithmetic and copies ran while one was open for 0% of the time, Pallas kernels for 7%

profile of v5, /device:TPU:0, one launch (start us, length us, event | category | flops | bytes accessed | tf_op | source)
XLA Modules:
  0.0 18.4 jit_solution(16838568130236518992)
XLA Ops:
  0.6 0.0 copy-start.2
  0.6 1.3 %shard_map.95 = (bf16[432,128]{1,0:T(8,128)(2,1)S(1)}, bf16[224,128]{1,0:T(8,128)(2,1)S(1)}) custom-call(s32[128]{0:T(128)} %occ_ref.1, bf16[512,128]{1,0:T(8,128)(2,1)} %coeffs_ref.1), custom_call_target="tpu_custom_call" | custom-call | tf_op jit(solution)/shard_map/pallas_call | solution.py:326
  1.9 0.0 copy-start
  1.9 4.1 %collective-permute-start.3 = (bf16[224,128]{1,0:T(8,128)(2,1)S(1)}, bf16[224,128]{1,0:T(8,128)(2,1)S(1)}, u32[]{:S(2)}, u32[]{:S(2)}) collective-permute-start(bf16[224,128]{1,0:T(8,128)(2,1)S(1)} %get-tuple-element.15), channel_id=1, source_target_pairs={{0,8},{1,9},{2,26},{3,27},{4,12},{5,13},{6,30},{7,31},{8,0},{9,1},... | collective-permute-start | bytes 172040 | tf_op jit(solution)/shard_map/ppermute | solution.py:315
  6.0 1.6 %collective-permute-start.2 = (bf16[432,128]{1,0:T(8,128)(2,1)S(1)}, bf16[432,128]{1,0:T(8,128)(2,1)S(1)}, u32[]{:S(2)}, u32[]{:S(2)}) collective-permute-start(bf16[432,128]{1,0:T(8,128)(2,1)S(1)} %get-tuple-element.13.block_ref), channel_id=1, source_target_pairs={{0,4},{1,21},{2,6},{3,23},{4,0},{5,17},{6,2},{7,19},{8,12},{9,29},... | collective-permute-start | bytes 331784 | tf_op jit(solution)/shard_map/ppermute | solution.py:315
  7.6 0.0 collective-permute-start.1
  7.6 1.7 %collective-permute-start = (bf16[432,128]{1,0:T(8,128)(2,1)S(1)}, bf16[432,128]{1,0:T(8,128)(2,1)S(1)}, u32[]{:S(2)}, u32[]{:S(2)}) collective-permute-start(bf16[432,128]{1,0:T(8,128)(2,1)S(1)} %get-tuple-element.13.block_ref), channel_id=1, source_target_pairs={{0,16},{1,17},{2,18},{3,19},{4,20},{5,21},{6,22},{7,23},{8,24},{9,... | collective-permute-start | bytes 331784 | tf_op jit(solution)/shard_map/ppermute | solution.py:315
  9.3 0.0 collective-permute-done.3
  9.3 0.0 copy-done.2
  9.3 2.3 %collective-permute-start.4 = (bf16[352,128]{1,0:T(8,128)(2,1)S(1)}, bf16[352,128]{1,0:T(8,128)(2,1)S(1)}, u32[]{:S(2)}, u32[]{:S(2)}) collective-permute-start(bf16[352,128]{1,0:T(8,128)(2,1)S(1)} %pad_maximum_fusion.1), channel_id=1, source_target_pairs={{0,2},{1,3},{2,0},{3,1},{4,6},{5,7},{6,4},{7,5},{8,10},{9,11},{10,... | collective-permute-start | bytes 270344 | tf_op jit(solution)/shard_map/ppermute | solution.py:315
  11.6 0.0 copy-done.3
  11.6 0.7 %copy-done.1 = bf16[128,128]{1,0:T(8,128)(2,1)S(1)} copy-done((bf16[128,128]{1,0:T(8,128)(2,1)S(1)}, bf16[128,128]{1,0:T(8,128)(2,1)}, u32[]{:S(2)}) %copy-start.1) | copy-done | bytes 32792
  12.4 1.2 %shard_map.96 = (bf16[2,384,432]{2,1,0:T(8,128)(2,1)S(1)}, bf16[512,432]{1,0:T(8,128)(2,1)S(1)}) custom-call(s32[8,32]{1,0:T(8,128)} %bitcast.11, s32[64]{0:T(128)} %counts_hbm.1, bf16[128,128]{1,0:T(8,128)(2,1)S(1)} %copy-done.1, bf16[128,512]{1,0:T(8,128)(2,1)S(1)} %copy-done, bf16[128,16]{1,0:T(8,128)(2,1)S(1)} %bitcast.7), custom_call_target="tpu_custom_call" | custom-call | flops 200000000 | bytes 2000000 | tf_op jit(solution)/shard_map/pallas_call | solution.py:348
  13.6 0.0 collective-permute-done.2.a_ref
  13.6 1.0 %collective-permute-done.1.c_ref = bf16[432,128]{1,0:T(8,128)(2,1)S(1)} collective-permute-done((bf16[432,128]{1,0:T(8,128)(2,1)S(1)}, bf16[432,128]{1,0:T(8,128)(2,1)S(1)}, u32[]{:S(2)}, u32[]{:S(2)}) %collective-permute-start.1) | collective-permute-done | bytes 110624 | tf_op jit(solution)/shard_map/ppermute | solution.py:315
  14.6 0.0 collective-permute-done.other_ref
  14.6 0.0 collective-permute-done.4
  14.7 0.1 collective-permute-start.5
  14.7 0.5 %collective-permute-start.6 = (bf16[432,128]{1,0:T(8,128)(2,1)S(1)}, bf16[432,128]{1,0:T(8,128)(2,1)S(1)}, u32[]{:S(2)}, u32[]{:S(2)}) collective-permute-start(bf16[432,128]{1,0:T(8,128)(2,1)S(1)} %collective-permute-done.2.a_ref), channel_id=1, source_target_pairs={{0,1},{1,0},{2,3},{3,2},{4,5},{5,4},{6,7},{7,6},{8,9},{9,8},{10,11... | collective-permute-start | bytes 331784 | tf_op jit(solution)/shard_map/ppermute | solution.py:315
  15.2 0.1 collective-permute-start.7
  15.3 1.0 %collective-permute-done.6.b_ref = bf16[432,128]{1,0:T(8,128)(2,1)S(1)} collective-permute-done((bf16[432,128]{1,0:T(8,128)(2,1)S(1)}, bf16[432,128]{1,0:T(8,128)(2,1)S(1)}, u32[]{:S(2)}, u32[]{:S(2)}) %collective-permute-start.6) | collective-permute-done | bytes 110624 | tf_op jit(solution)/shard_map/ppermute | solution.py:315
  16.3 0.3 %collective-permute-done.7.d_ref = bf16[432,128]{1,0:T(8,128)(2,1)S(1)} collective-permute-done((bf16[432,128]{1,0:T(8,128)(2,1)S(1)}, bf16[432,128]{1,0:T(8,128)(2,1)S(1)}, u32[]{:S(2)}, u32[]{:S(2)}) %collective-permute-start.7) | collective-permute-done | bytes 110624 | tf_op jit(solution)/shard_map/ppermute | solution.py:315
  16.6 0.0 collective-permute-done.5.next_ref
  16.6 1.8 %shard_map.97 = (f32[1,128]{1,0:T(1,128)}, f32[8,256]{1,0:T(8,128)}) custom-call(bf16[2,384,432]{2,1,0:T(8,128)(2,1)S(1)} %get-tuple-element.16.left_ref, bf16[512,432]{1,0:T(8,128)(2,1)S(1)} %get-tuple-element.17.columns_ref, bf16[432,128]{1,0:T(8,128)(2,1)S(1)} %get-tuple-element.13.block_ref, bf16[432,128]{1,0:T(8,128)(2,1)S(1)} %collective-permute-done.other_ref, ...), custom_call_target="tpu_custom_call" | custom-call | tf_op jit(solution)/shard_map/pallas_call | solution.py:377
  (6 shorter events, 0.0 us)
Async XLA Ops:
  0.6 8.7 %copy-start.2 = (bf16[8,16,128]{2,1,0:T(8,128)(2,1)S(1)}, bf16[8,16,128]{2,1,0:T(8,128)(2,1)}, u32[]{:S(2)}) copy-start(bf16[8,16,128]{2,1,0:T(8,128)(2,1)} %param.15) | copy-start | bytes 98308
  1.9 9.7 %copy-start = (bf16[128,512]{1,0:T(8,128)(2,1)S(1)}, bf16[128,512]{1,0:T(8,128)(2,1)}, u32[]{:S(2)}) copy-start(bf16[128,512]{1,0:T(8,128)(2,1)} %panel_ref.1) | copy-start | bytes 393220
  1.9 7.4 %collective-permute-start.3 = (bf16[224,128]{1,0:T(8,128)(2,1)S(1)}, bf16[224,128]{1,0:T(8,128)(2,1)S(1)}, u32[]{:S(2)}, u32[]{:S(2)}) collective-permute-start(bf16[224,128]{1,0:T(8,128)(2,1)S(1)} %get-tuple-element.15), channel_id=1, source_target_pairs={{0,8},{1,9},{2,26},{3,27},{4,12},{5,13},{6,30},{7,31},{8,0},{9,1},... | collective-permute-start | bytes 172040 | tf_op jit(solution)/shard_map/ppermute | solution.py:315
  6.0 7.6 %collective-permute-start.2 = (bf16[432,128]{1,0:T(8,128)(2,1)S(1)}, bf16[432,128]{1,0:T(8,128)(2,1)S(1)}, u32[]{:S(2)}, u32[]{:S(2)}) collective-permute-start(bf16[432,128]{1,0:T(8,128)(2,1)S(1)} %get-tuple-element.13.block_ref), channel_id=1, source_target_pairs={{0,4},{1,21},{2,6},{3,23},{4,0},{5,17},{6,2},{7,19},{8,12},{9,29},... | collective-permute-start | bytes 331784 | tf_op jit(solution)/shard_map/ppermute | solution.py:315
  7.6 7.0 %collective-permute-start.1 = (bf16[432,128]{1,0:T(8,128)(2,1)S(1)}, bf16[432,128]{1,0:T(8,128)(2,1)S(1)}, u32[]{:S(2)}, u32[]{:S(2)}) collective-permute-start(bf16[432,128]{1,0:T(8,128)(2,1)S(1)} %get-tuple-element.13.block_ref), channel_id=1, source_target_pairs={{0,12},{1,29},{2,14},{3,31},{4,8},{5,25},{6,10},{7,27},{8,4},{9,21... | collective-permute-start | bytes 331784 | tf_op jit(solution)/shard_map/ppermute | solution.py:315
  7.6 7.0 %collective-permute-start = (bf16[432,128]{1,0:T(8,128)(2,1)S(1)}, bf16[432,128]{1,0:T(8,128)(2,1)S(1)}, u32[]{:S(2)}, u32[]{:S(2)}) collective-permute-start(bf16[432,128]{1,0:T(8,128)(2,1)S(1)} %get-tuple-element.13.block_ref), channel_id=1, source_target_pairs={{0,16},{1,17},{2,18},{3,19},{4,20},{5,21},{6,22},{7,23},{8,24},{9,... | collective-permute-start | bytes 331784 | tf_op jit(solution)/shard_map/ppermute | solution.py:315
  9.3 2.3 %copy-start.3 = (bf16[8,16,16]{2,1,0:T(8,128)(2,1)S(1)}, bf16[8,16,16]{2,1,0:T(8,128)(2,1)}, u32[]{:S(2)}) copy-start(bf16[8,16,16]{2,1,0:T(8,128)(2,1)} %param.14) | copy-start | bytes 12292
  9.3 5.3 %collective-permute-start.4 = (bf16[352,128]{1,0:T(8,128)(2,1)S(1)}, bf16[352,128]{1,0:T(8,128)(2,1)S(1)}, u32[]{:S(2)}, u32[]{:S(2)}) collective-permute-start(bf16[352,128]{1,0:T(8,128)(2,1)S(1)} %pad_maximum_fusion.1), channel_id=1, source_target_pairs={{0,2},{1,3},{2,0},{3,1},{4,6},{5,7},{6,4},{7,5},{8,10},{9,11},{10,... | collective-permute-start | bytes 270344 | tf_op jit(solution)/shard_map/ppermute | solution.py:315
  11.6 0.8 %copy-start.1 = (bf16[128,128]{1,0:T(8,128)(2,1)S(1)}, bf16[128,128]{1,0:T(8,128)(2,1)}, u32[]{:S(2)}) copy-start(bf16[128,128]{1,0:T(8,128)(2,1)} %phi_ref.1) | copy-start | bytes 98308
  14.7 1.9 %collective-permute-start.5 = (bf16[704,128]{1,0:T(8,128)(2,1)S(1)}, bf16[704,128]{1,0:T(8,128)(2,1)S(1)}, u32[]{:S(2)}, u32[]{:S(2)}) collective-permute-start(bf16[704,128]{1,0:T(8,128)(2,1)S(1)} %pad_maximum_fusion.here_ref), channel_id=1, source_target_pairs={{0,1},{1,0},{2,3},{3,2},{4,5},{5,4},{6,7},{7,6},{8,9},{9,8},{10,11... | collective-permute-start | bytes 540680 | tf_op jit(solution)/shard_map/ppermute | solution.py:315
  14.7 1.6 %collective-permute-start.6 = (bf16[432,128]{1,0:T(8,128)(2,1)S(1)}, bf16[432,128]{1,0:T(8,128)(2,1)S(1)}, u32[]{:S(2)}, u32[]{:S(2)}) collective-permute-start(bf16[432,128]{1,0:T(8,128)(2,1)S(1)} %collective-permute-done.2.a_ref), channel_id=1, source_target_pairs={{0,1},{1,0},{2,3},{3,2},{4,5},{5,4},{6,7},{7,6},{8,9},{9,8},{10,11... | collective-permute-start | bytes 331784 | tf_op jit(solution)/shard_map/ppermute | solution.py:315
  15.2 1.3 %collective-permute-start.7 = (bf16[432,128]{1,0:T(8,128)(2,1)S(1)}, bf16[432,128]{1,0:T(8,128)(2,1)S(1)}, u32[]{:S(2)}, u32[]{:S(2)}) collective-permute-start(bf16[432,128]{1,0:T(8,128)(2,1)S(1)} %collective-permute-done.1.c_ref), channel_id=1, source_target_pairs={{0,1},{1,0},{2,3},{3,2},{4,5},{5,4},{6,7},{7,6},{8,9},{9,8},{10,11... | collective-permute-start | bytes 331784 | tf_op jit(solution)/shard_map/ppermute | solution.py:315

commit v6 on v5

--- a/solution.py
+++ b/solution.py
@@ -122,24 +122,20 @@
     span = group * SLOTS
     groups = rows // span
     copies = [
-        pltpu.make_async_copy(
-            coeffs_ref.at[pl.ds(g * span, span)], held.at[pl.ds(g * span, span)], arrived.at[g]
-        )
-        for g in range(groups)
+        pltpu.make_async_copy(coeffs_ref, held, arrived.at[0]),
+        pltpu.make_async_copy(occ_ref, occ, arrived.at[1]),
     ]
-    last = pltpu.make_async_copy(occ_ref, occ, arrived.at[groups])
     for copy in copies:
         copy.start()
-    last.start()
     old = iota((group * LIVE, span), 1)
     slot = old & (SLOTS - 1)
     move = pick(((old >> 4) * LIVE + slot == iota((group * LIVE, span), 0)) & (slot < LIVE))
     tiles = []
-    for g, copy in enumerate(copies):
+    for copy in copies:
         copy.wait()
+    for g in range(groups):
         tiles.append(take(move, held[g * span : (g + 1) * span, :]))
         out_ref[g * group * LIVE : (g + 1) * group * LIVE, :] = tiles[-1]
-    last.wait()
     weights = occ[...].reshape(1, occ.shape[0]).astype(F32) * 0.5
     weights = jnp.broadcast_to(weights, (16, weights.shape[1])).astype(BF16)
     out_ref[rows // SLOTS * LIVE :, :] = weights
@@ -334,7 +330,7 @@
         scratch_shapes=[
             pltpu.VMEM((states,), jnp.int32),
             pltpu.VMEM((rows, states), BF16),
-            pltpu.SemaphoreType.DMA((rows // 256 + 1,)),
+            pltpu.SemaphoreType.DMA((2,)),
         ],
         compiler_params=PARAMS,
     )(

time: 18.7 us -> 18.5 us (0.989)
  no operation moved by 1% of the time
where the time goes in v6:
time: 18.5 us; the launch traced here: 18.3 us
  starting transfers between devices  10.3 us (56%)
  Pallas kernels  4.23 us (23%)
  waiting for transfers between devices  2.27 us (12%)
  local copies, waits for them, and re-layouts  0.76 us (4%)
  between operations  0.71 us (4%)
    ppermute x8, starting transfers between devices, move(): return lax.ppermute(block, axes, pairs)  10.3 us
    ppermute x8, waiting for transfers between devices, move(): return lax.ppermute(block, axes, pairs)  2.27 us
    pallas_call x1, Pallas kernels, gather_shards(): pl.pallas_call(functools.partial(sum_kernel, cells), out_shape=(jax.Shape...  1.85 us
    pallas_call x1, Pallas kernels, gather_shards(): pl.pallas_call(functools.partial(left_kernel, n_col, n_slab), out_shape=(...  1.25 us
    pallas_call x1, Pallas kernels, gather_shards(): pl.pallas_call(pack_kernel, out_shape=(jax.ShapeDtypeStruct((packed, stat...  1.13 us
    unnamed x8, local copies, waits for them, and re-layouts  0.75 us
  transfers between devices with their start and end apart: 8, of which 3 were waited for; matrix products, arithmetic and copies ran while one was open for 0% of the time, Pallas kernels for 7%

profile of v6, /device:TPU:0, one launch (start us, length us, event | category | flops | bytes accessed | tf_op | source)
XLA Modules:
  0.0 18.3 jit_solution(17340275229491467083)
XLA Ops:
  0.6 0.0 copy-start.2
  0.6 1.1 %shard_map.95 = (bf16[432,128]{1,0:T(8,128)(2,1)S(1)}, bf16[224,128]{1,0:T(8,128)(2,1)S(1)}) custom-call(s32[128]{0:T(128)} %occ_ref.1, bf16[512,128]{1,0:T(8,128)(2,1)} %coeffs_ref.1), custom_call_target="tpu_custom_call" | custom-call | tf_op jit(solution)/shard_map/pallas_call | solution.py:322
  1.8 0.0 copy-start
  1.8 4.1 %collective-permute-start.3 = (bf16[224,128]{1,0:T(8,128)(2,1)S(1)}, bf16[224,128]{1,0:T(8,128)(2,1)S(1)}, u32[]{:S(2)}, u32[]{:S(2)}) collective-permute-start(bf16[224,128]{1,0:T(8,128)(2,1)S(1)} %get-tuple-element.15), channel_id=1, source_target_pairs={{0,8},{1,9},{2,26},{3,27},{4,12},{5,13},{6,30},{7,31},{8,0},{9,1},... | collective-permute-start | bytes 172040 | tf_op jit(solution)/shard_map/ppermute | solution.py:311
  5.9 1.6 %collective-permute-start.2 = (bf16[432,128]{1,0:T(8,128)(2,1)S(1)}, bf16[432,128]{1,0:T(8,128)(2,1)S(1)}, u32[]{:S(2)}, u32[]{:S(2)}) collective-permute-start(bf16[432,128]{1,0:T(8,128)(2,1)S(1)} %get-tuple-element.13.block_ref), channel_id=1, source_target_pairs={{0,4},{1,21},{2,6},{3,23},{4,0},{5,17},{6,2},{7,19},{8,12},{9,29},... | collective-permute-start | bytes 331784 | tf_op jit(solution)/shard_map/ppermute | solution.py:311
  7.5 0.0 collective-permute-start.1
  7.5 1.7 %collective-permute-start = (bf16[432,128]{1,0:T(8,128)(2,1)S(1)}, bf16[432,128]{1,0:T(8,128)(2,1)S(1)}, u32[]{:S(2)}, u32[]{:S(2)}) collective-permute-start(bf16[432,128]{1,0:T(8,128)(2,1)S(1)} %get-tuple-element.13.block_ref), channel_id=1, source_target_pairs={{0,16},{1,17},{2,18},{3,19},{4,20},{5,21},{6,22},{7,23},{8,24},{9,... | collective-permute-start | bytes 331784 | tf_op jit(solution)/shard_map/ppermute | solution.py:311
  9.2 0.0 collective-permute-done.3
  9.2 0.0 copy-done.2
  9.2 2.3 %collective-permute-start.4 = (bf16[352,128]{1,0:T(8,128)(2,1)S(1)}, bf16[352,128]{1,0:T(8,128)(2,1)S(1)}, u32[]{:S(2)}, u32[]{:S(2)}) collective-permute-start(bf16[352,128]{1,0:T(8,128)(2,1)S(1)} %pad_maximum_fusion.1), channel_id=1, source_target_pairs={{0,2},{1,3},{2,0},{3,1},{4,6},{5,7},{6,4},{7,5},{8,10},{9,11},{10,... | collective-permute-start | bytes 270344 | tf_op jit(solution)/shard_map/ppermute | solution.py:311
  11.5 0.0 copy-done.3
  11.5 0.7 %copy-done.1 = bf16[128,128]{1,0:T(8,128)(2,1)S(1)} copy-done((bf16[128,128]{1,0:T(8,128)(2,1)S(1)}, bf16[128,128]{1,0:T(8,128)(2,1)}, u32[]{:S(2)}) %copy-start.1) | copy-done | bytes 32792
  12.2 1.2 %shard_map.96 = (bf16[2,384,432]{2,1,0:T(8,128)(2,1)S(1)}, bf16[512,432]{1,0:T(8,128)(2,1)S(1)}) custom-call(s32[8,32]{1,0:T(8,128)} %bitcast.11, s32[64]{0:T(128)} %counts_hbm.1, bf16[128,128]{1,0:T(8,128)(2,1)S(1)} %copy-done.1, bf16[128,512]{1,0:T(8,128)(2,1)S(1)} %copy-done, bf16[128,16]{1,0:T(8,128)(2,1)S(1)} %bitcast.7), custom_call_target="tpu_custom_call" | custom-call | flops 200000000 | bytes 2000000 | tf_op jit(solution)/shard_map/pallas_call | solution.py:344
  13.5 0.0 collective-permute-done.2.a_ref
  13.5 1.0 %collective-permute-done.1.c_ref = bf16[432,128]{1,0:T(8,128)(2,1)S(1)} collective-permute-done((bf16[432,128]{1,0:T(8,128)(2,1)S(1)}, bf16[432,128]{1,0:T(8,128)(2,1)S(1)}, u32[]{:S(2)}, u32[]{:S(2)}) %collective-permute-start.1) | collective-permute-done | bytes 110624 | tf_op jit(solution)/shard_map/ppermute | solution.py:311
  14.5 0.0 collective-permute-done.other_ref
  14.5 0.0 collective-permute-done.4
  14.5 0.1 collective-permute-start.5
  14.6 0.5 %collective-permute-start.6 = (bf16[432,128]{1,0:T(8,128)(2,1)S(1)}, bf16[432,128]{1,0:T(8,128)(2,1)S(1)}, u32[]{:S(2)}, u32[]{:S(2)}) collective-permute-start(bf16[432,128]{1,0:T(8,128)(2,1)S(1)} %collective-permute-done.2.a_ref), channel_id=1, source_target_pairs={{0,1},{1,0},{2,3},{3,2},{4,5},{5,4},{6,7},{7,6},{8,9},{9,8},{10,11... | collective-permute-start | bytes 331784 | tf_op jit(solution)/shard_map/ppermute | solution.py:311
  15.1 0.1 collective-permute-start.7
  15.2 1.0 %collective-permute-done.6.b_ref = bf16[432,128]{1,0:T(8,128)(2,1)S(1)} collective-permute-done((bf16[432,128]{1,0:T(8,128)(2,1)S(1)}, bf16[432,128]{1,0:T(8,128)(2,1)S(1)}, u32[]{:S(2)}, u32[]{:S(2)}) %collective-permute-start.6) | collective-permute-done | bytes 110624 | tf_op jit(solution)/shard_map/ppermute | solution.py:311
  16.2 0.3 %collective-permute-done.7.d_ref = bf16[432,128]{1,0:T(8,128)(2,1)S(1)} collective-permute-done((bf16[432,128]{1,0:T(8,128)(2,1)S(1)}, bf16[432,128]{1,0:T(8,128)(2,1)S(1)}, u32[]{:S(2)}, u32[]{:S(2)}) %collective-permute-start.7) | collective-permute-done | bytes 110624 | tf_op jit(solution)/shard_map/ppermute | solution.py:311
  16.4 0.0 collective-permute-done.5.next_ref
  16.4 1.8 %shard_map.97 = (f32[1,128]{1,0:T(1,128)}, f32[8,256]{1,0:T(8,128)}) custom-call(bf16[2,384,432]{2,1,0:T(8,128)(2,1)S(1)} %get-tuple-element.16.left_ref, bf16[512,432]{1,0:T(8,128)(2,1)S(1)} %get-tuple-element.17.columns_ref, bf16[432,128]{1,0:T(8,128)(2,1)S(1)} %get-tuple-element.13.block_ref, bf16[432,128]{1,0:T(8,128)(2,1)S(1)} %collective-permute-done.other_ref, ...), custom_call_target="tpu_custom_call" | custom-call | tf_op jit(solution)/shard_map/pallas_call | solution.py:373
  (6 shorter events, 0.0 us)
Async XLA Ops:
  0.6 8.6 %copy-start.2 = (bf16[8,16,128]{2,1,0:T(8,128)(2,1)S(1)}, bf16[8,16,128]{2,1,0:T(8,128)(2,1)}, u32[]{:S(2)}) copy-start(bf16[8,16,128]{2,1,0:T(8,128)(2,1)} %param.15) | copy-start | bytes 98308
  1.8 9.7 %copy-start = (bf16[128,512]{1,0:T(8,128)(2,1)S(1)}, bf16[128,512]{1,0:T(8,128)(2,1)}, u32[]{:S(2)}) copy-start(bf16[128,512]{1,0:T(8,128)(2,1)} %panel_ref.1) | copy-start | bytes 393220
  1.8 7.4 %collective-permute-start.3 = (bf16[224,128]{1,0:T(8,128)(2,1)S(1)}, bf16[224,128]{1,0:T(8,128)(2,1)S(1)}, u32[]{:S(2)}, u32[]{:S(2)}) collective-permute-start(bf16[224,128]{1,0:T(8,128)(2,1)S(1)} %get-tuple-element.15), channel_id=1, source_target_pairs={{0,8},{1,9},{2,26},{3,27},{4,12},{5,13},{6,30},{7,31},{8,0},{9,1},... | collective-permute-start | bytes 172040 | tf_op jit(solution)/shard_map/ppermute | solution.py:311
  5.9 7.6 %collective-permute-start.2 = (bf16[432,128]{1,0:T(8,128)(2,1)S(1)}, bf16[432,128]{1,0:T(8,128)(2,1)S(1)}, u32[]{:S(2)}, u32[]{:S(2)}) collective-permute-start(bf16[432,128]{1,0:T(8,128)(2,1)S(1)} %get-tuple-element.13.block_ref), channel_id=1, source_target_pairs={{0,4},{1,21},{2,6},{3,23},{4,0},{5,17},{6,2},{7,19},{8,12},{9,29},... | collective-permute-start | bytes 331784 | tf_op jit(solution)/shard_map/ppermute | solution.py:311
  7.5 7.0 %collective-permute-start.1 = (bf16[432,128]{1,0:T(8,128)(2,1)S(1)}, bf16[432,128]{1,0:T(8,128)(2,1)S(1)}, u32[]{:S(2)}, u32[]{:S(2)}) collective-permute-start(bf16[432,128]{1,0:T(8,128)(2,1)S(1)} %get-tuple-element.13.block_ref), channel_id=1, source_target_pairs={{0,12},{1,29},{2,14},{3,31},{4,8},{5,25},{6,10},{7,27},{8,4},{9,21... | collective-permute-start | bytes 331784 | tf_op jit(solution)/shard_map/ppermute | solution.py:311
  7.5 7.0 %collective-permute-start = (bf16[432,128]{1,0:T(8,128)(2,1)S(1)}, bf16[432,128]{1,0:T(8,128)(2,1)S(1)}, u32[]{:S(2)}, u32[]{:S(2)}) collective-permute-start(bf16[432,128]{1,0:T(8,128)(2,1)S(1)} %get-tuple-element.13.block_ref), channel_id=1, source_target_pairs={{0,16},{1,17},{2,18},{3,19},{4,20},{5,21},{6,22},{7,23},{8,24},{9,... | collective-permute-start | bytes 331784 | tf_op jit(solution)/shard_map/ppermute | solution.py:311
  9.2 2.3 %copy-start.3 = (bf16[8,16,16]{2,1,0:T(8,128)(2,1)S(1)}, bf16[8,16,16]{2,1,0:T(8,128)(2,1)}, u32[]{:S(2)}) copy-start(bf16[8,16,16]{2,1,0:T(8,128)(2,1)} %param.14) | copy-start | bytes 12292
  9.2 5.3 %collective-permute-start.4 = (bf16[352,128]{1,0:T(8,128)(2,1)S(1)}, bf16[352,128]{1,0:T(8,128)(2,1)S(1)}, u32[]{:S(2)}, u32[]{:S(2)}) collective-permute-start(bf16[352,128]{1,0:T(8,128)(2,1)S(1)} %pad_maximum_fusion.1), channel_id=1, source_target_pairs={{0,2},{1,3},{2,0},{3,1},{4,6},{5,7},{6,4},{7,5},{8,10},{9,11},{10,... | collective-permute-start | bytes 270344 | tf_op jit(solution)/shard_map/ppermute | solution.py:311
  11.5 0.8 %copy-start.1 = (bf16[128,128]{1,0:T(8,128)(2,1)S(1)}, bf16[128,128]{1,0:T(8,128)(2,1)}, u32[]{:S(2)}) copy-start(bf16[128,128]{1,0:T(8,128)(2,1)} %phi_ref.1) | copy-start | bytes 98308
  14.5 1.9 %collective-permute-start.5 = (bf16[704,128]{1,0:T(8,128)(2,1)S(1)}, bf16[704,128]{1,0:T(8,128)(2,1)S(1)}, u32[]{:S(2)}, u32[]{:S(2)}) collective-permute-start(bf16[704,128]{1,0:T(8,128)(2,1)S(1)} %pad_maximum_fusion.here_ref), channel_id=1, source_target_pairs={{0,1},{1,0},{2,3},{3,2},{4,5},{5,4},{6,7},{7,6},{8,9},{9,8},{10,11... | collective-permute-start | bytes 540680 | tf_op jit(solution)/shard_map/ppermute | solution.py:311
  14.6 1.6 %collective-permute-start.6 = (bf16[432,128]{1,0:T(8,128)(2,1)S(1)}, bf16[432,128]{1,0:T(8,128)(2,1)S(1)}, u32[]{:S(2)}, u32[]{:S(2)}) collective-permute-start(bf16[432,128]{1,0:T(8,128)(2,1)S(1)} %collective-permute-done.2.a_ref), channel_id=1, source_target_pairs={{0,1},{1,0},{2,3},{3,2},{4,5},{5,4},{6,7},{7,6},{8,9},{9,8},{10,11... | collective-permute-start | bytes 331784 | tf_op jit(solution)/shard_map/ppermute | solution.py:311
  15.1 1.3 %collective-permute-start.7 = (bf16[432,128]{1,0:T(8,128)(2,1)S(1)}, bf16[432,128]{1,0:T(8,128)(2,1)S(1)}, u32[]{:S(2)}, u32[]{:S(2)}) collective-permute-start(bf16[432,128]{1,0:T(8,128)(2,1)S(1)} %collective-permute-done.1.c_ref), channel_id=1, source_target_pairs={{0,1},{1,0},{2,3},{3,2},{4,5},{5,4},{6,7},{7,6},{8,9},{9,8},{10,11... | collective-permute-start | bytes 331784 | tf_op jit(solution)/shard_map/ppermute | solution.py:311

commit v7 on v6

--- a/solution.py
+++ b/solution.py
@@ -226,13 +226,15 @@
 
 def partial_sums(a, b, near, cells, left_ref, proj):
     weight_row = left_ref.shape[2] - 16
-    r = jnp.dot(left_ref[near], a, preferred_element_type=F32)
-    r += jnp.dot(left_ref[1 - near], b, preferred_element_type=F32)
-    right = jnp.dot(proj, jnp.where(near == 0, a, b), preferred_element_type=F32)
+    panel, rest = jnp.where(near == 0, a, b), jnp.where(near == 0, b, a)
+    r = jnp.dot(left_ref[0], panel, preferred_element_type=F32)
+    right = jnp.dot(proj, panel, preferred_element_type=F32)
+    listed = r[:cells] + jnp.dot(left_ref[1, :cells], rest, preferred_element_type=F32)
+    atoms = r[2 * cells :] + jnp.dot(left_ref[1, 2 * cells :], rest, preferred_element_type=F32)
     f = a[weight_row:, :].astype(F32)[0:1]
-    term = r[:cells] * f * r[cells : 2 * cells]
+    term = listed * f * r[cells : 2 * cells]
     term = sum(term[:, at : at + cells] for at in range(0, term.shape[1], cells))
-    high, low = split(r[2 * cells :] * f)
+    high, low = split(atoms * f)
     right_high, right_low = split(right)
     rho = sum(
         lax.dot_general(one, two, (((1,), (1,)), ((), ())), preferred_element_type=F32)

time: 18.5 us -> 18.4 us (level)
  no operation moved by 1% of the time
where the time goes in v7:
time: 18.4 us; the launch traced here: 18.2 us
  starting transfers between devices  10.3 us (56%)
  Pallas kernels  4.13 us (22%)
  waiting for transfers between devices  2.27 us (12%)
  local copies, waits for them, and re-layouts  0.76 us (4%)
  between operations  0.71 us (4%)
    ppermute x8, starting transfers between devices, move(): return lax.ppermute(block, axes, pairs)  10.3 us
    ppermute x8, waiting for transfers between devices, move(): return lax.ppermute(block, axes, pairs)  2.27 us
    pallas_call x1, Pallas kernels, gather_shards(): pl.pallas_call(functools.partial(sum_kernel, cells), out_shape=(jax.Shape...  1.75 us
    pallas_call x1, Pallas kernels, gather_shards(): pl.pallas_call(functools.partial(left_kernel, n_col, n_slab), out_shape=(...  1.25 us
    pallas_call x1, Pallas kernels, gather_shards(): pl.pallas_call(pack_kernel, out_shape=(jax.ShapeDtypeStruct((packed, stat...  1.13 us
    unnamed x8, local copies, waits for them, and re-layouts  0.75 us
  transfers between devices with their start and end apart: 8, of which 3 were waited for; matrix products, arithmetic and copies ran while one was open for 0% of the time, Pallas kernels for 7%

profile of v7, /device:TPU:0, one launch (start us, length us, event | category | flops | bytes accessed | tf_op | source)
XLA Modules:
  0.0 18.2 jit_solution(14002980002570072853)
XLA Ops:
  0.6 0.0 copy-start.2
  0.6 1.1 %shard_map.95 = (bf16[432,128]{1,0:T(8,128)(2,1)S(1)}, bf16[224,128]{1,0:T(8,128)(2,1)S(1)}) custom-call(s32[128]{0:T(128)} %occ_ref.1, bf16[512,128]{1,0:T(8,128)(2,1)} %coeffs_ref.1), custom_call_target="tpu_custom_call" | custom-call | tf_op jit(solution)/shard_map/pallas_call | solution.py:324
  1.8 0.0 copy-start
  1.8 4.1 %collective-permute-start.3 = (bf16[224,128]{1,0:T(8,128)(2,1)S(1)}, bf16[224,128]{1,0:T(8,128)(2,1)S(1)}, u32[]{:S(2)}, u32[]{:S(2)}) collective-permute-start(bf16[224,128]{1,0:T(8,128)(2,1)S(1)} %get-tuple-element.15), channel_id=1, source_target_pairs={{0,8},{1,9},{2,26},{3,27},{4,12},{5,13},{6,30},{7,31},{8,0},{9,1},... | collective-permute-start | bytes 172040 | tf_op jit(solution)/shard_map/ppermute | solution.py:313
  5.9 1.6 %collective-permute-start.2 = (bf16[432,128]{1,0:T(8,128)(2,1)S(1)}, bf16[432,128]{1,0:T(8,128)(2,1)S(1)}, u32[]{:S(2)}, u32[]{:S(2)}) collective-permute-start(bf16[432,128]{1,0:T(8,128)(2,1)S(1)} %get-tuple-element.13.block_ref), channel_id=1, source_target_pairs={{0,4},{1,21},{2,6},{3,23},{4,0},{5,17},{6,2},{7,19},{8,12},{9,29},... | collective-permute-start | bytes 331784 | tf_op jit(solution)/shard_map/ppermute | solution.py:313
  7.5 0.0 collective-permute-start.1
  7.5 1.7 %collective-permute-start = (bf16[432,128]{1,0:T(8,128)(2,1)S(1)}, bf16[432,128]{1,0:T(8,128)(2,1)S(1)}, u32[]{:S(2)}, u32[]{:S(2)}) collective-permute-start(bf16[432,128]{1,0:T(8,128)(2,1)S(1)} %get-tuple-element.13.block_ref), channel_id=1, source_target_pairs={{0,16},{1,17},{2,18},{3,19},{4,20},{5,21},{6,22},{7,23},{8,24},{9,... | collective-permute-start | bytes 331784 | tf_op jit(solution)/shard_map/ppermute | solution.py:313
  9.2 0.0 collective-permute-done.3
  9.2 0.0 copy-done.2
  9.2 2.3 %collective-permute-start.4 = (bf16[352,128]{1,0:T(8,128)(2,1)S(1)}, bf16[352,128]{1,0:T(8,128)(2,1)S(1)}, u32[]{:S(2)}, u32[]{:S(2)}) collective-permute-start(bf16[352,128]{1,0:T(8,128)(2,1)S(1)} %pad_maximum_fusion.1), channel_id=1, source_target_pairs={{0,2},{1,3},{2,0},{3,1},{4,6},{5,7},{6,4},{7,5},{8,10},{9,11},{10,... | collective-permute-start | bytes 270344 | tf_op jit(solution)/shard_map/ppermute | solution.py:313
  11.5 0.0 copy-done
  11.5 0.7 %copy-done.1 = bf16[128,128]{1,0:T(8,128)(2,1)S(1)} copy-done((bf16[128,128]{1,0:T(8,128)(2,1)S(1)}, bf16[128,128]{1,0:T(8,128)(2,1)}, u32[]{:S(2)}) %copy-start.1) | copy-done | bytes 32792
  12.2 1.2 %shard_map.96 = (bf16[2,384,432]{2,1,0:T(8,128)(2,1)S(1)}, bf16[512,432]{1,0:T(8,128)(2,1)S(1)}) custom-call(s32[8,32]{1,0:T(8,128)} %bitcast.11, s32[64]{0:T(128)} %counts_hbm.1, bf16[128,128]{1,0:T(8,128)(2,1)S(1)} %copy-done.1, bf16[128,512]{1,0:T(8,128)(2,1)S(1)} %copy-done, bf16[128,16]{1,0:T(8,128)(2,1)S(1)} %bitcast.7), custom_call_target="tpu_custom_call" | custom-call | flops 200000000 | bytes 2000000 | tf_op jit(solution)/shard_map/pallas_call | solution.py:346
  13.5 0.0 collective-permute-done.2.a_ref
  13.5 1.0 %collective-permute-done.1.c_ref = bf16[432,128]{1,0:T(8,128)(2,1)S(1)} collective-permute-done((bf16[432,128]{1,0:T(8,128)(2,1)S(1)}, bf16[432,128]{1,0:T(8,128)(2,1)S(1)}, u32[]{:S(2)}, u32[]{:S(2)}) %collective-permute-start.1) | collective-permute-done | bytes 110624 | tf_op jit(solution)/shard_map/ppermute | solution.py:313
  14.5 0.0 collective-permute-done.other_ref
  14.5 0.0 collective-permute-done.4
  14.5 0.1 collective-permute-start.5
  14.6 0.5 %collective-permute-start.6 = (bf16[432,128]{1,0:T(8,128)(2,1)S(1)}, bf16[432,128]{1,0:T(8,128)(2,1)S(1)}, u32[]{:S(2)}, u32[]{:S(2)}) collective-permute-start(bf16[432,128]{1,0:T(8,128)(2,1)S(1)} %collective-permute-done.2.a_ref), channel_id=1, source_target_pairs={{0,1},{1,0},{2,3},{3,2},{4,5},{5,4},{6,7},{7,6},{8,9},{9,8},{10,11... | collective-permute-start | bytes 331784 | tf_op jit(solution)/shard_map/ppermute | solution.py:313
  15.1 0.1 collective-permute-start.7
  15.2 1.0 %collective-permute-done.6.b_ref = bf16[432,128]{1,0:T(8,128)(2,1)S(1)} collective-permute-done((bf16[432,128]{1,0:T(8,128)(2,1)S(1)}, bf16[432,128]{1,0:T(8,128)(2,1)S(1)}, u32[]{:S(2)}, u32[]{:S(2)}) %collective-permute-start.6) | collective-permute-done | bytes 110624 | tf_op jit(solution)/shard_map/ppermute | solution.py:313
  16.2 0.3 %collective-permute-done.7.d_ref = bf16[432,128]{1,0:T(8,128)(2,1)S(1)} collective-permute-done((bf16[432,128]{1,0:T(8,128)(2,1)S(1)}, bf16[432,128]{1,0:T(8,128)(2,1)S(1)}, u32[]{:S(2)}, u32[]{:S(2)}) %collective-permute-start.7) | collective-permute-done | bytes 110624 | tf_op jit(solution)/shard_map/ppermute | solution.py:313
  16.4 0.0 collective-permute-done.5.next_ref
  16.4 1.8 %shard_map.97 = (f32[1,128]{1,0:T(1,128)}, f32[8,256]{1,0:T(8,128)}) custom-call(bf16[2,384,432]{2,1,0:T(8,128)(2,1)S(1)} %get-tuple-element.16.left_ref, bf16[512,432]{1,0:T(8,128)(2,1)S(1)} %get-tuple-element.17.columns_ref, bf16[432,128]{1,0:T(8,128)(2,1)S(1)} %get-tuple-element.13.block_ref, bf16[432,128]{1,0:T(8,128)(2,1)S(1)} %collective-permute-done.other_ref, ...), custom_call_target="tpu_custom_call" | custom-call | tf_op jit(solution)/shard_map/pallas_call | solution.py:375
  (6 shorter events, 0.0 us)
Async XLA Ops:
  0.6 8.6 %copy-start.2 = (bf16[8,16,128]{2,1,0:T(8,128)(2,1)S(1)}, bf16[8,16,128]{2,1,0:T(8,128)(2,1)}, u32[]{:S(2)}) copy-start(bf16[8,16,128]{2,1,0:T(8,128)(2,1)} %param.15) | copy-start | bytes 98308
  1.8 9.7 %copy-start = (bf16[128,512]{1,0:T(8,128)(2,1)S(1)}, bf16[128,512]{1,0:T(8,128)(2,1)}, u32[]{:S(2)}) copy-start(bf16[128,512]{1,0:T(8,128)(2,1)} %panel_ref.1) | copy-start | bytes 393220
  1.8 7.4 %collective-permute-start.3 = (bf16[224,128]{1,0:T(8,128)(2,1)S(1)}, bf16[224,128]{1,0:T(8,128)(2,1)S(1)}, u32[]{:S(2)}, u32[]{:S(2)}) collective-permute-start(bf16[224,128]{1,0:T(8,128)(2,1)S(1)} %get-tuple-element.15), channel_id=1, source_target_pairs={{0,8},{1,9},{2,26},{3,27},{4,12},{5,13},{6,30},{7,31},{8,0},{9,1},... | collective-permute-start | bytes 172040 | tf_op jit(solution)/shard_map/ppermute | solution.py:313
  5.9 7.6 %collective-permute-start.2 = (bf16[432,128]{1,0:T(8,128)(2,1)S(1)}, bf16[432,128]{1,0:T(8,128)(2,1)S(1)}, u32[]{:S(2)}, u32[]{:S(2)}) collective-permute-start(bf16[432,128]{1,0:T(8,128)(2,1)S(1)} %get-tuple-element.13.block_ref), channel_id=1, source_target_pairs={{0,4},{1,21},{2,6},{3,23},{4,0},{5,17},{6,2},{7,19},{8,12},{9,29},... | collective-permute-start | bytes 331784 | tf_op jit(solution)/shard_map/ppermute | solution.py:313
  7.5 7.0 %collective-permute-start.1 = (bf16[432,128]{1,0:T(8,128)(2,1)S(1)}, bf16[432,128]{1,0:T(8,128)(2,1)S(1)}, u32[]{:S(2)}, u32[]{:S(2)}) collective-permute-start(bf16[432,128]{1,0:T(8,128)(2,1)S(1)} %get-tuple-element.13.block_ref), channel_id=1, source_target_pairs={{0,12},{1,29},{2,14},{3,31},{4,8},{5,25},{6,10},{7,27},{8,4},{9,21... | collective-permute-start | bytes 331784 | tf_op jit(solution)/shard_map/ppermute | solution.py:313
  7.5 7.0 %collective-permute-start = (bf16[432,128]{1,0:T(8,128)(2,1)S(1)}, bf16[432,128]{1,0:T(8,128)(2,1)S(1)}, u32[]{:S(2)}, u32[]{:S(2)}) collective-permute-start(bf16[432,128]{1,0:T(8,128)(2,1)S(1)} %get-tuple-element.13.block_ref), channel_id=1, source_target_pairs={{0,16},{1,17},{2,18},{3,19},{4,20},{5,21},{6,22},{7,23},{8,24},{9,... | collective-permute-start | bytes 331784 | tf_op jit(solution)/shard_map/ppermute | solution.py:313
  9.2 2.3 %copy-start.3 = (bf16[8,16,16]{2,1,0:T(8,128)(2,1)S(1)}, bf16[8,16,16]{2,1,0:T(8,128)(2,1)}, u32[]{:S(2)}) copy-start(bf16[8,16,16]{2,1,0:T(8,128)(2,1)} %param.14) | copy-start | bytes 12292
  9.2 5.3 %collective-permute-start.4 = (bf16[352,128]{1,0:T(8,128)(2,1)S(1)}, bf16[352,128]{1,0:T(8,128)(2,1)S(1)}, u32[]{:S(2)}, u32[]{:S(2)}) collective-permute-start(bf16[352,128]{1,0:T(8,128)(2,1)S(1)} %pad_maximum_fusion.1), channel_id=1, source_target_pairs={{0,2},{1,3},{2,0},{3,1},{4,6},{5,7},{6,4},{7,5},{8,10},{9,11},{10,... | collective-permute-start | bytes 270344 | tf_op jit(solution)/shard_map/ppermute | solution.py:313
  11.5 0.8 %copy-start.1 = (bf16[128,128]{1,0:T(8,128)(2,1)S(1)}, bf16[128,128]{1,0:T(8,128)(2,1)}, u32[]{:S(2)}) copy-start(bf16[128,128]{1,0:T(8,128)(2,1)} %phi_ref.1) | copy-start | bytes 98308
  14.5 1.9 %collective-permute-start.5 = (bf16[704,128]{1,0:T(8,128)(2,1)S(1)}, bf16[704,128]{1,0:T(8,128)(2,1)S(1)}, u32[]{:S(2)}, u32[]{:S(2)}) collective-permute-start(bf16[704,128]{1,0:T(8,128)(2,1)S(1)} %pad_maximum_fusion.here_ref), channel_id=1, source_target_pairs={{0,1},{1,0},{2,3},{3,2},{4,5},{5,4},{6,7},{7,6},{8,9},{9,8},{10,11... | collective-permute-start | bytes 540680 | tf_op jit(solution)/shard_map/ppermute | solution.py:313
  14.6 1.6 %collective-permute-start.6 = (bf16[432,128]{1,0:T(8,128)(2,1)S(1)}, bf16[432,128]{1,0:T(8,128)(2,1)S(1)}, u32[]{:S(2)}, u32[]{:S(2)}) collective-permute-start(bf16[432,128]{1,0:T(8,128)(2,1)S(1)} %collective-permute-done.2.a_ref), channel_id=1, source_target_pairs={{0,1},{1,0},{2,3},{3,2},{4,5},{5,4},{6,7},{7,6},{8,9},{9,8},{10,11... | collective-permute-start | bytes 331784 | tf_op jit(solution)/shard_map/ppermute | solution.py:313
  15.1 1.3 %collective-permute-start.7 = (bf16[432,128]{1,0:T(8,128)(2,1)S(1)}, bf16[432,128]{1,0:T(8,128)(2,1)S(1)}, u32[]{:S(2)}, u32[]{:S(2)}) collective-permute-start(bf16[432,128]{1,0:T(8,128)(2,1)S(1)} %collective-permute-done.1.c_ref), channel_id=1, source_target_pairs={{0,1},{1,0},{2,3},{3,2},{4,5},{5,4},{6,7},{7,6},{8,9},{9,8},{10,11... | collective-permute-start | bytes 331784 | tf_op jit(solution)/shard_map/ppermute | solution.py:313

commit v8 on v6

--- a/solution.py
+++ b/solution.py
@@ -224,11 +224,11 @@
     return high, (values - high.astype(F32)).astype(BF16)
 
 
-def partial_sums(a, b, near, cells, left_ref, proj):
+def partial_sums(a, b, near, cells, left_ref, proj_ref):
     weight_row = left_ref.shape[2] - 16
     r = jnp.dot(left_ref[near], a, preferred_element_type=F32)
     r += jnp.dot(left_ref[1 - near], b, preferred_element_type=F32)
-    right = jnp.dot(proj, jnp.where(near == 0, a, b), preferred_element_type=F32)
+    right = jnp.dot(proj_ref[...], jnp.where(near == 0, a, b), preferred_element_type=F32)
     f = a[weight_row:, :].astype(F32)[0:1]
     term = r[:cells] * f * r[cells : 2 * cells]
     term = sum(term[:, at : at + cells] for at in range(0, term.shape[1], cells))
@@ -241,20 +241,8 @@
     return term, rho
 
 
-def sum_kernel(
-    cells,
-    left_ref,
-    columns_ref,
-    block_ref,
-    other_ref,
-    here_ref,
-    next_ref,
-    a_ref,
-    b_ref,
-    c_ref,
-    d_ref,
-    density_ref,
-    rho_ref,
+def early_kernel(
+    cells, left_ref, columns_ref, a_ref, b_ref, here_ref, next_ref, term_ref, rho_ref, proj_ref
 ):
     x, s = lax.axis_index("prow"), lax.axis_index("dz")
     odd, back = (s & 1) == 1, (s & 2) == 2
@@ -267,21 +255,25 @@
         return jnp.concatenate([evens[at : at + half], odds[at : at + size]], axis=0)
 
     one, two = joined(0), joined(size)
-    fetched = jnp.concatenate([a_ref[...], c_ref[...]], axis=1)
-    swapped = jnp.concatenate([b_ref[...], d_ref[...]], axis=1)
-    near = jnp.concatenate(
-        [block_ref[...], jnp.where(back, two, one), jnp.where(odd, swapped, fetched)], axis=1
-    )
-    far = jnp.concatenate(
-        [other_ref[...], jnp.where(back, one, two), jnp.where(odd, fetched, swapped)], axis=1
-    )
-    own = left_ref.shape[1] - 2 * cells
-    last, first = 2 * size, 2 * size + own
-    front = [jnp.where(back, part[last:first], part[first:]) for part in (evens, odds)]
-    rear = [jnp.where(back, part[first:], part[last:first]) for part in (evens, odds)]
-    proj = take(jnp.concatenate(front + rear, axis=1), columns_ref[...])
-    term, rho = partial_sums(near, far, x, cells, left_ref, proj)
+    a = jnp.concatenate([a_ref[...], jnp.where(back, two, one)], axis=1)
+    b = jnp.concatenate([b_ref[...], jnp.where(back, one, two)], axis=1)
+    own = proj_ref.shape[0]
+    far, near = 2 * size, 2 * size + own
+    front = [jnp.where(back, part[far:near], part[near:]) for part in (evens, odds)]
+    rear = [jnp.where(back, part[near:], part[far:near]) for part in (evens, odds)]
+    proj_ref[...] = take(jnp.concatenate(front + rear, axis=1), columns_ref[...])
+    term_ref[...], rho_ref[...] = partial_sums(a, b, x, cells, left_ref, proj_ref)
+
+
+def late_kernel(cells, left_ref, proj_ref, a_ref, b_ref, c_ref, d_ref, term_ref, part_ref, density_ref, rho_ref):
+    near = lax.axis_index("prow") ^ (lax.axis_index("dz") & 1)
+    a = jnp.concatenate([a_ref[...], c_ref[...]], axis=1)
+    b = jnp.concatenate([b_ref[...], d_ref[...]], axis=1)
+    term, rho = partial_sums(a, b, near, cells, left_ref, proj_ref)
+    term += term_ref[...]
+    rho += part_ref[...]
     density_ref[...] = jnp.sum(term.T, axis=0, keepdims=True)
+    own = proj_ref.shape[0]
     atoms = own // NPROJ
     rho = jnp.where((iota((own, own), 0) & (atoms - 1)) == (iota((own, own), 1) >> 4), rho, 0.0)
     wide = NPROJ * NPROJ
@@ -292,6 +284,7 @@
 
 
 VMEM = pl.BlockSpec(memory_space=pltpu.VMEM)
+SMEM = pl.BlockSpec(memory_space=pltpu.SMEM)
 HBM = pl.BlockSpec(memory_space=pltpu.HBM)
 PARAMS = pltpu.CompilerParams(vmem_limit_bytes=32 * 2**20)
 
@@ -365,21 +358,32 @@
     )
     projectors = proj_panel.reshape(own, -1)
     far = move(jnp.concatenate([part, projectors], axis=0), lambda x, z, s: (x, z, s ^ 2))
-    other, got[3], got[1], left, far = lax.optimization_barrier((other, got[3], got[1], left, far))
+    got[1], got[3], other, left, far = lax.optimization_barrier((got[1], got[3], other, left, far))
     here = jnp.concatenate([part, far, projectors], axis=0)
     after = swap(here)
     swapped = {1: swap(got[1])}
+    term, rho, proj = pl.pallas_call(
+        functools.partial(early_kernel, cells),
+        out_shape=(
+            jax.ShapeDtypeStruct((cells, states), F32),
+            jax.ShapeDtypeStruct((own, own), F32),
+            jax.ShapeDtypeStruct((own, packed), BF16),
+        ),
+        in_specs=[VMEM] * 6,
+        out_specs=(VMEM, VMEM, VMEM),
+        compiler_params=PARAMS,
+    )(left, columns, block, other, here, after)
     swapped[3] = swap(got[3])
     density, rho = pl.pallas_call(
-        functools.partial(sum_kernel, cells),
+        functools.partial(late_kernel, cells),
         out_shape=(
             jax.ShapeDtypeStruct((1, cells), F32),
             jax.ShapeDtypeStruct((atoms_own, NPROJ * NPROJ), F32),
         ),
-        in_specs=[VMEM] * 10,
+        in_specs=[VMEM] * 8,
         out_specs=(VMEM, VMEM),
         compiler_params=PARAMS,
-    )(left, columns, block, other, here, after, got[1], swapped[1], got[3], swapped[3])
+    )(left, proj, got[1], swapped[1], got[3], swapped[3], term, rho)
     return density.reshape(cells), rho
 
 
@@ -387,7 +391,7 @@
     n_row, n_col, n_slab = (lax.axis_size(a) for a in ("prow", "pcol", "dz"))
     rows = coeffs.shape[0]
     fits = coeffs.size * 2 * n_row * n_col <= GATHER_LIMIT
-    regular = n_row == 2 and n_col == 4 and n_slab == 4 and rows >= PW and rows % 512 == 0
+    regular = n_row == 2 and n_col == 4 and n_slab == 4 and rows >= PW and rows % 256 == 0
     plan = gather_shards if fits and regular else exchange_shards
     return plan(coeffs, occupations, counts, intersection, phi_values, panel_values, proj_site, proj_panel)
 

time: 18.5 us -> 18.5 us (level)
  waiting for transfers between devices: 2.27 us -> 1.86 us
  Pallas kernels: 4.23 us -> 4.55 us
    ppermute x8, waiting for transfers between devices: 2.27 us -> 1.86 us  [move(): return lax.ppermute(block, axes, pairs)]
    pallas_call x1 -> x2, Pallas kernels: 1.85 us -> 2.17 us  [the longest x1 1.44 us: gather_shards(): pl.pallas_call(functools.partial(late_kernel, cells), out_shape=(jax.Shap...]
  transfers between devices with their start and end apart: 8 -> 8, of which waited for: 3 -> 2; matrix products, arithmetic and copies ran while one was open for 0% -> 0% of each run, Pallas kernels for 7% -> 11%
where the time goes in v8:
time: 18.5 us; the launch traced here: 18.2 us
  starting transfers between devices  10.3 us (56%)
  Pallas kernels  4.55 us (25%)
  waiting for transfers between devices  1.86 us (10%)
  local copies, waits for them, and re-layouts  0.76 us (4%)
  between operations  0.73 us (4%)
    ppermute x8, starting transfers between devices, move(): return lax.ppermute(block, axes, pairs)  10.3 us
    ppermute x8, waiting for transfers between devices, move(): return lax.ppermute(block, axes, pairs)  1.86 us
    pallas_call x1, Pallas kernels, gather_shards(): pl.pallas_call(functools.partial(late_kernel, cells), out_shape=(jax.Shap...  1.44 us
    pallas_call x1, Pallas kernels, gather_shards(): pl.pallas_call(functools.partial(left_kernel, n_col, n_slab), out_shape=(...  1.25 us
    pallas_call x1, Pallas kernels, gather_shards(): pl.pallas_call(pack_kernel, out_shape=(jax.ShapeDtypeStruct((packed, stat...  1.13 us
    unnamed x8, local copies, waits for them, and re-layouts  0.75 us
    pallas_call x1, Pallas kernels, gather_shards(): pl.pallas_call(functools.partial(early_kernel, cells), out_shape=(jax.Sha...  0.73 us
  transfers between devices with their start and end apart: 8, of which 2 were waited for; matrix products, arithmetic and copies ran while one was open for 0% of the time, Pallas kernels for 11%

profile of v8, /device:TPU:0, one launch (start us, length us, event | category | flops | bytes accessed | tf_op | source)
XLA Modules:
  0.0 18.2 jit_solution(17213869931686854224)
XLA Ops:
  0.6 1.1 %shard_map.95 = (bf16[432,128]{1,0:T(8,128)(2,1)S(1)}, bf16[224,128]{1,0:T(8,128)(2,1)S(1)}) custom-call(s32[128]{0:T(128)} %occ_ref.1, bf16[512,128]{1,0:T(8,128)(2,1)} %coeffs_ref.1), custom_call_target="tpu_custom_call" | custom-call | tf_op jit(solution)/shard_map/pallas_call | solution.py:315
  1.8 0.0 copy-start
  1.8 4.1 %collective-permute-start.3 = (bf16[224,128]{1,0:T(8,128)(2,1)S(1)}, bf16[224,128]{1,0:T(8,128)(2,1)S(1)}, u32[]{:S(2)}, u32[]{:S(2)}) collective-permute-start(bf16[224,128]{1,0:T(8,128)(2,1)S(1)} %get-tuple-element.18), channel_id=1, source_target_pairs={{0,8},{1,9},{2,26},{3,27},{4,12},{5,13},{6,30},{7,31},{8,0},{9,1},... | collective-permute-start | bytes 172040 | tf_op jit(solution)/shard_map/ppermute | solution.py:304
  5.9 1.6 %collective-permute-start = (bf16[432,128]{1,0:T(8,128)(2,1)S(1)}, bf16[432,128]{1,0:T(8,128)(2,1)S(1)}, u32[]{:S(2)}, u32[]{:S(2)}) collective-permute-start(bf16[432,128]{1,0:T(8,128)(2,1)S(1)} %get-tuple-element.16.a_ref), channel_id=1, source_target_pairs={{0,4},{1,21},{2,6},{3,23},{4,0},{5,17},{6,2},{7,19},{8,12},{9,29},... | collective-permute-start | bytes 331784 | tf_op jit(solution)/shard_map/ppermute | solution.py:304
  7.5 0.0 collective-permute-start.1
  7.5 1.7 %collective-permute-start.2 = (bf16[432,128]{1,0:T(8,128)(2,1)S(1)}, bf16[432,128]{1,0:T(8,128)(2,1)S(1)}, u32[]{:S(2)}, u32[]{:S(2)}) collective-permute-start(bf16[432,128]{1,0:T(8,128)(2,1)S(1)} %get-tuple-element.16.a_ref), channel_id=1, source_target_pairs={{0,16},{1,17},{2,18},{3,19},{4,20},{5,21},{6,22},{7,23},{8,24},{9,... | collective-permute-start | bytes 331784 | tf_op jit(solution)/shard_map/ppermute | solution.py:304
  9.2 0.0 collective-permute-done.3
  9.2 0.0 copy-done.2
  9.2 2.3 %collective-permute-start.4 = (bf16[352,128]{1,0:T(8,128)(2,1)S(1)}, bf16[352,128]{1,0:T(8,128)(2,1)S(1)}, u32[]{:S(2)}, u32[]{:S(2)}) collective-permute-start(bf16[352,128]{1,0:T(8,128)(2,1)S(1)} %pad_maximum_fusion.1), channel_id=1, source_target_pairs={{0,2},{1,3},{2,0},{3,1},{4,6},{5,7},{6,4},{7,5},{8,10},{9,11},{10,... | collective-permute-start | bytes 270344 | tf_op jit(solution)/shard_map/ppermute | solution.py:304
  11.5 0.0 copy-done
  11.5 0.7 %copy-done.1 = bf16[128,128]{1,0:T(8,128)(2,1)S(1)} copy-done((bf16[128,128]{1,0:T(8,128)(2,1)S(1)}, bf16[128,128]{1,0:T(8,128)(2,1)}, u32[]{:S(2)}) %copy-start.1) | copy-done | bytes 32792
  12.2 1.2 %shard_map.96 = (bf16[2,384,432]{2,1,0:T(8,128)(2,1)S(1)}, bf16[512,432]{1,0:T(8,128)(2,1)S(1)}) custom-call(s32[8,32]{1,0:T(8,128)} %bitcast.11, s32[64]{0:T(128)} %counts_hbm.1, bf16[128,128]{1,0:T(8,128)(2,1)S(1)} %copy-done.1, bf16[128,512]{1,0:T(8,128)(2,1)S(1)} %copy-done, bf16[128,16]{1,0:T(8,128)(2,1)S(1)} %bitcast.7), custom_call_target="tpu_custom_call" | custom-call | flops 200000000 | bytes 2000000 | tf_op jit(solution)/shard_map/pallas_call | solution.py:337
  13.5 0.0 collective-permute-done.a_ref
  13.5 1.0 %collective-permute-done.1.c_ref = bf16[432,128]{1,0:T(8,128)(2,1)S(1)} collective-permute-done((bf16[432,128]{1,0:T(8,128)(2,1)S(1)}, bf16[432,128]{1,0:T(8,128)(2,1)S(1)}, u32[]{:S(2)}, u32[]{:S(2)}) %collective-permute-start.1) | collective-permute-done | bytes 110624 | tf_op jit(solution)/shard_map/ppermute | solution.py:304
  14.5 0.0 collective-permute-done.2.b_ref
  14.5 0.0 collective-permute-done.4
  14.5 0.1 collective-permute-start.5
  14.6 0.5 %collective-permute-start.6 = (bf16[432,128]{1,0:T(8,128)(2,1)S(1)}, bf16[432,128]{1,0:T(8,128)(2,1)S(1)}, u32[]{:S(2)}, u32[]{:S(2)}) collective-permute-start(bf16[432,128]{1,0:T(8,128)(2,1)S(1)} %collective-permute-done.a_ref), channel_id=1, source_target_pairs={{0,1},{1,0},{2,3},{3,2},{4,5},{5,4},{6,7},{7,6},{8,9},{9,8},{10,11... | collective-permute-start | bytes 331784 | tf_op jit(solution)/shard_map/ppermute | solution.py:304
  15.1 0.1 collective-permute-start.7
  15.2 0.8 %collective-permute-done.5.next_ref = bf16[704,128]{1,0:T(8,128)(2,1)S(1)} collective-permute-done((bf16[704,128]{1,0:T(8,128)(2,1)S(1)}, bf16[704,128]{1,0:T(8,128)(2,1)S(1)}, u32[]{:S(2)}, u32[]{:S(2)}) %collective-permute-start.5) | collective-permute-done | bytes 180256 | tf_op jit(solution)/shard_map/ppermute | solution.py:304
  16.0 0.7 %shard_map.97 = (f32[128,128]{1,0:T(8,128)S(1)}, f32[128,128]{1,0:T(8,128)S(1)}, bf16[128,432]{1,0:T(8,128)(2,1)S(1)}) custom-call(bf16[2,384,432]{2,1,0:T(8,128)(2,1)S(1)} %get-tuple-element.19.left_ref, bf16[512,432]{1,0:T(8,128)(2,1)S(1)} %get-tuple-element.20.columns_ref, bf16[432,128]{1,0:T(8,128)(2,1)S(1)} %get-tuple-element.16.a_ref, ...), custom_call_target="tpu_custom_call" | custom-call | tf_op jit(solution)/shard_map/pallas_call | solution.py:365
  16.8 0.0 collective-permute-done.6.b_ref
  16.8 0.0 collective-permute-done.7.d_ref
  16.8 1.4 %shard_map.98 = (f32[1,128]{1,0:T(1,128)}, f32[8,256]{1,0:T(8,128)}) custom-call(bf16[2,384,432]{2,1,0:T(8,128)(2,1)S(1)} %get-tuple-element.19.left_ref, bf16[128,432]{1,0:T(8,128)(2,1)S(1)} %get-tuple-element.23.proj_ref, bf16[432,128]{1,0:T(8,128)(2,1)S(1)} %collective-permute-done.a_ref, bf16[432,128]{1,0:T(8,128)(2,1)S(1)} %collective-permute-done.6.b_ref, ...), custom_call_target="tpu_custom_call" | custom-call | tf_op jit(solution)/shard_map/pallas_call | solution.py:377
  (7 shorter events, 0.0 us)
Async XLA Ops:
  0.6 8.6 %copy-start.2 = (bf16[8,16,128]{2,1,0:T(8,128)(2,1)S(1)}, bf16[8,16,128]{2,1,0:T(8,128)(2,1)}, u32[]{:S(2)}) copy-start(bf16[8,16,128]{2,1,0:T(8,128)(2,1)} %param.15) | copy-start | bytes 98308
  1.8 9.7 %copy-start = (bf16[128,512]{1,0:T(8,128)(2,1)S(1)}, bf16[128,512]{1,0:T(8,128)(2,1)}, u32[]{:S(2)}) copy-start(bf16[128,512]{1,0:T(8,128)(2,1)} %panel_ref.1) | copy-start | bytes 393220
  1.8 7.4 %collective-permute-start.3 = (bf16[224,128]{1,0:T(8,128)(2,1)S(1)}, bf16[224,128]{1,0:T(8,128)(2,1)S(1)}, u32[]{:S(2)}, u32[]{:S(2)}) collective-permute-start(bf16[224,128]{1,0:T(8,128)(2,1)S(1)} %get-tuple-element.18), channel_id=1, source_target_pairs={{0,8},{1,9},{2,26},{3,27},{4,12},{5,13},{6,30},{7,31},{8,0},{9,1},... | collective-permute-start | bytes 172040 | tf_op jit(solution)/shard_map/ppermute | solution.py:304
  5.9 7.6 %collective-permute-start = (bf16[432,128]{1,0:T(8,128)(2,1)S(1)}, bf16[432,128]{1,0:T(8,128)(2,1)S(1)}, u32[]{:S(2)}, u32[]{:S(2)}) collective-permute-start(bf16[432,128]{1,0:T(8,128)(2,1)S(1)} %get-tuple-element.16.a_ref), channel_id=1, source_target_pairs={{0,4},{1,21},{2,6},{3,23},{4,0},{5,17},{6,2},{7,19},{8,12},{9,29},... | collective-permute-start | bytes 331784 | tf_op jit(solution)/shard_map/ppermute | solution.py:304
  7.5 7.0 %collective-permute-start.1 = (bf16[432,128]{1,0:T(8,128)(2,1)S(1)}, bf16[432,128]{1,0:T(8,128)(2,1)S(1)}, u32[]{:S(2)}, u32[]{:S(2)}) collective-permute-start(bf16[432,128]{1,0:T(8,128)(2,1)S(1)} %get-tuple-element.16.a_ref), channel_id=1, source_target_pairs={{0,12},{1,29},{2,14},{3,31},{4,8},{5,25},{6,10},{7,27},{8,4},{9,21... | collective-permute-start | bytes 331784 | tf_op jit(solution)/shard_map/ppermute | solution.py:304
  7.5 7.0 %collective-permute-start.2 = (bf16[432,128]{1,0:T(8,128)(2,1)S(1)}, bf16[432,128]{1,0:T(8,128)(2,1)S(1)}, u32[]{:S(2)}, u32[]{:S(2)}) collective-permute-start(bf16[432,128]{1,0:T(8,128)(2,1)S(1)} %get-tuple-element.16.a_ref), channel_id=1, source_target_pairs={{0,16},{1,17},{2,18},{3,19},{4,20},{5,21},{6,22},{7,23},{8,24},{9,... | collective-permute-start | bytes 331784 | tf_op jit(solution)/shard_map/ppermute | solution.py:304
  9.2 2.3 %copy-start.3 = (bf16[8,16,16]{2,1,0:T(8,128)(2,1)S(1)}, bf16[8,16,16]{2,1,0:T(8,128)(2,1)}, u32[]{:S(2)}) copy-start(bf16[8,16,16]{2,1,0:T(8,128)(2,1)} %param.14) | copy-start | bytes 12292
  9.2 5.3 %collective-permute-start.4 = (bf16[352,128]{1,0:T(8,128)(2,1)S(1)}, bf16[352,128]{1,0:T(8,128)(2,1)S(1)}, u32[]{:S(2)}, u32[]{:S(2)}) collective-permute-start(bf16[352,128]{1,0:T(8,128)(2,1)S(1)} %pad_maximum_fusion.1), channel_id=1, source_target_pairs={{0,2},{1,3},{2,0},{3,1},{4,6},{5,7},{6,4},{7,5},{8,10},{9,11},{10,... | collective-permute-start | bytes 270344 | tf_op jit(solution)/shard_map/ppermute | solution.py:304
  11.5 0.8 %copy-start.1 = (bf16[128,128]{1,0:T(8,128)(2,1)S(1)}, bf16[128,128]{1,0:T(8,128)(2,1)}, u32[]{:S(2)}) copy-start(bf16[128,128]{1,0:T(8,128)(2,1)} %phi_ref.1) | copy-start | bytes 98308
  14.5 1.5 %collective-permute-start.5 = (bf16[704,128]{1,0:T(8,128)(2,1)S(1)}, bf16[704,128]{1,0:T(8,128)(2,1)S(1)}, u32[]{:S(2)}, u32[]{:S(2)}) collective-permute-start(bf16[704,128]{1,0:T(8,128)(2,1)S(1)} %pad_maximum_fusion.here_ref), channel_id=1, source_target_pairs={{0,1},{1,0},{2,3},{3,2},{4,5},{5,4},{6,7},{7,6},{8,9},{9,8},{10,11... | collective-permute-start | bytes 540680 | tf_op jit(solution)/shard_map/ppermute | solution.py:304
  14.6 2.1 %collective-permute-start.6 = (bf16[432,128]{1,0:T(8,128)(2,1)S(1)}, bf16[432,128]{1,0:T(8,128)(2,1)S(1)}, u32[]{:S(2)}, u32[]{:S(2)}) collective-permute-start(bf16[432,128]{1,0:T(8,128)(2,1)S(1)} %collective-permute-done.a_ref), channel_id=1, source_target_pairs={{0,1},{1,0},{2,3},{3,2},{4,5},{5,4},{6,7},{7,6},{8,9},{9,8},{10,11... | collective-permute-start | bytes 331784 | tf_op jit(solution)/shard_map/ppermute | solution.py:304
  15.1 1.7 %collective-permute-start.7 = (bf16[432,128]{1,0:T(8,128)(2,1)S(1)}, bf16[432,128]{1,0:T(8,128)(2,1)S(1)}, u32[]{:S(2)}, u32[]{:S(2)}) collective-permute-start(bf16[432,128]{1,0:T(8,128)(2,1)S(1)} %collective-permute-done.1.c_ref), channel_id=1, source_target_pairs={{0,1},{1,0},{2,3},{3,2},{4,5},{5,4},{6,7},{7,6},{8,9},{9,8},{10,11... | collective-permute-start | bytes 331784 | tf_op jit(solution)/shard_map/ppermute | solution.py:304
